TPU v7x, 256 devices: a whole 4x4x8 slice. The times are simulated.
256 devices in a mesh: row: 32 (over z_hi, x, core), col: 8 (over z_lo, y).
Axes of the slice: x: 4, y: 4, z: 8 (z_hi: 4, z_lo: 2; z = z_hi * 2 + z_lo), core: 2. Of those that a mesh axis runs over, the one named last changes fastest.
Arguments:
- eta_ladder: bfloat16 [20480, 1024], P('row', 'col'), may hold values from -1.0546875 to 1.0546875
- gamma_ladder: bfloat16 [20480, 1024], P('row', 'col'), may hold values from -1.0546875 to 1.0546875
- occupation: int32 [1024], replicated, may hold values from 0 to 4
- gamma: bfloat16 [20480, 20480], P('row', 'col'), may hold values from -6 to 6
Outputs:
- gamma_next: bfloat16 [20480, 20480], P('row', 'col')
All inputs are finite; a program needn't handle non-finite values.
Results may differ from a plain program's by a relative error of at most 0.001.
Values may be sent and summed in bfloat16 or wider, within the bound.
No kernel may reach another device: no remote copies, remote signals or barrier semaphores. Data moves between devices by JAX's collectives and lax.ppermute only.
A program may use at most 128 MiB of HBM per device.

v0:
```python
import jax
import jax.numpy as jnp
from jax import lax
from jax.sharding import PartitionSpec as P

euler_step = 0.5


def spread(value, axis, root):
    mine = lax.axis_index(axis) == root
    return lax.psum(jnp.where(mine, value, jnp.zeros_like(value)), axis)


def per_device(eta_ladder, gamma_ladder, occupation, gamma):
    weights = 1.0 - 0.5 * occupation.astype(jnp.float32)
    eta_rows, gamma_rows = (
        lax.all_gather(eta_ladder, "col", axis=1, tiled=True),
        lax.all_gather(gamma_ladder, "col", axis=1, tiled=True),
    )
    left_panel = jnp.concatenate(
        [
            (eta_rows.astype(jnp.float32) * weights).astype(jnp.bfloat16),
            (gamma_rows.astype(jnp.float32) * weights).astype(jnp.bfloat16),
        ],
        1,
    )
    stride = lax.axis_size("row") // lax.axis_size("col")
    column = lax.axis_index("col")
    eta_parts = []
    gamma_parts = []
    for member in range(stride):
        eta_piece, gamma_piece = (
            spread(eta_rows, "row", column * stride + member),
            spread(gamma_rows, "row", column * stride + member),
        )
        eta_parts.append(eta_piece)
        gamma_parts.append(gamma_piece)
    eta_right = jnp.concatenate(eta_parts, 0)
    gamma_right = jnp.concatenate(gamma_parts, 0)
    right_panel = jnp.concatenate([gamma_right, eta_right], 1)
    commutator = lax.dot_general(
        left_panel, right_panel, (((1,), (1,)), ((), ())), preferred_element_type=jnp.float32
    )
    return (gamma.astype(jnp.float32) + euler_step * commutator).astype(jnp.bfloat16)


def solution(mesh):
    placed = (P("row", "col"), P("row", "col"), P(), P("row", "col"))
    return jax.shard_map(
        per_device, mesh=mesh, in_specs=placed, out_specs=P("row", "col"), check_vma=False
    )
```

profile of v0, /device:TPU:25, one launch (start us, length us, event | category | flops | bytes accessed | tf_op | source)
XLA Modules:
  0.0 479.2 jit_solution(10947082188139162341)
XLA Ops:
  6.5 0.0 all-gather.5.cloned.1.call-start
  6.5 0.7 all-gather.5.cloned.1.call-update
  7.3 0.0 all-gather.3.cloned.1.call-start
  7.3 0.7 all-gather.3.cloned.1.call-update
  8.0 0.0 all-reduce.3.cloned.1.call-start
  8.1 42.1 %all-gather.5.cloned.1.call-done = bf16[640,1024]{1,0:T(8,128)(2,1)} async-done(((bf16[640,128]{1,0:T(8,128)(2,1)}), bf16[640,1024]{1,0:T(8,128)(2,1)}) %all-gather.5.cloned.1.call-update) | async-done | bytes 1310736 | tf_op jit(solution)/shard_map/all_gather | solution.py:18
  50.2 3.7 broadcast_select_fusion.7
  53.9 40.9 %all-gather.3.cloned.1.call-done = bf16[640,1024]{1,0:T(8,128)(2,1)} async-done(((bf16[640,128]{1,0:T(8,128)(2,1)}), bf16[640,1024]{1,0:T(8,128)(2,1)}) %all-gather.3.cloned.1.call-update) | async-done | bytes 1310736 | tf_op jit(solution)/shard_map/all_gather | solution.py:17
  94.7 3.7 broadcast_select_fusion.6
  98.5 0.0 copy-start.2
  98.5 0.0 copy-start
  98.5 0.0 copy-start.1
  98.5 0.0 all-reduce.3.cloned.1.call-update
  98.5 0.7 copy-done.2
  99.2 0.6 copy-done
  99.8 0.4 copy-done.1
  100.2 2.3 multiply_convert_fusion.1
  102.5 344.5 %all-reduce.3.cloned.1.call-done = (bf16[640,1024]{1,0:T(8,128)(2,1)}, bf16[640,1024]{1,0:T(8,128)(2,1)}, bf16[640,1024]{1,0:T(8,128)(2,1)}, bf16[640,1024]{1,0:...) async-done(((bf16[640,1024]{1,0:T(8,128)(2,1)}, bf16[640,1024]{1,0:T(8,128)(2,1)}, ...) | async-done | bytes 10485776 | tf_op jit(solution)/shard_map/psum | solution.py:11
  447.0 25.7 %add_convert_fusion = bf16[640,2560]{1,0:T(8,128)(2,1)} fusion(bf16[640,2560]{1,0:T(8,128)(2,1)} %param.7, bf16[640,1024]{1,0:T(8,128)(2,1)} %get-tuple-element.5, bf16[640,1024]{1,0:T(8,128)(2,1)} %get-tuple-element.6, bf16[640,1024]{1,0:T(8,128)(2,1)} %get-tuple-element.7, bf16[640,1024]{1,0:T(8,128)(2,1)} %get-tuple-element.8, ...), kind=kOutput, calls=%fused_computation.16 | convolution fusion | flops 6806568960 | bytes 19660800 | tf_op jit(solution)/shard_map/dot_general | solution.py:41
  (1 shorter events, 0.0 us)
Async XLA Ops:
  6.5 43.6 %all-gather.5.cloned.1.call-start = ((), (), s32[]{:S(2)}) async-start(), calls=%async_computation.1 | async-start | bytes 1474560 | tf_op jit(solution)/shard_map/all_gather | solution.py:18
  7.3 87.5 %all-gather.3.cloned.1.call-start = ((), (), s32[]{:S(2)}) async-start(), calls=%async_computation | async-start | bytes 1474560 | tf_op jit(solution)/shard_map/all_gather | solution.py:17
  8.0 439.0 %all-reduce.3.cloned.1.call-start = ((), (), s32[]{:S(2)}) async-start(), calls=%async_computation.2 | async-start | bytes 20971520 | tf_op jit(solution)/shard_map/psum | solution.py:11
  98.5 0.7 copy-start.2
  98.5 1.3 copy-start
  98.5 1.7 copy-start.1
Sparse Core Ops, SparseCore 0:
  9.1 41.0 all-gather.4
  51.9 42.8 all-gather.2
  98.6 348.3 all-reduce.2
where the time goes:
time: 483 us; the launch traced here: 479 us
  waiting for transfers between devices  429 us (89%)
  matrix products  25.7 us (5%)
  between operations  13.1 us (3%)
  other arithmetic  9.73 us (2%)
    psum x1, waiting for transfers between devices, spread(): return lax.psum(jnp.where(mine, value, jnp.zeros_like(value)), axis)  345 us
    all_gather x1, waiting for transfers between devices, per_device(): lax.all_gather(gamma_ladder, 'col', axis=1, tiled=True)  42.1 us
    all_gather x1, waiting for transfers between devices, per_device(): lax.all_gather(eta_ladder, 'col', axis=1, tiled=True)  40.9 us
    dot_general x1, matrix products, per_device(): lax.dot_general(left_panel, right_panel, (((1,), (1,)), ((), ())), prefer...  25.7 us
  transfers between devices with their start and end apart: 3, of which 3 were waited for; matrix products, arithmetic and copies ran while one was open for 1% of the time, Pallas kernels for 0%

commit v1 on v0

v1 whole, which is shorter than its diff:
```python
import functools

import jax
import jax.numpy as jnp
from jax import lax
from jax.experimental import pallas as pl
from jax.experimental.pallas import tpu as pltpu
from jax.sharding import PartitionSpec as P

euler_step = 0.5
ZH, X, CORE, ZL, Y = 4, 4, 2, 2, 4
AXES = ("row", "col")


def every_device():
    for zh in range(ZH):
        for x in range(X):
            for core in range(CORE):
                for zl in range(ZL):
                    for y in range(Y):
                        yield zh, x, core, zl, y


def flat(zh, x, core, zl, y):
    return ((((zh % ZH) * X + x % X) * CORE + core % CORE) * ZL + zl % ZL) * Y + y % Y


def home(zh, x, core, zl, y):
    group = zh * 2 + x // 2
    return flat(zh + 2 * core + x % 2, y + 2 * core, zl, group // Y, group % Y)


def pairs(target):
    return [(flat(*d), target(*d)) for d in every_device()]


TO_HOME = pairs(home)
ALONG_Z = pairs(lambda zh, x, core, zl, y: flat(zh + 1 - 2 * core, x, core, zl, y))
ALONG_X = pairs(lambda zh, x, core, zl, y: flat(zh, x + 1 - 2 * core, core, zl, y))
OTHER_CORE = pairs(lambda zh, x, core, zl, y: flat(zh, x, core + 1, zl, y))


def send(value, way):
    return lax.ppermute(value, AXES, way)


def other(value):
    return send(value, OTHER_CORE)


def after(value, *earlier):
    return lax.optimization_barrier((value, *earlier))[0]


def weigh(panel_ref, weights_ref, out_ref):
    half = panel_ref.shape[-1] // 2
    weights = weights_ref[...]
    panel = panel_ref[...].astype(jnp.float32)
    out_ref[:, :half] = (panel[:, half:] * weights).astype(jnp.bfloat16)
    out_ref[:, half:] = (panel[:, :half] * weights).astype(jnp.bfloat16)


def left_panel_of(gathered, weights):
    parts, height, width = gathered.shape
    return pl.pallas_call(
        weigh,
        grid=(parts,),
        in_specs=[
            pl.BlockSpec((None, height, width), lambda k: (k, 0, 0)),
            pl.BlockSpec((None, 1, width // 2), lambda k: (k, 0, 0)),
        ],
        out_specs=pl.BlockSpec((height, width), lambda k: (0, k)),
        out_shape=jax.ShapeDtypeStruct((height, parts * width), jnp.bfloat16),
        compiler_params=pltpu.CompilerParams(vmem_limit_bytes=8 * 2**20),
        cost_estimate=pl.CostEstimate(
            flops=parts * height * width, bytes_accessed=4 * parts * height * width, transcendentals=0
        ),
        name="weigh_left",
    )(gathered, weights.reshape(parts, 1, width // 2))


def rem(value, length):
    return lax.rem(value, jnp.int32(length))


def block_kernel(dz, places, left_ref, *refs):
    count = len(places)
    pieces, gamma_ref = refs[:count], refs[count]
    out_ref, right, old, new, sems = refs[-5:]
    height, width = pieces[0].shape
    row, col = lax.axis_index("row"), lax.axis_index("col")
    zh, x, core = lax.div(row, jnp.int32(X * CORE)), rem(lax.div(row, jnp.int32(CORE)), X), rem(row, CORE)
    way = 2 * core - 1
    turn = rem(zh + dz[0] + dz[1] * way + 2 * ZH - lax.div(col, jnp.int32(2)), ZH)
    low, high = rem(turn, 2), lax.div(turn, jnp.int32(2))
    columns = pl.ds(pl.multiple_of((low * 2 + high) * height, 128), height)
    copies = [pltpu.make_async_copy(gamma_ref.at[:, columns], old, sems.at[count])]
    for index, (piece, (dx, other_core)) in enumerate(zip(pieces, places)):
        part = rem(core + other_core, CORE) * Y + rem(x + dx[0] + dx[1] * way + 2 * X - 2 * high, X)
        place = pl.ds(pl.multiple_of(part * width, width), width)
        copies.append(pltpu.make_async_copy(piece, right.at[:, place], sems.at[index]))
    for copy in copies:
        copy.start()
    for copy in copies:
        copy.wait()
    for first in range(0, height, 256):
        size = min(256, height - first)
        commutator = lax.dot_general(
            left_ref[...],
            right[first : first + size, :],
            (((1,), (1,)), ((), ())),
            preferred_element_type=jnp.float32,
        )
        new[:, first : first + size] = (
            old[:, first : first + size].astype(jnp.float32) + euler_step * commutator
        ).astype(jnp.bfloat16)
    back = pltpu.make_async_copy(new, out_ref.at[:, columns], sems.at[count + 1])
    back.start()
    back.wait()


def block_step(dz, places, left, pieces, gamma, out):
    count = len(pieces)
    height, width = pieces[0].shape
    anywhere = pl.BlockSpec(memory_space=pl.ANY)
    operands = [left, *pieces, gamma]
    aliases = {}
    if out is not None:
        aliases = {len(operands): 0}
        operands.append(out)
    return pl.pallas_call(
        functools.partial(block_kernel, dz, places),
        in_specs=[
            pl.BlockSpec(memory_space=pltpu.VMEM),
            *[anywhere] * (len(operands) - 1),
        ],
        out_specs=anywhere,
        out_shape=jax.ShapeDtypeStruct(gamma.shape, gamma.dtype),
        input_output_aliases=aliases,
        scratch_shapes=[
            pltpu.VMEM((height, count * width), jnp.bfloat16),
            pltpu.VMEM((height, height), jnp.bfloat16),
            pltpu.VMEM((height, height), jnp.bfloat16),
            pltpu.SemaphoreType.DMA((count + 2,)),
        ],
        compiler_params=pltpu.CompilerParams(vmem_limit_bytes=20 * 2**20),
        cost_estimate=pl.CostEstimate(
            flops=2 * height * height * count * width,
            bytes_accessed=4 * height * count * width + 4 * height * height,
            transcendentals=0,
        ),
        name="block_step",
    )(*operands)


HERE, BACK, AHEAD, ACROSS = (0, 0), (0, 1), (0, -1), (2, 0)
ALIKE = [(HERE, 0), (HERE, 1), (BACK, 0), (BACK, 1), (AHEAD, 1), (AHEAD, 0), (ACROSS, 0), (ACROSS, 1)]
DIRECT = [(HERE, 0), (HERE, 1), (BACK, 0), (BACK, 1), (AHEAD, 0), (AHEAD, 1), (ACROSS, 0), (ACROSS, 1)]
SWAPPED = [(dx, 1 - core) for dx, core in DIRECT]


def per_device(eta_ladder, gamma_ladder, occupation, gamma):
    weights = 1.0 - 0.5 * occupation.astype(jnp.float32)
    shard = jnp.concatenate([gamma_ladder, eta_ladder], 1)
    gathered = lax.all_gather(shard, "col")
    left = left_panel_of(gathered, weights)

    p = send(shard, TO_HOME)
    ps = other(p)
    za, zb = send(p, ALONG_Z), send(ps, ALONG_Z)
    xp, xps = send(p, ALONG_X), send(ps, ALONG_X)
    fxp = send(xp, ALONG_X)
    z2 = send(za, ALONG_Z)
    sa, sb = other(za), other(zb)
    z2s = other(z2)
    xza, xzb = send(za, ALONG_X), send(zb, ALONG_X)
    xsa, xsb = send(sa, ALONG_X), send(sb, ALONG_X)
    fxza, fxzb = send(xza, ALONG_X), send(xzb, ALONG_X)
    xz2, xz2s = send(z2, ALONG_X), send(z2s, ALONG_X)
    block0 = [p, ps, xp, xps, other(xp), other(xps), fxp, other(fxp)]
    out = block_step(HERE, ALIKE, left, block0, gamma, None)
    fxz2 = send(after(xz2, out), ALONG_X)
    blocka = [za, zb, xza, xzb, other(xsa), other(xsb), fxza, fxzb]
    blockb = [sa, sb, xsa, xsb, other(xza), other(xzb), other(fxza), other(fxzb)]
    block2 = [z2, z2s, xz2, xz2s, other(xz2), other(xz2s), fxz2, other(fxz2)]
    out = block_step(BACK, DIRECT, left, blocka, gamma, out)
    out = block_step(AHEAD, SWAPPED, left, blockb, gamma, out)
    return block_step(ACROSS, ALIKE, left, block2, gamma, out)


def solution(mesh):
    placed = (P("row", "col"), P("row", "col"), P(), P("row", "col"))
    return jax.shard_map(
        per_device, mesh=mesh, in_specs=placed, out_specs=P("row", "col"), check_vma=False
    )
```

time: 483 us -> 140 us (0.29)
  waiting for transfers between devices: 429 us -> 13 us
  starting transfers between devices: 0.08 us -> 81.7 us
  matrix products: 25.7 us -> 0 us
  Pallas kernels: 0 us -> 18.4 us
  local copies, waits for them, and re-layouts: 1.69 us -> 12.6 us
  other arithmetic: 9.73 us -> 0.69 us
    psum x1 -> x0, waiting for transfers between devices: 345 us -> none  [spread(): return lax.psum(jnp.where(mine, value, jnp.zeros_like(value)), axis)]
    all_gather x2 -> x1, waiting for transfers between devices: 83 us -> 0.01 us  [per_device(): gathered = lax.all_gather(shard, 'col')]
    ppermute x0 -> x32, starting transfers between devices: none -> 81.7 us  [send(): return lax.ppermute(value, AXES, way)]
    dot_general x1 -> x0, matrix products: 25.7 us -> none  [per_device(): lax.dot_general(left_panel, right_panel, (((1,), (1,)), ((), ())), prefer...]
    pallas_call x0 -> x5, Pallas kernels: none -> 18.4 us  [the longest x4 17.5 us: block_step(): pl.pallas_call(functools.partial(block_kernel, dz, places), in_specs=[pl....]
    ppermute x0 -> x32, waiting for transfers between devices: none -> 13 us  [send(): return lax.ppermute(value, AXES, way)]
    unnamed x6 -> x49, local copies, waits for them, and re-layouts: 1.69 us -> 11 us
    select_n x2 -> x0, other arithmetic: 7.45 us -> none  [spread(): return lax.psum(jnp.where(mine, value, jnp.zeros_like(value)), axis)]
  transfers between devices with their start and end apart: 3 -> 33, of which waited for: 3 -> 4; matrix products, arithmetic and copies ran while one was open for 1% -> 0% of each run, Pallas kernels for 0% -> 10%
where the time goes in v1:
time: 140 us
  starting transfers between devices  81.7 us (58%)
  Pallas kernels  18.4 us (13%)
  between operations  13.7 us (10%)
  waiting for transfers between devices  13 us (9%)
  local copies, waits for them, and re-layouts  12.6 us (9%)
    ppermute x32, starting transfers between devices, send(): return lax.ppermute(value, AXES, way)  81.7 us
    pallas_call x4, Pallas kernels, block_step(): pl.pallas_call(functools.partial(block_kernel, dz, places), in_specs=[pl....  17.5 us
    ppermute x32, waiting for transfers between devices, send(): return lax.ppermute(value, AXES, way)  13 us
    unnamed x49, local copies, waits for them, and re-layouts  11 us
  transfers between devices with their start and end apart: 33, of which 4 were waited for; matrix products, arithmetic and copies ran while one was open for 0% of the time, Pallas kernels for 10%

profile of v1, /device:TPU:25, one launch (start us, length us, event | category | flops | bytes accessed | tf_op | source)
XLA Modules:
  0.0 140.0 jit_solution(15263270512213499671)
XLA Ops:
  6.5 1.7 %constant_dynamic-update-slice_fusion.1 = bf16[640,256]{1,0:T(8,128)(2,1)} fusion(bf16[640,128]{1,0:T(8,128)(2,1)} %param.5), kind=kLoop, calls=%fused_computation.1 | loop fusion | bytes 327680
  9.9 10.0 %collective-permute-start = (bf16[640,256]{1,0:T(8,128)(2,1)}, bf16[640,256]{1,0:T(8,128)(2,1)S(1)}, u32[]{:S(2)}, u32[]{:S(2)}) collective-permute-start(bf16[640,256]{1,0:T(8,128)(2,1)} %constant_dynamic-update-slice_fusion), channel_id=1, source_target_pairs={{0,0},{1,16},{2,32},{3,48},{4,8},{5,24},{6,40},{7,56},{8,160},{9,1... | collective-permute-start | bytes 983048 | tf_op jit(solution)/shard_map/ppermute | solution.py:44
  19.9 4.4 %collective-permute-done.refs_0_ = bf16[640,256]{1,0:T(8,128)(2,1)S(1)} collective-permute-done((bf16[640,256]{1,0:T(8,128)(2,1)}, bf16[640,256]{1,0:T(8,128)(2,1)S(1)}, u32[]{:S(2)}, u32[]{:S(2)}) %collective-permute-start) | collective-permute-done | bytes 327712 | tf_op jit(solution)/shard_map/ppermute | solution.py:44
  24.3 2.5 %collective-permute-start.8 = (bf16[640,256]{1,0:T(8,128)(2,1)S(1)}, bf16[640,256]{1,0:T(8,128)(2,1)S(1)}, u32[]{:S(2)}, u32[]{:S(2)}) collective-permute-start(bf16[640,256]{1,0:T(8,128)(2,1)S(1)} %collective-permute-done.refs_0_), channel_id=1, source_target_pairs={{0,8},{1,9},{2,10},{3,11},{4,12},{5,13},{6,14},{7,15},{8,0},{9,1},... | collective-permute-start | bytes 983048 | tf_op jit(solution)/shard_map/ppermute | solution.py:44
  26.8 8.1 %collective-permute-start.9 = (bf16[640,256]{1,0:T(8,128)(2,1)S(1)}, bf16[640,256]{1,0:T(8,128)(2,1)S(1)}, u32[]{:S(2)}, u32[]{:S(2)}) collective-permute-start(bf16[640,256]{1,0:T(8,128)(2,1)S(1)} %collective-permute-done.refs_0_), channel_id=1, source_target_pairs={{0,16},{1,17},{2,18},{3,19},{4,20},{5,21},{6,22},{7,23},{8,56},{9,... | collective-permute-start | bytes 983048 | tf_op jit(solution)/shard_map/ppermute | solution.py:44
  34.9 11.2 %collective-permute-start.1 = (bf16[640,256]{1,0:T(8,128)(2,1)S(1)}, bf16[640,256]{1,0:T(8,128)(2,1)S(1)}, u32[]{:S(2)}, u32[]{:S(2)}) collective-permute-start(bf16[640,256]{1,0:T(8,128)(2,1)S(1)} %collective-permute-done.refs_0_), channel_id=1, source_target_pairs={{0,64},{1,65},{2,66},{3,67},{4,68},{5,69},{6,70},{7,71},{8,200},{9... | collective-permute-start | bytes 983048 | tf_op jit(solution)/shard_map/ppermute | solution.py:44
  48.4 3.4 %collective-permute-done.1.refs_0_ = bf16[640,256]{1,0:T(8,128)(2,1)S(1)} collective-permute-done((bf16[640,256]{1,0:T(8,128)(2,1)S(1)}, bf16[640,256]{1,0:T(8,128)(2,1)S(1)}, u32[]{:S(2)}, u32[]{:S(2)}) %collective-permute-start.1) | collective-permute-done | bytes 327712 | tf_op jit(solution)/shard_map/ppermute | solution.py:44
  51.9 4.5 %collective-permute-start.2 = (bf16[640,256]{1,0:T(8,128)(2,1)S(1)}, bf16[640,256]{1,0:T(8,128)(2,1)}, u32[]{:S(2)}, u32[]{:S(2)}) collective-permute-start(bf16[640,256]{1,0:T(8,128)(2,1)S(1)} %collective-permute-done.1.refs_0_), channel_id=1, source_target_pairs={{0,64},{1,65},{2,66},{3,67},{4,68},{5,69},{6,70},{7,71},{8,200},{9... | collective-permute-start | bytes 983048 | tf_op jit(solution)/shard_map/ppermute | solution.py:44
  57.5 12.7 %collective-permute-start.17 = (bf16[640,256]{1,0:T(8,128)(2,1)S(1)}, bf16[640,256]{1,0:T(8,128)(2,1)}, u32[]{:S(2)}, u32[]{:S(2)}) collective-permute-start(bf16[640,256]{1,0:T(8,128)(2,1)S(1)} %collective-permute-done.1.refs_0_), channel_id=1, source_target_pairs={{0,8},{1,9},{2,10},{3,11},{4,12},{5,13},{6,14},{7,15},{8,0},{9,1},... | collective-permute-start | bytes 983048 | tf_op jit(solution)/shard_map/ppermute | solution.py:44
  72.4 8.0 %collective-permute-start.14 = (bf16[640,256]{1,0:T(8,128)(2,1)S(1)}, bf16[640,256]{1,0:T(8,128)(2,1)S(1)}, u32[]{:S(2)}, u32[]{:S(2)}) collective-permute-start(bf16[640,256]{1,0:T(8,128)(2,1)S(1)} %collective-permute-done.13.refs_6_), channel_id=1, source_target_pairs={{0,8},{1,9},{2,10},{3,11},{4,12},{5,13},{6,14},{7,15},{8,0},{9,1},... | collective-permute-start | bytes 983048 | tf_op jit(solution)/shard_map/ppermute | solution.py:44
  81.9 2.6 %collective-permute-start.19 = (bf16[640,256]{1,0:T(8,128)(2,1)S(1)}, bf16[640,256]{1,0:T(8,128)(2,1)}, u32[]{:S(2)}, u32[]{:S(2)}) collective-permute-start(bf16[640,256]{1,0:T(8,128)(2,1)S(1)} %collective-permute-done.18.refs_1_), channel_id=1, source_target_pairs={{0,8},{1,9},{2,10},{3,11},{4,12},{5,13},{6,14},{7,15},{8,0},{9,1},... | collective-permute-start | bytes 983048 | tf_op jit(solution)/shard_map/ppermute | solution.py:44
  86.0 2.9 %collective-permute-start.26 = (bf16[640,256]{1,0:T(8,128)(2,1)}, bf16[640,256]{1,0:T(8,128)(2,1)}, u32[]{:S(2)}, u32[]{:S(2)}) collective-permute-start(bf16[640,256]{1,0:T(8,128)(2,1)} %collective-permute-done.22.refs_2_), channel_id=1, source_target_pairs={{0,16},{1,17},{2,18},{3,19},{4,20},{5,21},{6,22},{7,23},{8,56},{9,... | collective-permute-start | bytes 983048 | tf_op jit(solution)/shard_map/ppermute | solution.py:44
  92.3 3.6 %collective-permute-start.3 = (bf16[640,256]{1,0:T(8,128)(2,1)}, bf16[640,256]{1,0:T(8,128)(2,1)}, u32[]{:S(2)}, u32[]{:S(2)}) collective-permute-start(bf16[640,256]{1,0:T(8,128)(2,1)} %collective-permute-done.2.refs_0_), channel_id=1, source_target_pairs={{0,8},{1,9},{2,10},{3,11},{4,12},{5,13},{6,14},{7,15},{8,0},{9,1},... | collective-permute-start | bytes 983048 | tf_op jit(solution)/shard_map/ppermute | solution.py:44
  97.0 1.7 %copy-done.1 = bf16[5120,256]{1,0:T(8,128)(2,1)S(1)} copy-done((bf16[5120,256]{1,0:T(8,128)(2,1)S(1)}, bf16[5120,256]{1,0:T(8,128)(2,1)}, u32[]{:S(2)}) %copy-start.1) | copy-done | bytes 2621464
  99.8 3.1 %collective-permute-start.25 = (bf16[640,256]{1,0:T(8,128)(2,1)}, bf16[640,256]{1,0:T(8,128)(2,1)S(1)}, u32[]{:S(2)}, u32[]{:S(2)}) collective-permute-start(bf16[640,256]{1,0:T(8,128)(2,1)} %collective-permute-done.24.refs_3_), channel_id=1, source_target_pairs={{0,8},{1,9},{2,10},{3,11},{4,12},{5,13},{6,14},{7,15},{8,0},{9,1},... | collective-permute-start | bytes 983048 | tf_op jit(solution)/shard_map/ppermute | solution.py:44
  103.1 3.7 %block_step.4.refs_9_ = bf16[640,2560]{1,0:T(8,128)(2,1)} custom-call(bf16[640,2048]{1,0:T(8,128)(2,1)S(1)} %weigh_left.1.left_ref, bf16[640,256]{1,0:T(8,128)(2,1)S(1)} %copy-done.3, bf16[640,256]{1,0:T(8,128)(2,1)S(1)} %copy-done.5, bf16[640,256]{1,0:T(8,128)(2,1)S(1)} %copy-done.7, bf16[640,256]{1,0:T(8,128)(2,1)S(1)} %copy-done.9, ...), custom_call_target="tpu_custom_call" | custom-call | flops 1677721600 | bytes 6881280 | tf_op jit(solution)/shard_map/block_step/pallas_call | solution.py:131
  106.8 3.0 %collective-permute-start.5 = (bf16[640,256]{1,0:T(8,128)(2,1)}, bf16[640,256]{1,0:T(8,128)(2,1)S(1)}, u32[]{:S(2)}, u32[]{:S(2)}) collective-permute-start(bf16[640,256]{1,0:T(8,128)(2,1)} %collective-permute-done.3.refs_1_), channel_id=1, source_target_pairs={{0,16},{1,17},{2,18},{3,19},{4,20},{5,21},{6,22},{7,23},{8,56},{9,... | collective-permute-start | bytes 983048 | tf_op jit(solution)/shard_map/ppermute | solution.py:44
  110.9 3.3 %collective-permute-done.5.refs_3_ = bf16[640,256]{1,0:T(8,128)(2,1)S(1)} collective-permute-done((bf16[640,256]{1,0:T(8,128)(2,1)}, bf16[640,256]{1,0:T(8,128)(2,1)S(1)}, u32[]{:S(2)}, u32[]{:S(2)}) %collective-permute-start.5) | collective-permute-done | bytes 327712 | tf_op jit(solution)/shard_map/ppermute | solution.py:44
  114.2 1.6 %collective-permute-start.6 = (bf16[640,256]{1,0:T(8,128)(2,1)S(1)}, bf16[640,256]{1,0:T(8,128)(2,1)S(1)}, u32[]{:S(2)}, u32[]{:S(2)}) collective-permute-start(bf16[640,256]{1,0:T(8,128)(2,1)S(1)} %copy-done.23), channel_id=1, source_target_pairs={{0,8},{1,9},{2,10},{3,11},{4,12},{5,13},{6,14},{7,15},{8,0},{9,1},... | collective-permute-start | bytes 983048 | tf_op jit(solution)/shard_map/ppermute | solution.py:44
  115.8 1.8 %collective-permute-done.15.refs_6_ = bf16[640,256]{1,0:T(8,128)(2,1)S(1)} collective-permute-done((bf16[640,256]{1,0:T(8,128)(2,1)S(1)}, bf16[640,256]{1,0:T(8,128)(2,1)S(1)}, u32[]{:S(2)}, u32[]{:S(2)}) %collective-permute-start.15) | collective-permute-done | bytes 327712 | tf_op jit(solution)/shard_map/ppermute | solution.py:44
  117.6 1.7 %collective-permute-start.16 = (bf16[640,256]{1,0:T(8,128)(2,1)S(1)}, bf16[640,256]{1,0:T(8,128)(2,1)S(1)}, u32[]{:S(2)}, u32[]{:S(2)}) collective-permute-start(bf16[640,256]{1,0:T(8,128)(2,1)S(1)} %collective-permute-done.15.refs_6_), channel_id=1, source_target_pairs={{0,8},{1,9},{2,10},{3,11},{4,12},{5,13},{6,14},{7,15},{8,0},{9,1},... | collective-permute-start | bytes 983048 | tf_op jit(solution)/shard_map/ppermute | solution.py:44
  119.3 4.7 %block_step.5.refs_9_ = bf16[640,2560]{1,0:T(8,128)(2,1)} custom-call(bf16[640,2048]{1,0:T(8,128)(2,1)S(1)} %weigh_left.1.left_ref, bf16[640,256]{1,0:T(8,128)(2,1)S(1)} %copy-done.19, bf16[640,256]{1,0:T(8,128)(2,1)S(1)} %copy-done.21, bf16[640,256]{1,0:T(8,128)(2,1)} %collective-permute-done.22.refs_2_, ...), custom_call_target="tpu_custom_call", output_to_operand_aliasing={{}: (10, {})} | custom-call | flops 1677721600 | bytes 6881280 | tf_op jit(solution)/shard_map/block_step/pallas_call | solution.py:131
  124.0 4.7 %block_step.6.refs_9_ = bf16[640,2560]{1,0:T(8,128)(2,1)} custom-call(bf16[640,2048]{1,0:T(8,128)(2,1)S(1)} %weigh_left.1.left_ref, bf16[640,256]{1,0:T(8,128)(2,1)} %collective-permute-done.17.refs_0_, bf16[640,256]{1,0:T(8,128)(2,1)} %collective-permute-done.19.refs_1_, ...), custom_call_target="tpu_custom_call", output_to_operand_aliasing={{}: (10, {})} | custom-call | flops 1677721600 | bytes 6881280 | tf_op jit(solution)/shard_map/block_step/pallas_call | solution.py:131
  128.8 4.4 %block_step.7 = bf16[640,2560]{1,0:T(8,128)(2,1)} custom-call(bf16[640,2048]{1,0:T(8,128)(2,1)S(1)} %weigh_left.1.left_ref, bf16[640,256]{1,0:T(8,128)(2,1)} %collective-permute-done.2.refs_0_, bf16[640,256]{1,0:T(8,128)(2,1)} %collective-permute-done.3.refs_1_, bf16[640,256]{1,0:T(8,128)(2,1)S(1)} %copy-done.23, ...), custom_call_target="tpu_custom_call", output_to_operand_aliasing={{}: (10, {})} | custom-call | flops 1677721600 | bytes 6881280 | tf_op jit(solution)/shard_map/block_step/pallas_call | solution.py:131
  (99 shorter events, 17.0 us)
Async XLA Ops:
  6.5 90.5 %all-gather.3.cloned.1.call-start = ((), (), s32[]{:S(2)}) async-start(), calls=%async_computation | async-start | bytes 2949120 | tf_op jit(solution)/shard_map/all_gather | solution.py:165
  9.9 14.4 %collective-permute-start = (bf16[640,256]{1,0:T(8,128)(2,1)}, bf16[640,256]{1,0:T(8,128)(2,1)S(1)}, u32[]{:S(2)}, u32[]{:S(2)}) collective-permute-start(bf16[640,256]{1,0:T(8,128)(2,1)} %constant_dynamic-update-slice_fusion), channel_id=1, source_target_pairs={{0,0},{1,16},{2,32},{3,48},{4,8},{5,24},{6,40},{7,56},{8,160},{9,1... | collective-permute-start | bytes 983048 | tf_op jit(solution)/shard_map/ppermute | solution.py:44
  24.3 22.6 %collective-permute-start.8 = (bf16[640,256]{1,0:T(8,128)(2,1)S(1)}, bf16[640,256]{1,0:T(8,128)(2,1)S(1)}, u32[]{:S(2)}, u32[]{:S(2)}) collective-permute-start(bf16[640,256]{1,0:T(8,128)(2,1)S(1)} %collective-permute-done.refs_0_), channel_id=1, source_target_pairs={{0,8},{1,9},{2,10},{3,11},{4,12},{5,13},{6,14},{7,15},{8,0},{9,1},... | collective-permute-start | bytes 983048 | tf_op jit(solution)/shard_map/ppermute | solution.py:44
  26.8 20.4 %collective-permute-start.9 = (bf16[640,256]{1,0:T(8,128)(2,1)S(1)}, bf16[640,256]{1,0:T(8,128)(2,1)S(1)}, u32[]{:S(2)}, u32[]{:S(2)}) collective-permute-start(bf16[640,256]{1,0:T(8,128)(2,1)S(1)} %collective-permute-done.refs_0_), channel_id=1, source_target_pairs={{0,16},{1,17},{2,18},{3,19},{4,20},{5,21},{6,22},{7,23},{8,56},{9,... | collective-permute-start | bytes 983048 | tf_op jit(solution)/shard_map/ppermute | solution.py:44
  34.9 16.9 %collective-permute-start.1 = (bf16[640,256]{1,0:T(8,128)(2,1)S(1)}, bf16[640,256]{1,0:T(8,128)(2,1)S(1)}, u32[]{:S(2)}, u32[]{:S(2)}) collective-permute-start(bf16[640,256]{1,0:T(8,128)(2,1)S(1)} %collective-permute-done.refs_0_), channel_id=1, source_target_pairs={{0,64},{1,65},{2,66},{3,67},{4,68},{5,69},{6,70},{7,71},{8,200},{9... | collective-permute-start | bytes 983048 | tf_op jit(solution)/shard_map/ppermute | solution.py:44
  47.7 23.2 %collective-permute-start.11 = (bf16[640,256]{1,0:T(8,128)(2,1)S(1)}, bf16[640,256]{1,0:T(8,128)(2,1)S(1)}, u32[]{:S(2)}, u32[]{:S(2)}) collective-permute-start(bf16[640,256]{1,0:T(8,128)(2,1)S(1)} %collective-permute-done.9.refs_2_), channel_id=1, source_target_pairs={{0,8},{1,9},{2,10},{3,11},{4,12},{5,13},{6,14},{7,15},{8,0},{9,1},... | collective-permute-start | bytes 983048 | tf_op jit(solution)/shard_map/ppermute | solution.py:44
  51.9 20.5 %collective-permute-start.2 = (bf16[640,256]{1,0:T(8,128)(2,1)S(1)}, bf16[640,256]{1,0:T(8,128)(2,1)}, u32[]{:S(2)}, u32[]{:S(2)}) collective-permute-start(bf16[640,256]{1,0:T(8,128)(2,1)S(1)} %collective-permute-done.1.refs_0_), channel_id=1, source_target_pairs={{0,64},{1,65},{2,66},{3,67},{4,68},{5,69},{6,70},{7,71},{8,200},{9... | collective-permute-start | bytes 983048 | tf_op jit(solution)/shard_map/ppermute | solution.py:44
  56.3 24.8 %collective-permute-start.18 = (bf16[640,256]{1,0:T(8,128)(2,1)S(1)}, bf16[640,256]{1,0:T(8,128)(2,1)S(1)}, u32[]{:S(2)}, u32[]{:S(2)}) collective-permute-start(bf16[640,256]{1,0:T(8,128)(2,1)S(1)} %collective-permute-done.8.refs_1_), channel_id=1, source_target_pairs={{0,64},{1,65},{2,66},{3,67},{4,68},{5,69},{6,70},{7,71},{8,200},{9... | collective-permute-start | bytes 983048 | tf_op jit(solution)/shard_map/ppermute | solution.py:44
  57.1 24.7 %collective-permute-start.22 = (bf16[640,256]{1,0:T(8,128)(2,1)S(1)}, bf16[640,256]{1,0:T(8,128)(2,1)}, u32[]{:S(2)}, u32[]{:S(2)}) collective-permute-start(bf16[640,256]{1,0:T(8,128)(2,1)S(1)} %collective-permute-done.1.refs_0_), channel_id=1, source_target_pairs={{0,16},{1,17},{2,18},{3,19},{4,20},{5,21},{6,22},{7,23},{8,56},{9,... | collective-permute-start | bytes 983048 | tf_op jit(solution)/shard_map/ppermute | solution.py:44
  57.5 24.5 %collective-permute-start.17 = (bf16[640,256]{1,0:T(8,128)(2,1)S(1)}, bf16[640,256]{1,0:T(8,128)(2,1)}, u32[]{:S(2)}, u32[]{:S(2)}) collective-permute-start(bf16[640,256]{1,0:T(8,128)(2,1)S(1)} %collective-permute-done.1.refs_0_), channel_id=1, source_target_pairs={{0,8},{1,9},{2,10},{3,11},{4,12},{5,13},{6,14},{7,15},{8,0},{9,1},... | collective-permute-start | bytes 983048 | tf_op jit(solution)/shard_map/ppermute | solution.py:44
  71.7 13.6 %collective-permute-start.12 = (bf16[640,256]{1,0:T(8,128)(2,1)S(1)}, bf16[640,256]{1,0:T(8,128)(2,1)S(1)}, u32[]{:S(2)}, u32[]{:S(2)}) collective-permute-start(bf16[640,256]{1,0:T(8,128)(2,1)S(1)} %collective-permute-done.10.refs_3_), channel_id=1, source_target_pairs={{0,8},{1,9},{2,10},{3,11},{4,12},{5,13},{6,14},{7,15},{8,0},{9,1},... | collective-permute-start | bytes 983048 | tf_op jit(solution)/shard_map/ppermute | solution.py:44
  72.4 16.5 %collective-permute-start.14 = (bf16[640,256]{1,0:T(8,128)(2,1)S(1)}, bf16[640,256]{1,0:T(8,128)(2,1)S(1)}, u32[]{:S(2)}, u32[]{:S(2)}) collective-permute-start(bf16[640,256]{1,0:T(8,128)(2,1)S(1)} %collective-permute-done.13.refs_6_), channel_id=1, source_target_pairs={{0,8},{1,9},{2,10},{3,11},{4,12},{5,13},{6,14},{7,15},{8,0},{9,1},... | collective-permute-start | bytes 983048 | tf_op jit(solution)/shard_map/ppermute | solution.py:44
  81.9 10.4 %collective-permute-start.24 = (bf16[640,256]{1,0:T(8,128)(2,1)S(1)}, bf16[640,256]{1,0:T(8,128)(2,1)}, u32[]{:S(2)}, u32[]{:S(2)}) collective-permute-start(bf16[640,256]{1,0:T(8,128)(2,1)S(1)} %collective-permute-done.18.refs_1_), channel_id=1, source_target_pairs={{0,16},{1,17},{2,18},{3,19},{4,20},{5,21},{6,22},{7,23},{8,56},{9,... | collective-permute-start | bytes 983048 | tf_op jit(solution)/shard_map/ppermute | solution.py:44
  81.9 13.9 %collective-permute-start.19 = (bf16[640,256]{1,0:T(8,128)(2,1)S(1)}, bf16[640,256]{1,0:T(8,128)(2,1)}, u32[]{:S(2)}, u32[]{:S(2)}) collective-permute-start(bf16[640,256]{1,0:T(8,128)(2,1)S(1)} %collective-permute-done.18.refs_1_), channel_id=1, source_target_pairs={{0,8},{1,9},{2,10},{3,11},{4,12},{5,13},{6,14},{7,15},{8,0},{9,1},... | collective-permute-start | bytes 983048 | tf_op jit(solution)/shard_map/ppermute | solution.py:44
  90.7 12.2 %collective-permute-start.23 = (bf16[640,256]{1,0:T(8,128)(2,1)}, bf16[640,256]{1,0:T(8,128)(2,1)}, u32[]{:S(2)}, u32[]{:S(2)}) collective-permute-start(bf16[640,256]{1,0:T(8,128)(2,1)} %collective-permute-done.22.refs_2_), channel_id=1, source_target_pairs={{0,8},{1,9},{2,10},{3,11},{4,12},{5,13},{6,14},{7,15},{8,0},{9,1},... | collective-permute-start | bytes 983048 | tf_op jit(solution)/shard_map/ppermute | solution.py:44
  92.3 14.6 %collective-permute-start.3 = (bf16[640,256]{1,0:T(8,128)(2,1)}, bf16[640,256]{1,0:T(8,128)(2,1)}, u32[]{:S(2)}, u32[]{:S(2)}) collective-permute-start(bf16[640,256]{1,0:T(8,128)(2,1)} %collective-permute-done.2.refs_0_), channel_id=1, source_target_pairs={{0,8},{1,9},{2,10},{3,11},{4,12},{5,13},{6,14},{7,15},{8,0},{9,1},... | collective-permute-start | bytes 983048 | tf_op jit(solution)/shard_map/ppermute | solution.py:44
  95.9 14.0 %collective-permute-start.28 = (bf16[640,256]{1,0:T(8,128)(2,1)}, bf16[640,256]{1,0:T(8,128)(2,1)}, u32[]{:S(2)}, u32[]{:S(2)}) collective-permute-start(bf16[640,256]{1,0:T(8,128)(2,1)} %collective-permute-done.24.refs_3_), channel_id=1, source_target_pairs={{0,16},{1,17},{2,18},{3,19},{4,20},{5,21},{6,22},{7,23},{8,56},{9,... | collective-permute-start | bytes 983048 | tf_op jit(solution)/shard_map/ppermute | solution.py:44
  95.9 14.0 %collective-permute-start.21 = (bf16[640,256]{1,0:T(8,128)(2,1)}, bf16[640,256]{1,0:T(8,128)(2,1)}, u32[]{:S(2)}, u32[]{:S(2)}) collective-permute-start(bf16[640,256]{1,0:T(8,128)(2,1)} %collective-permute-done.19.refs_1_), channel_id=1, source_target_pairs={{0,16},{1,17},{2,18},{3,19},{4,20},{5,21},{6,22},{7,23},{8,56},{9,... | collective-permute-start | bytes 983048 | tf_op jit(solution)/shard_map/ppermute | solution.py:44
  99.8 10.7 %collective-permute-start.25 = (bf16[640,256]{1,0:T(8,128)(2,1)}, bf16[640,256]{1,0:T(8,128)(2,1)S(1)}, u32[]{:S(2)}, u32[]{:S(2)}) collective-permute-start(bf16[640,256]{1,0:T(8,128)(2,1)} %collective-permute-done.24.refs_3_), channel_id=1, source_target_pairs={{0,8},{1,9},{2,10},{3,11},{4,12},{5,13},{6,14},{7,15},{8,0},{9,1},... | collective-permute-start | bytes 983048 | tf_op jit(solution)/shard_map/ppermute | solution.py:44
  110.4 13.6 %collective-permute-start.27 = (bf16[640,256]{1,0:T(8,128)(2,1)}, bf16[640,256]{1,0:T(8,128)(2,1)S(1)}, u32[]{:S(2)}, u32[]{:S(2)}) collective-permute-start(bf16[640,256]{1,0:T(8,128)(2,1)} %collective-permute-done.26.refs_6_), channel_id=1, source_target_pairs={{0,8},{1,9},{2,10},{3,11},{4,12},{5,13},{6,14},{7,15},{8,0},{9,1},... | collective-permute-start | bytes 983048 | tf_op jit(solution)/shard_map/ppermute | solution.py:44
  110.5 13.5 %collective-permute-start.29 = (bf16[640,256]{1,0:T(8,128)(2,1)}, bf16[640,256]{1,0:T(8,128)(2,1)S(1)}, u32[]{:S(2)}, u32[]{:S(2)}) collective-permute-start(bf16[640,256]{1,0:T(8,128)(2,1)} %collective-permute-done.28.refs_7_), channel_id=1, source_target_pairs={{0,8},{1,9},{2,10},{3,11},{4,12},{5,13},{6,14},{7,15},{8,0},{9,1},... | collective-permute-start | bytes 983048 | tf_op jit(solution)/shard_map/ppermute | solution.py:44
  114.2 14.5 %collective-permute-start.6 = (bf16[640,256]{1,0:T(8,128)(2,1)S(1)}, bf16[640,256]{1,0:T(8,128)(2,1)S(1)}, u32[]{:S(2)}, u32[]{:S(2)}) collective-permute-start(bf16[640,256]{1,0:T(8,128)(2,1)S(1)} %copy-done.23), channel_id=1, source_target_pairs={{0,8},{1,9},{2,10},{3,11},{4,12},{5,13},{6,14},{7,15},{8,0},{9,1},... | collective-permute-start | bytes 983048 | tf_op jit(solution)/shard_map/ppermute | solution.py:44
  115.8 12.9 %collective-permute-start.7 = (bf16[640,256]{1,0:T(8,128)(2,1)S(1)}, bf16[640,256]{1,0:T(8,128)(2,1)S(1)}, u32[]{:S(2)}, u32[]{:S(2)}) collective-permute-start(bf16[640,256]{1,0:T(8,128)(2,1)S(1)} %collective-permute-done.5.refs_3_), channel_id=1, source_target_pairs={{0,8},{1,9},{2,10},{3,11},{4,12},{5,13},{6,14},{7,15},{8,0},{9,1},... | collective-permute-start | bytes 983048 | tf_op jit(solution)/shard_map/ppermute | solution.py:44
  117.6 11.2 %collective-permute-start.16 = (bf16[640,256]{1,0:T(8,128)(2,1)S(1)}, bf16[640,256]{1,0:T(8,128)(2,1)S(1)}, u32[]{:S(2)}, u32[]{:S(2)}) collective-permute-start(bf16[640,256]{1,0:T(8,128)(2,1)S(1)} %collective-permute-done.15.refs_6_), channel_id=1, source_target_pairs={{0,8},{1,9},{2,10},{3,11},{4,12},{5,13},{6,14},{7,15},{8,0},{9,1},... | collective-permute-start | bytes 983048 | tf_op jit(solution)/shard_map/ppermute | solution.py:44
  (33 other events, 273.0 us)
Sparse Core Ops, SparseCore 0:
  10.0 61.9 all-gather.2

commit v2 on v1

--- a/solution.py
+++ b/solution.py
@@ -83,28 +83,56 @@
     return lax.rem(value, jnp.int32(length))
 
 
-def block_kernel(dz, places, left_ref, *refs):
-    count = len(places)
-    pieces, gamma_ref = refs[:count], refs[count]
+def join(left_ref, right_ref, out_ref):
+    half = left_ref.shape[-1]
+    out_ref[:, :half] = left_ref[...]
+    out_ref[:, half:] = right_ref[...]
+
+
+def side_by_side(first, second):
+    height, width = first.shape
+    return pl.pallas_call(
+        join,
+        out_shape=jax.ShapeDtypeStruct((height, 2 * width), first.dtype),
+        compiler_params=pltpu.CompilerParams(vmem_limit_bytes=4 * 2**20),
+        name="join_shard",
+    )(first, second)
+
+
+def block_kernel(dz, places, operands, height, left_ref, *refs):
+    arrays, gamma_ref = refs[:operands], refs[operands]
     out_ref, right, old, new, sems = refs[-5:]
-    height, width = pieces[0].shape
+    width = arrays[0].shape[-1]
     row, col = lax.axis_index("row"), lax.axis_index("col")
     zh, x, core = lax.div(row, jnp.int32(X * CORE)), rem(lax.div(row, jnp.int32(CORE)), X), rem(row, CORE)
     way = 2 * core - 1
     turn = rem(zh + dz[0] + dz[1] * way + 2 * ZH - lax.div(col, jnp.int32(2)), ZH)
     low, high = rem(turn, 2), lax.div(turn, jnp.int32(2))
-    columns = pl.ds(pl.multiple_of((low * 2 + high) * height, 128), height)
-    copies = [pltpu.make_async_copy(gamma_ref.at[:, columns], old, sems.at[count])]
-    for index, (piece, (dx, other_core)) in enumerate(zip(pieces, places)):
+    start = (low * 2 + high) * height
+    spots = []
+    for dx, other_core in (place[2:] for place in places):
         part = rem(core + other_core, CORE) * Y + rem(x + dx[0] + dx[1] * way + 2 * X - 2 * high, X)
-        place = pl.ds(pl.multiple_of(part * width, width), width)
-        copies.append(pltpu.make_async_copy(piece, right.at[:, place], sems.at[index]))
-    for copy in copies:
-        copy.start()
-    for copy in copies:
-        copy.wait()
-    for first in range(0, height, 256):
-        size = min(256, height - first)
+        spots.append(pl.ds(pl.multiple_of(part * width, width), width))
+    chunks = [(first, min(256, height - first)) for first in range(0, height, 256)]
+    coming = []
+    for turn_of, (first, size) in enumerate(chunks):
+        columns = pl.ds(pl.multiple_of(start + first, 128), size)
+        copies = [pltpu.make_async_copy(gamma_ref.at[:, columns], old.at[:, pl.ds(first, size)], sems.at[turn_of, 0])]
+        for index, ((array, skip, _, _), spot) in enumerate(zip(places, spots)):
+            copies.append(
+                pltpu.make_async_copy(
+                    arrays[array].at[pl.ds(skip * height + first, size), :],
+                    right.at[pl.ds(first, size), spot],
+                    sems.at[turn_of, 1 + index],
+                )
+            )
+        for copy in copies:
+            copy.start()
+        coming.append(copies)
+    going = []
+    for turn_of, (first, size) in enumerate(chunks):
+        for copy in coming[turn_of]:
+            copy.wait()
         commutator = lax.dot_general(
             left_ref[...],
             right[first : first + size, :],
@@ -114,22 +142,32 @@
         new[:, first : first + size] = (
             old[:, first : first + size].astype(jnp.float32) + euler_step * commutator
         ).astype(jnp.bfloat16)
-    back = pltpu.make_async_copy(new, out_ref.at[:, columns], sems.at[count + 1])
-    back.start()
-    back.wait()
-
-
-def block_step(dz, places, left, pieces, gamma, out):
-    count = len(pieces)
-    height, width = pieces[0].shape
+        columns = pl.ds(pl.multiple_of(start + first, 128), size)
+        copy = pltpu.make_async_copy(new.at[:, pl.ds(first, size)], out_ref.at[:, columns], sems.at[turn_of, 1 + len(places)])
+        copy.start()
+        going.append(copy)
+    for copy in going:
+        copy.wait()
+
+
+def block_step(dz, pieces, left, gamma, out):
+    arrays = []
+    places = []
+    for array, skip, dx, core in pieces:
+        known = [index for index, had in enumerate(arrays) if had is array]
+        if not known:
+            known = [len(arrays)]
+            arrays.append(array)
+        places.append((known[0], skip, dx, core))
+    height, count, width = left.shape[0], len(pieces), arrays[0].shape[-1]
     anywhere = pl.BlockSpec(memory_space=pl.ANY)
-    operands = [left, *pieces, gamma]
+    operands = [left, *arrays, gamma]
     aliases = {}
     if out is not None:
         aliases = {len(operands): 0}
         operands.append(out)
     return pl.pallas_call(
-        functools.partial(block_kernel, dz, places),
+        functools.partial(block_kernel, dz, places, len(arrays), height),
         in_specs=[
             pl.BlockSpec(memory_space=pltpu.VMEM),
             *[anywhere] * (len(operands) - 1),
@@ -141,7 +179,7 @@
             pltpu.VMEM((height, count * width), jnp.bfloat16),
             pltpu.VMEM((height, height), jnp.bfloat16),
             pltpu.VMEM((height, height), jnp.bfloat16),
-            pltpu.SemaphoreType.DMA((count + 2,)),
+            pltpu.SemaphoreType.DMA((3, count + 2)),
         ],
         compiler_params=pltpu.CompilerParams(vmem_limit_bytes=20 * 2**20),
         cost_estimate=pl.CostEstimate(
@@ -154,38 +192,52 @@
 
 
 HERE, BACK, AHEAD, ACROSS = (0, 0), (0, 1), (0, -1), (2, 0)
-ALIKE = [(HERE, 0), (HERE, 1), (BACK, 0), (BACK, 1), (AHEAD, 1), (AHEAD, 0), (ACROSS, 0), (ACROSS, 1)]
-DIRECT = [(HERE, 0), (HERE, 1), (BACK, 0), (BACK, 1), (AHEAD, 0), (AHEAD, 1), (ACROSS, 0), (ACROSS, 1)]
-SWAPPED = [(dx, 1 - core) for dx, core in DIRECT]
 
 
 def per_device(eta_ladder, gamma_ladder, occupation, gamma):
     weights = 1.0 - 0.5 * occupation.astype(jnp.float32)
-    shard = jnp.concatenate([gamma_ladder, eta_ladder], 1)
+    shard = side_by_side(gamma_ladder, eta_ladder)
     gathered = lax.all_gather(shard, "col")
     left = left_panel_of(gathered, weights)
+    height = shard.shape[0]
 
     p = send(shard, TO_HOME)
     ps = other(p)
-    za, zb = send(p, ALONG_Z), send(ps, ALONG_Z)
     xp, xps = send(p, ALONG_X), send(ps, ALONG_X)
+    zz = send(jnp.concatenate([p, ps], 0), ALONG_Z)
     fxp = send(xp, ALONG_X)
-    z2 = send(za, ALONG_Z)
-    sa, sb = other(za), other(zb)
+    zz = after(zz, xps, fxp)
+    zs = other(zz)
+    z2 = send(zz[:height], ALONG_Z)
     z2s = other(z2)
-    xza, xzb = send(za, ALONG_X), send(zb, ALONG_X)
-    xsa, xsb = send(sa, ALONG_X), send(sb, ALONG_X)
-    fxza, fxzb = send(xza, ALONG_X), send(xzb, ALONG_X)
+    xzz, xzs = send(zz, ALONG_X), send(zs, ALONG_X)
+    fxzz = send(xzz, ALONG_X)
     xz2, xz2s = send(z2, ALONG_X), send(z2s, ALONG_X)
-    block0 = [p, ps, xp, xps, other(xp), other(xps), fxp, other(fxp)]
-    out = block_step(HERE, ALIKE, left, block0, gamma, None)
+
+    def alike(mine, swapped, x_mine, x_swapped, fx_mine):
+        return [
+            (mine, 0, HERE, 0),
+            (swapped, 0, HERE, 1),
+            (x_mine, 0, BACK, 0),
+            (x_swapped, 0, BACK, 1),
+            (other(x_mine), 0, AHEAD, 1),
+            (other(x_swapped), 0, AHEAD, 0),
+            (fx_mine, 0, ACROSS, 0),
+            (other(fx_mine), 0, ACROSS, 1),
+        ]
+
+    def both(arrays, first_core):
+        return [
+            (array, half, dx, core)
+            for array, dx in zip(arrays, (HERE, BACK, AHEAD, ACROSS))
+            for half, core in ((0, first_core), (1, 1 - first_core))
+        ]
+
+    out = block_step(HERE, alike(p, ps, xp, xps, fxp), left, gamma, None)
+    out = block_step(BACK, both([zz, xzz, other(xzs), fxzz], 0), left, gamma, out)
     fxz2 = send(after(xz2, out), ALONG_X)
-    blocka = [za, zb, xza, xzb, other(xsa), other(xsb), fxza, fxzb]
-    blockb = [sa, sb, xsa, xsb, other(xza), other(xzb), other(fxza), other(fxzb)]
-    block2 = [z2, z2s, xz2, xz2s, other(xz2), other(xz2s), fxz2, other(fxz2)]
-    out = block_step(BACK, DIRECT, left, blocka, gamma, out)
-    out = block_step(AHEAD, SWAPPED, left, blockb, gamma, out)
-    return block_step(ACROSS, ALIKE, left, block2, gamma, out)
+    out = block_step(AHEAD, both([zs, xzs, other(xzz), other(fxzz)], 1), left, gamma, out)
+    return block_step(ACROSS, alike(z2, z2s, xz2, xz2s, fxz2), left, gamma, out)
 
 
 def solution(mesh):

time: 140 us -> 139 us (level)
  starting transfers between devices: 81.7 us -> 64.7 us
  waiting for transfers between devices: 13 us -> 26.2 us
  Pallas kernels: 18.4 us -> 25.9 us
  local copies, waits for them, and re-layouts: 12.6 us -> 7.38 us
    ppermute x32 -> x24, starting transfers between devices: 81.7 us -> 64.6 us  [send(): return lax.ppermute(value, AXES, way)]
    ppermute x32 -> x24, waiting for transfers between devices: 13 us -> 26.2 us  [send(): return lax.ppermute(value, AXES, way)]
    pallas_call x4 -> x5, Pallas kernels: 17.5 us -> 25 us  [the longest x4 24.2 us: block_step(): pl.pallas_call(functools.partial(block_kernel, dz, places, len(arrays), h...]
    unnamed x49 -> x40, local copies, waits for them, and re-layouts: 11 us -> 7.36 us
    concatenate x1 -> x0, local copies, waits for them, and re-layouts: 1.59 us -> none  [per_device(): shard = jnp.concatenate([gamma_ladder, eta_ladder], 1)]
  transfers between devices with their start and end apart: 33 -> 25, of which waited for: 4 -> 7; matrix products, arithmetic and copies ran while one was open for 0% -> 1% of each run, Pallas kernels for 10% -> 14%
where the time goes in v2:
time: 139 us; the launch traced here: 138 us
  starting transfers between devices  64.7 us (47%)
  waiting for transfers between devices  26.2 us (19%)
  Pallas kernels  25.9 us (19%)
  between operations  13.6 us (10%)
  local copies, waits for them, and re-layouts  7.38 us (5%)
    ppermute x24, starting transfers between devices, send(): return lax.ppermute(value, AXES, way)  64.6 us
    ppermute x24, waiting for transfers between devices, send(): return lax.ppermute(value, AXES, way)  26.2 us
    pallas_call x4, Pallas kernels, block_step(): pl.pallas_call(functools.partial(block_kernel, dz, places, len(arrays), h...  24.2 us
    unnamed x40, local copies, waits for them, and re-layouts  7.36 us
  transfers between devices with their start and end apart: 25, of which 7 were waited for; matrix products, arithmetic and copies ran while one was open for 1% of the time, Pallas kernels for 14%

profile of v2, /device:TPU:25, one launch (start us, length us, event | category | flops | bytes accessed | tf_op | source)
XLA Modules:
  0.0 138.5 jit_solution(17081357072421167828)
XLA Ops:
  9.2 10.0 %collective-permute-start = (bf16[640,256]{1,0:T(8,128)(2,1)}, bf16[640,256]{1,0:T(8,128)(2,1)S(1)}, u32[]{:S(2)}, u32[]{:S(2)}) collective-permute-start(bf16[640,256]{1,0:T(8,128)(2,1)} %join_shard.1), channel_id=1, source_target_pairs={{0,0},{1,16},{2,32},{3,48},{4,8},{5,24},{6,40},{7,56},{8,160},{9,1... | collective-permute-start | bytes 983048 | tf_op jit(solution)/shard_map/ppermute | solution.py:44
  19.1 4.4 %collective-permute-done.refs_0_ = bf16[640,256]{1,0:T(8,128)(2,1)S(1)} collective-permute-done((bf16[640,256]{1,0:T(8,128)(2,1)}, bf16[640,256]{1,0:T(8,128)(2,1)S(1)}, u32[]{:S(2)}, u32[]{:S(2)}) %collective-permute-start) | collective-permute-done | bytes 327712 | tf_op jit(solution)/shard_map/ppermute | solution.py:44
  23.6 2.5 %collective-permute-start.1 = (bf16[640,256]{1,0:T(8,128)(2,1)S(1)}, bf16[640,256]{1,0:T(8,128)(2,1)S(1)}, u32[]{:S(2)}, u32[]{:S(2)}) collective-permute-start(bf16[640,256]{1,0:T(8,128)(2,1)S(1)} %collective-permute-done.refs_0_), channel_id=1, source_target_pairs={{0,8},{1,9},{2,10},{3,11},{4,12},{5,13},{6,14},{7,15},{8,0},{9,1},... | collective-permute-start | bytes 983048 | tf_op jit(solution)/shard_map/ppermute | solution.py:44
  26.1 8.1 %collective-permute-start.4 = (bf16[640,256]{1,0:T(8,128)(2,1)S(1)}, bf16[640,256]{1,0:T(8,128)(2,1)S(1)}, u32[]{:S(2)}, u32[]{:S(2)}) collective-permute-start(bf16[640,256]{1,0:T(8,128)(2,1)S(1)} %collective-permute-done.refs_0_), channel_id=1, source_target_pairs={{0,16},{1,17},{2,18},{3,19},{4,20},{5,21},{6,22},{7,23},{8,56},{9,... | collective-permute-start | bytes 983048 | tf_op jit(solution)/shard_map/ppermute | solution.py:44
  34.3 11.3 %collective-permute-start.2 = (bf16[1280,256]{1,0:T(8,128)(2,1)S(1)}, bf16[1280,256]{1,0:T(8,128)(2,1)S(1)}, u32[]{:S(2)}, u32[]{:S(2)}) collective-permute-start(bf16[1280,256]{1,0:T(8,128)(2,1)S(1)} %pad_maximum_fusion), channel_id=1, source_target_pairs={{0,64},{1,65},{2,66},{3,67},{4,68},{5,69},{6,70},{7,71},{8,200},{9... | collective-permute-start | bytes 1966088 | tf_op jit(solution)/shard_map/ppermute | solution.py:44
  45.6 1.6 %collective-permute-start.3 = (bf16[640,256]{1,0:T(8,128)(2,1)S(1)}, bf16[640,256]{1,0:T(8,128)(2,1)S(1)}, u32[]{:S(2)}, u32[]{:S(2)}) collective-permute-start(bf16[640,256]{1,0:T(8,128)(2,1)S(1)} %collective-permute-done.1.refs_1_), channel_id=1, source_target_pairs={{0,16},{1,17},{2,18},{3,19},{4,20},{5,21},{6,22},{7,23},{8,56},{9,... | collective-permute-start | bytes 983048 | tf_op jit(solution)/shard_map/ppermute | solution.py:44
  47.2 4.7 %collective-permute-done.3.refs_3_ = bf16[640,256]{1,0:T(8,128)(2,1)S(1)} collective-permute-done((bf16[640,256]{1,0:T(8,128)(2,1)S(1)}, bf16[640,256]{1,0:T(8,128)(2,1)S(1)}, u32[]{:S(2)}, u32[]{:S(2)}) %collective-permute-start.3) | collective-permute-done | bytes 327712 | tf_op jit(solution)/shard_map/ppermute | solution.py:44
  51.9 3.5 %collective-permute-done.5.refs_6_ = bf16[640,256]{1,0:T(8,128)(2,1)} collective-permute-done((bf16[640,256]{1,0:T(8,128)(2,1)S(1)}, bf16[640,256]{1,0:T(8,128)(2,1)}, u32[]{:S(2)}, u32[]{:S(2)}) %collective-permute-start.5) | collective-permute-done | bytes 327712 | tf_op jit(solution)/shard_map/ppermute | solution.py:44
  55.4 17.3 %collective-permute-start.13 = (bf16[1280,256]{1,0:T(8,128)(2,1)S(1)}, bf16[1280,256]{1,0:T(8,128)(2,1)S(1)}, u32[]{:S(2)}, u32[]{:S(2)}) collective-permute-start(bf16[1280,256]{1,0:T(8,128)(2,1)S(1)} %collective-permute-done.2.refs_0_), channel_id=1, source_target_pairs={{0,8},{1,9},{2,10},{3,11},{4,12},{5,13},{6,14},{7,15},{8,0},{9,1},... | collective-permute-start | bytes 1966088 | tf_op jit(solution)/shard_map/ppermute | solution.py:44
  73.5 0.9 collective-permute-done.13.refs_0_
  76.1 1.3 collective-permute-start.6
  78.2 4.4 %collective-permute-done.12.refs_1_ = bf16[1280,256]{1,0:T(8,128)(2,1)} collective-permute-done((bf16[1280,256]{1,0:T(8,128)(2,1)S(1)}, bf16[1280,256]{1,0:T(8,128)(2,1)}, u32[]{:S(2)}, u32[]{:S(2)}) %collective-permute-start.12) | collective-permute-done | bytes 655392 | tf_op jit(solution)/shard_map/ppermute | solution.py:44
  82.6 2.0 %collective-permute-start.16 = (bf16[1280,256]{1,0:T(8,128)(2,1)}, bf16[1280,256]{1,0:T(8,128)(2,1)}, u32[]{:S(2)}, u32[]{:S(2)}) collective-permute-start(bf16[1280,256]{1,0:T(8,128)(2,1)} %collective-permute-done.12.refs_1_), channel_id=1, source_target_pairs={{0,16},{1,17},{2,18},{3,19},{4,20},{5,21},{6,22},{7,23},{8,56},{9,... | collective-permute-start | bytes 1966088 | tf_op jit(solution)/shard_map/ppermute | solution.py:44
  85.5 4.1 %collective-permute-done.14.refs_1_ = bf16[1280,256]{1,0:T(8,128)(2,1)} collective-permute-done((bf16[1280,256]{1,0:T(8,128)(2,1)S(1)}, bf16[1280,256]{1,0:T(8,128)(2,1)}, u32[]{:S(2)}, u32[]{:S(2)}) %collective-permute-start.14) | collective-permute-done | bytes 655392 | tf_op jit(solution)/shard_map/ppermute | solution.py:44
  89.6 2.1 %collective-permute-start.15 = (bf16[1280,256]{1,0:T(8,128)(2,1)}, bf16[1280,256]{1,0:T(8,128)(2,1)}, u32[]{:S(2)}, u32[]{:S(2)}) collective-permute-start(bf16[1280,256]{1,0:T(8,128)(2,1)} %collective-permute-done.14.refs_1_), channel_id=1, source_target_pairs={{0,8},{1,9},{2,10},{3,11},{4,12},{5,13},{6,14},{7,15},{8,0},{9,1},... | collective-permute-start | bytes 1966088 | tf_op jit(solution)/shard_map/ppermute | solution.py:44
  94.4 1.7 %copy-done.1 = bf16[5120,256]{1,0:T(8,128)(2,1)S(1)} copy-done((bf16[5120,256]{1,0:T(8,128)(2,1)S(1)}, bf16[5120,256]{1,0:T(8,128)(2,1)}, u32[]{:S(2)}) %copy-start.1) | copy-done | bytes 2621464
  97.7 1.0 collective-permute-start.23
  98.7 6.0 %block_step.4.refs_5_ = bf16[640,2560]{1,0:T(8,128)(2,1)} custom-call(bf16[640,2048]{1,0:T(8,128)(2,1)S(1)} %weigh_left.1.left_ref, bf16[640,256]{1,0:T(8,128)(2,1)S(1)} %copy-done.5, bf16[640,256]{1,0:T(8,128)(2,1)S(1)} %copy-done.7, bf16[640,256]{1,0:T(8,128)(2,1)S(1)} %copy-done.11, bf16[640,256]{1,0:T(8,128)(2,1)S(1)} %copy-done.13, ...), custom_call_target="tpu_custom_call" | custom-call | flops 1677721600 | bytes 6881280 | tf_op jit(solution)/shard_map/block_step/pallas_call | solution.py:169
  104.8 6.2 %block_step.5.refs_5_ = bf16[640,2560]{1,0:T(8,128)(2,1)} custom-call(bf16[640,2048]{1,0:T(8,128)(2,1)S(1)} %weigh_left.1.left_ref, bf16[1280,256]{1,0:T(8,128)(2,1)S(1)} %copy-done.3, bf16[1280,256]{1,0:T(8,128)(2,1)} %collective-permute-done.12.refs_1_, bf16[1280,256]{1,0:T(8,128)(2,1)} %collective-permute-done.15.refs_2_, ...), custom_call_target="tpu_custom_call", output_to_operand_aliasing={{}: (6, {})} | custom-call | flops 1677721600 | bytes 6881280 | tf_op jit(solution)/shard_map/block_step/pallas_call | solution.py:169
  111.1 1.9 %collective-permute-start.20 = (bf16[640,256]{1,0:T(8,128)(2,1)}, bf16[640,256]{1,0:T(8,128)(2,1)S(1)}, u32[]{:S(2)}, u32[]{:S(2)}) collective-permute-start(bf16[640,256]{1,0:T(8,128)(2,1)} %collective-permute-done.8.refs_2_), channel_id=1, source_target_pairs={{0,16},{1,17},{2,18},{3,19},{4,20},{5,21},{6,22},{7,23},{8,56},{9,... | collective-permute-start | bytes 983048 | tf_op jit(solution)/shard_map/ppermute | solution.py:44
  113.4 4.1 %collective-permute-done.20.refs_6_ = bf16[640,256]{1,0:T(8,128)(2,1)S(1)} collective-permute-done((bf16[640,256]{1,0:T(8,128)(2,1)}, bf16[640,256]{1,0:T(8,128)(2,1)S(1)}, u32[]{:S(2)}, u32[]{:S(2)}) %collective-permute-start.20) | collective-permute-done | bytes 327712 | tf_op jit(solution)/shard_map/ppermute | solution.py:44
  117.6 2.1 %collective-permute-start.21 = (bf16[640,256]{1,0:T(8,128)(2,1)S(1)}, bf16[640,256]{1,0:T(8,128)(2,1)S(1)}, u32[]{:S(2)}, u32[]{:S(2)}) collective-permute-start(bf16[640,256]{1,0:T(8,128)(2,1)S(1)} %collective-permute-done.20.refs_6_), channel_id=1, source_target_pairs={{0,8},{1,9},{2,10},{3,11},{4,12},{5,13},{6,14},{7,15},{8,0},{9,1},... | collective-permute-start | bytes 983048 | tf_op jit(solution)/shard_map/ppermute | solution.py:44
  119.7 6.0 %block_step.6.refs_9_ = bf16[640,2560]{1,0:T(8,128)(2,1)} custom-call(bf16[640,2048]{1,0:T(8,128)(2,1)S(1)} %weigh_left.1.left_ref, bf16[1280,256]{1,0:T(8,128)(2,1)S(1)} %copy-done.9, bf16[1280,256]{1,0:T(8,128)(2,1)} %collective-permute-done.14.refs_1_, bf16[1280,256]{1,0:T(8,128)(2,1)S(1)} %collective-permute-done.22.refs_2_, ...), custom_call_target="tpu_custom_call", output_to_operand_aliasing={{}: (6, {})} | custom-call | flops 1677721600 | bytes 6881280 | tf_op jit(solution)/shard_map/block_step/pallas_call | solution.py:169
  125.7 6.0 %block_step.7 = bf16[640,2560]{1,0:T(8,128)(2,1)} custom-call(bf16[640,2048]{1,0:T(8,128)(2,1)S(1)} %weigh_left.1.left_ref, bf16[640,256]{1,0:T(8,128)(2,1)} %collective-permute-done.6.refs_0_, bf16[640,256]{1,0:T(8,128)(2,1)} %collective-permute-done.7.refs_1_, bf16[640,256]{1,0:T(8,128)(2,1)} %collective-permute-done.8.refs_2_, ...), custom_call_target="tpu_custom_call", output_to_operand_aliasing={{}: (10, {})} | custom-call | flops 1677721600 | bytes 6881280 | tf_op jit(solution)/shard_map/block_step/pallas_call | solution.py:169
  (76 shorter events, 11.6 us)
Async XLA Ops:
  6.5 87.8 %all-gather.3.cloned.1.call-start = ((), (), s32[]{:S(2)}) async-start(), calls=%async_computation | async-start | bytes 2949120 | tf_op jit(solution)/shard_map/all_gather | solution.py:200
  9.2 14.4 %collective-permute-start = (bf16[640,256]{1,0:T(8,128)(2,1)}, bf16[640,256]{1,0:T(8,128)(2,1)S(1)}, u32[]{:S(2)}, u32[]{:S(2)}) collective-permute-start(bf16[640,256]{1,0:T(8,128)(2,1)} %join_shard.1), channel_id=1, source_target_pairs={{0,0},{1,16},{2,32},{3,48},{4,8},{5,24},{6,40},{7,56},{8,160},{9,1... | collective-permute-start | bytes 983048 | tf_op jit(solution)/shard_map/ppermute | solution.py:44
  23.6 10.6 %collective-permute-start.1 = (bf16[640,256]{1,0:T(8,128)(2,1)S(1)}, bf16[640,256]{1,0:T(8,128)(2,1)S(1)}, u32[]{:S(2)}, u32[]{:S(2)}) collective-permute-start(bf16[640,256]{1,0:T(8,128)(2,1)S(1)} %collective-permute-done.refs_0_), channel_id=1, source_target_pairs={{0,8},{1,9},{2,10},{3,11},{4,12},{5,13},{6,14},{7,15},{8,0},{9,1},... | collective-permute-start | bytes 983048 | tf_op jit(solution)/shard_map/ppermute | solution.py:44
  26.1 21.1 %collective-permute-start.4 = (bf16[640,256]{1,0:T(8,128)(2,1)S(1)}, bf16[640,256]{1,0:T(8,128)(2,1)S(1)}, u32[]{:S(2)}, u32[]{:S(2)}) collective-permute-start(bf16[640,256]{1,0:T(8,128)(2,1)S(1)} %collective-permute-done.refs_0_), channel_id=1, source_target_pairs={{0,16},{1,17},{2,18},{3,19},{4,20},{5,21},{6,22},{7,23},{8,56},{9,... | collective-permute-start | bytes 983048 | tf_op jit(solution)/shard_map/ppermute | solution.py:44
  34.3 21.1 %collective-permute-start.2 = (bf16[1280,256]{1,0:T(8,128)(2,1)S(1)}, bf16[1280,256]{1,0:T(8,128)(2,1)S(1)}, u32[]{:S(2)}, u32[]{:S(2)}) collective-permute-start(bf16[1280,256]{1,0:T(8,128)(2,1)S(1)} %pad_maximum_fusion), channel_id=1, source_target_pairs={{0,64},{1,65},{2,66},{3,67},{4,68},{5,69},{6,70},{7,71},{8,200},{9... | collective-permute-start | bytes 1966088 | tf_op jit(solution)/shard_map/ppermute | solution.py:44
  45.6 6.3 %collective-permute-start.3 = (bf16[640,256]{1,0:T(8,128)(2,1)S(1)}, bf16[640,256]{1,0:T(8,128)(2,1)S(1)}, u32[]{:S(2)}, u32[]{:S(2)}) collective-permute-start(bf16[640,256]{1,0:T(8,128)(2,1)S(1)} %collective-permute-done.1.refs_1_), channel_id=1, source_target_pairs={{0,16},{1,17},{2,18},{3,19},{4,20},{5,21},{6,22},{7,23},{8,56},{9,... | collective-permute-start | bytes 983048 | tf_op jit(solution)/shard_map/ppermute | solution.py:44
  47.2 8.2 %collective-permute-start.5 = (bf16[640,256]{1,0:T(8,128)(2,1)S(1)}, bf16[640,256]{1,0:T(8,128)(2,1)}, u32[]{:S(2)}, u32[]{:S(2)}) collective-permute-start(bf16[640,256]{1,0:T(8,128)(2,1)S(1)} %collective-permute-done.4.refs_2_), channel_id=1, source_target_pairs={{0,16},{1,17},{2,18},{3,19},{4,20},{5,21},{6,22},{7,23},{8,56},{9,... | collective-permute-start | bytes 983048 | tf_op jit(solution)/shard_map/ppermute | solution.py:44
  55.4 19.1 %collective-permute-start.13 = (bf16[1280,256]{1,0:T(8,128)(2,1)S(1)}, bf16[1280,256]{1,0:T(8,128)(2,1)S(1)}, u32[]{:S(2)}, u32[]{:S(2)}) collective-permute-start(bf16[1280,256]{1,0:T(8,128)(2,1)S(1)} %collective-permute-done.2.refs_0_), channel_id=1, source_target_pairs={{0,8},{1,9},{2,10},{3,11},{4,12},{5,13},{6,14},{7,15},{8,0},{9,1},... | collective-permute-start | bytes 1966088 | tf_op jit(solution)/shard_map/ppermute | solution.py:44
  72.8 9.8 %collective-permute-start.12 = (bf16[1280,256]{1,0:T(8,128)(2,1)S(1)}, bf16[1280,256]{1,0:T(8,128)(2,1)}, u32[]{:S(2)}, u32[]{:S(2)}) collective-permute-start(bf16[1280,256]{1,0:T(8,128)(2,1)S(1)} %collective-permute-done.2.refs_0_), channel_id=1, source_target_pairs={{0,16},{1,17},{2,18},{3,19},{4,20},{5,21},{6,22},{7,23},{8,56},{9,... | collective-permute-start | bytes 1966088 | tf_op jit(solution)/shard_map/ppermute | solution.py:44
  74.5 15.1 %collective-permute-start.14 = (bf16[1280,256]{1,0:T(8,128)(2,1)S(1)}, bf16[1280,256]{1,0:T(8,128)(2,1)}, u32[]{:S(2)}, u32[]{:S(2)}) collective-permute-start(bf16[1280,256]{1,0:T(8,128)(2,1)S(1)} %collective-permute-done.13.refs_0_), channel_id=1, source_target_pairs={{0,16},{1,17},{2,18},{3,19},{4,20},{5,21},{6,22},{7,23},{8,56},{9,... | collective-permute-start | bytes 1966088 | tf_op jit(solution)/shard_map/ppermute | solution.py:44
  76.1 15.5 %collective-permute-start.6 = (bf16[640,256]{1,0:T(8,128)(2,1)S(1)}, bf16[640,256]{1,0:T(8,128)(2,1)}, u32[]{:S(2)}, u32[]{:S(2)}) collective-permute-start(bf16[640,256]{1,0:T(8,128)(2,1)S(1)} %slice.3), channel_id=1, source_target_pairs={{0,64},{1,65},{2,66},{3,67},{4,68},{5,69},{6,70},{7,71},{8,200},{9... | collective-permute-start | bytes 983048 | tf_op jit(solution)/shard_map/ppermute | solution.py:44
  77.5 14.2 %collective-permute-start.17 = (bf16[640,256]{1,0:T(8,128)(2,1)S(1)}, bf16[640,256]{1,0:T(8,128)(2,1)S(1)}, u32[]{:S(2)}, u32[]{:S(2)}) collective-permute-start(bf16[640,256]{1,0:T(8,128)(2,1)S(1)} %collective-permute-done.4.refs_2_), channel_id=1, source_target_pairs={{0,8},{1,9},{2,10},{3,11},{4,12},{5,13},{6,14},{7,15},{8,0},{9,1},... | collective-permute-start | bytes 983048 | tf_op jit(solution)/shard_map/ppermute | solution.py:44
  82.6 15.1 %collective-permute-start.16 = (bf16[1280,256]{1,0:T(8,128)(2,1)}, bf16[1280,256]{1,0:T(8,128)(2,1)}, u32[]{:S(2)}, u32[]{:S(2)}) collective-permute-start(bf16[1280,256]{1,0:T(8,128)(2,1)} %collective-permute-done.12.refs_1_), channel_id=1, source_target_pairs={{0,16},{1,17},{2,18},{3,19},{4,20},{5,21},{6,22},{7,23},{8,56},{9,... | collective-permute-start | bytes 1966088 | tf_op jit(solution)/shard_map/ppermute | solution.py:44
  84.6 8.3 %collective-permute-start.18 = (bf16[640,256]{1,0:T(8,128)(2,1)S(1)}, bf16[640,256]{1,0:T(8,128)(2,1)S(1)}, u32[]{:S(2)}, u32[]{:S(2)}) collective-permute-start(bf16[640,256]{1,0:T(8,128)(2,1)S(1)} %collective-permute-done.3.refs_3_), channel_id=1, source_target_pairs={{0,8},{1,9},{2,10},{3,11},{4,12},{5,13},{6,14},{7,15},{8,0},{9,1},... | collective-permute-start | bytes 983048 | tf_op jit(solution)/shard_map/ppermute | solution.py:44
  89.6 15.2 %collective-permute-start.15 = (bf16[1280,256]{1,0:T(8,128)(2,1)}, bf16[1280,256]{1,0:T(8,128)(2,1)}, u32[]{:S(2)}, u32[]{:S(2)}) collective-permute-start(bf16[1280,256]{1,0:T(8,128)(2,1)} %collective-permute-done.14.refs_1_), channel_id=1, source_target_pairs={{0,8},{1,9},{2,10},{3,11},{4,12},{5,13},{6,14},{7,15},{8,0},{9,1},... | collective-permute-start | bytes 1966088 | tf_op jit(solution)/shard_map/ppermute | solution.py:44
  91.7 5.4 %collective-permute-start.7 = (bf16[640,256]{1,0:T(8,128)(2,1)}, bf16[640,256]{1,0:T(8,128)(2,1)}, u32[]{:S(2)}, u32[]{:S(2)}) collective-permute-start(bf16[640,256]{1,0:T(8,128)(2,1)} %collective-permute-done.6.refs_0_), channel_id=1, source_target_pairs={{0,8},{1,9},{2,10},{3,11},{4,12},{5,13},{6,14},{7,15},{8,0},{9,1},... | collective-permute-start | bytes 983048 | tf_op jit(solution)/shard_map/ppermute | solution.py:44
  93.7 17.4 %collective-permute-start.8 = (bf16[640,256]{1,0:T(8,128)(2,1)}, bf16[640,256]{1,0:T(8,128)(2,1)}, u32[]{:S(2)}, u32[]{:S(2)}) collective-permute-start(bf16[640,256]{1,0:T(8,128)(2,1)} %collective-permute-done.6.refs_0_), channel_id=1, source_target_pairs={{0,16},{1,17},{2,18},{3,19},{4,20},{5,21},{6,22},{7,23},{8,56},{9,... | collective-permute-start | bytes 983048 | tf_op jit(solution)/shard_map/ppermute | solution.py:44
  97.1 15.9 %collective-permute-start.9 = (bf16[640,256]{1,0:T(8,128)(2,1)}, bf16[640,256]{1,0:T(8,128)(2,1)S(1)}, u32[]{:S(2)}, u32[]{:S(2)}) collective-permute-start(bf16[640,256]{1,0:T(8,128)(2,1)} %collective-permute-done.7.refs_1_), channel_id=1, source_target_pairs={{0,16},{1,17},{2,18},{3,19},{4,20},{5,21},{6,22},{7,23},{8,56},{9,... | collective-permute-start | bytes 983048 | tf_op jit(solution)/shard_map/ppermute | solution.py:44
  97.7 21.9 %collective-permute-start.22 = (bf16[1280,256]{1,0:T(8,128)(2,1)}, bf16[1280,256]{1,0:T(8,128)(2,1)S(1)}, u32[]{:S(2)}, u32[]{:S(2)}) collective-permute-start(bf16[1280,256]{1,0:T(8,128)(2,1)} %collective-permute-done.12.refs_1_), channel_id=1, source_target_pairs={{0,8},{1,9},{2,10},{3,11},{4,12},{5,13},{6,14},{7,15},{8,0},{9,1},... | collective-permute-start | bytes 1966088 | tf_op jit(solution)/shard_map/ppermute | solution.py:44
  97.7 21.9 %collective-permute-start.23 = (bf16[1280,256]{1,0:T(8,128)(2,1)}, bf16[1280,256]{1,0:T(8,128)(2,1)S(1)}, u32[]{:S(2)}, u32[]{:S(2)}) collective-permute-start(bf16[1280,256]{1,0:T(8,128)(2,1)} %collective-permute-done.16.refs_3_), channel_id=1, source_target_pairs={{0,8},{1,9},{2,10},{3,11},{4,12},{5,13},{6,14},{7,15},{8,0},{9,1},... | collective-permute-start | bytes 1966088 | tf_op jit(solution)/shard_map/ppermute | solution.py:44
  111.1 6.5 %collective-permute-start.20 = (bf16[640,256]{1,0:T(8,128)(2,1)}, bf16[640,256]{1,0:T(8,128)(2,1)S(1)}, u32[]{:S(2)}, u32[]{:S(2)}) collective-permute-start(bf16[640,256]{1,0:T(8,128)(2,1)} %collective-permute-done.8.refs_2_), channel_id=1, source_target_pairs={{0,16},{1,17},{2,18},{3,19},{4,20},{5,21},{6,22},{7,23},{8,56},{9,... | collective-permute-start | bytes 983048 | tf_op jit(solution)/shard_map/ppermute | solution.py:44
  112.9 12.7 %collective-permute-start.10 = (bf16[640,256]{1,0:T(8,128)(2,1)}, bf16[640,256]{1,0:T(8,128)(2,1)S(1)}, u32[]{:S(2)}, u32[]{:S(2)}) collective-permute-start(bf16[640,256]{1,0:T(8,128)(2,1)} %collective-permute-done.8.refs_2_), channel_id=1, source_target_pairs={{0,8},{1,9},{2,10},{3,11},{4,12},{5,13},{6,14},{7,15},{8,0},{9,1},... | collective-permute-start | bytes 983048 | tf_op jit(solution)/shard_map/ppermute | solution.py:44
  112.9 12.7 %collective-permute-start.11 = (bf16[640,256]{1,0:T(8,128)(2,1)S(1)}, bf16[640,256]{1,0:T(8,128)(2,1)S(1)}, u32[]{:S(2)}, u32[]{:S(2)}) collective-permute-start(bf16[640,256]{1,0:T(8,128)(2,1)S(1)} %collective-permute-done.9.refs_3_), channel_id=1, source_target_pairs={{0,8},{1,9},{2,10},{3,11},{4,12},{5,13},{6,14},{7,15},{8,0},{9,1},... | collective-permute-start | bytes 983048 | tf_op jit(solution)/shard_map/ppermute | solution.py:44
  117.6 8.1 %collective-permute-start.21 = (bf16[640,256]{1,0:T(8,128)(2,1)S(1)}, bf16[640,256]{1,0:T(8,128)(2,1)S(1)}, u32[]{:S(2)}, u32[]{:S(2)}) collective-permute-start(bf16[640,256]{1,0:T(8,128)(2,1)S(1)} %collective-permute-done.20.refs_6_), channel_id=1, source_target_pairs={{0,8},{1,9},{2,10},{3,11},{4,12},{5,13},{6,14},{7,15},{8,0},{9,1},... | collective-permute-start | bytes 983048 | tf_op jit(solution)/shard_map/ppermute | solution.py:44
  (21 other events, 235.1 us)
Sparse Core Ops, SparseCore 0:
  9.3 61.1 all-gather.2

commit v3 on v2

v3 whole, which is shorter than its diff:
```python
import functools

import jax
import jax.numpy as jnp
from jax import lax
from jax.experimental import pallas as pl
from jax.experimental.pallas import tpu as pltpu
from jax.sharding import PartitionSpec as P

euler_step = 0.5
ZH, X, CORE, ZL, Y = 4, 4, 2, 2, 4
AXES = ("row", "col")


def every_device():
    for zh in range(ZH):
        for x in range(X):
            for core in range(CORE):
                for zl in range(ZL):
                    for y in range(Y):
                        yield zh, x, core, zl, y


def flat(zh, x, core, zl, y):
    return ((((zh % ZH) * X + x % X) * CORE + core % CORE) * ZL + zl % ZL) * Y + y % Y


def home(zh, x, core, zl, y):
    group = zh * 2 + x // 2
    return flat(zh + 2 * core + x % 2, y + 2 * core, zl, group // Y, group % Y)


def pairs(target):
    return [(flat(*d), target(*d)) for d in every_device()]


TO_HOME = pairs(home)
ALONG_Z = pairs(lambda zh, x, core, zl, y: flat(zh + 1 - 2 * core, x, core, zl, y))
ALONG_X = pairs(lambda zh, x, core, zl, y: flat(zh, x + 1 - 2 * core, core, zl, y))
OTHER_ZL = pairs(lambda zh, x, core, zl, y: flat(zh, x, core, zl + 1, y))
OTHER_CORE = pairs(lambda zh, x, core, zl, y: flat(zh, x, core + 1, zl, y))


def send(value, way):
    return lax.ppermute(value, AXES, way)


def other(value):
    return send(value, OTHER_CORE)


def after(value, *earlier):
    return lax.optimization_barrier((value, *earlier))[0]


def weigh(panel_ref, weights_ref, out_ref):
    half = panel_ref.shape[-1] // 2
    k = pl.program_id(0)
    side = rem(lax.div(lax.axis_index("col"), jnp.int32(Y)) + k, ZL)
    weights = weights_ref[side * Y + lax.div(k, jnp.int32(ZL))]
    panel = panel_ref[...].astype(jnp.float32)
    out_ref[:, :half] = (panel[:, half:] * weights).astype(jnp.bfloat16)
    out_ref[:, half:] = (panel[:, :half] * weights).astype(jnp.bfloat16)


def left_panel_of(gathered, weights):
    parts, height, width = gathered.shape
    return pl.pallas_call(
        weigh,
        grid=(parts,),
        in_specs=[
            pl.BlockSpec((None, height, width), lambda k: (k, 0, 0)),
            pl.BlockSpec((parts, 1, width // 2), lambda k: (0, 0, 0)),
        ],
        out_specs=pl.BlockSpec((None, height, width), lambda k: (k, 0, 0)),
        out_shape=jax.ShapeDtypeStruct((parts, height, width), jnp.bfloat16),
        compiler_params=pltpu.CompilerParams(vmem_limit_bytes=8 * 2**20),
        cost_estimate=pl.CostEstimate(
            flops=parts * height * width, bytes_accessed=4 * parts * height * width, transcendentals=0
        ),
        name="weigh_left",
    )(gathered, weights.reshape(parts, 1, width // 2))


def rem(value, length):
    return lax.rem(value, jnp.int32(length))


def join(left_ref, right_ref, out_ref):
    half = left_ref.shape[-1]
    out_ref[:, :half] = left_ref[...]
    out_ref[:, half:] = right_ref[...]


def side_by_side(first, second):
    height, width = first.shape
    return pl.pallas_call(
        join,
        out_shape=jax.ShapeDtypeStruct((height, 2 * width), first.dtype),
        compiler_params=pltpu.CompilerParams(vmem_limit_bytes=4 * 2**20),
        name="join_shard",
    )(first, second)


def block_kernel(dz, places, operands, height, left_ref, *refs):
    arrays, gamma_ref = refs[:operands], refs[operands]
    out_ref, old, new, sems = refs[-4:]
    row, col = lax.axis_index("row"), lax.axis_index("col")
    zh, x, core = lax.div(row, jnp.int32(X * CORE)), rem(lax.div(row, jnp.int32(CORE)), X), rem(row, CORE)
    way = 2 * core - 1
    turn = rem(zh + dz[0] + dz[1] * way + 2 * ZH - lax.div(col, jnp.int32(2)), ZH)
    low, high = rem(turn, 2), lax.div(turn, jnp.int32(2))
    columns = pl.ds(pl.multiple_of((low * 2 + high) * height, 128), height)
    come = pltpu.make_async_copy(gamma_ref.at[:, columns], old, sems.at[0])
    come.start()
    left, right = [], []
    for array, skip, dx, other_core in places:
        zl, y = rem(core + other_core, CORE), rem(x + dx[0] + dx[1] * way + 2 * X - 2 * high, X)
        left.append(left_ref[y * ZL + rem(zl + lax.div(col, jnp.int32(Y)), ZL)])
        right.append(arrays[array][skip * height : (skip + 1) * height, :])
    commutator = lax.dot_general(
        jnp.concatenate(left, 1),
        jnp.concatenate(right, 1),
        (((1,), (1,)), ((), ())),
        preferred_element_type=jnp.float32,
    )
    come.wait()
    new[...] = (old[...].astype(jnp.float32) + euler_step * commutator).astype(jnp.bfloat16)
    go = pltpu.make_async_copy(new, out_ref.at[:, columns], sems.at[1])
    go.start()
    go.wait()


def block_step(dz, pieces, left, gamma, out):
    arrays = []
    places = []
    for array, skip, dx, core in pieces:
        known = [index for index, had in enumerate(arrays) if had is array]
        if not known:
            known = [len(arrays)]
            arrays.append(array)
        places.append((known[0], skip, dx, core))
    height, count, width = left.shape[1], len(pieces), arrays[0].shape[-1]
    anywhere = pl.BlockSpec(memory_space=pl.ANY)
    operands = [left, *arrays, gamma]
    aliases = {}
    if out is not None:
        aliases = {len(operands): 0}
        operands.append(out)
    return pl.pallas_call(
        functools.partial(block_kernel, dz, places, len(arrays), height),
        in_specs=[
            *[pl.BlockSpec(memory_space=pltpu.VMEM)] * (1 + len(arrays)),
            *[anywhere] * (len(operands) - 1 - len(arrays)),
        ],
        out_specs=anywhere,
        out_shape=jax.ShapeDtypeStruct(gamma.shape, gamma.dtype),
        input_output_aliases=aliases,
        scratch_shapes=[
            pltpu.VMEM((height, height), jnp.bfloat16),
            pltpu.VMEM((height, height), jnp.bfloat16),
            pltpu.SemaphoreType.DMA((2,)),
        ],
        compiler_params=pltpu.CompilerParams(vmem_limit_bytes=20 * 2**20),
        cost_estimate=pl.CostEstimate(
            flops=height * height, bytes_accessed=height * height, transcendentals=0
        ),
        name="block_step",
    )(*operands)


HERE, BACK, AHEAD, ACROSS = (0, 0), (0, 1), (0, -1), (2, 0)


def per_device(eta_ladder, gamma_ladder, occupation, gamma):
    weights = 1.0 - 0.5 * occupation.astype(jnp.float32)
    shard = side_by_side(gamma_ladder, eta_ladder)
    height, width = shard.shape
    other_zl = send(shard, OTHER_ZL)

    p = send(shard, TO_HOME)
    ps = other(p)
    sides = jnp.stack([shard, after(other_zl, ps)])
    alike_y = [[zl * Y + y for y in range(Y)] for zl in range(ZL)]
    gathered = lax.all_gather(sides, "col", axis_index_groups=alike_y).reshape(ZL * Y, height, width)
    xp, xps = send(p, ALONG_X), send(ps, ALONG_X)
    zz = send(jnp.concatenate([p, ps], 0), ALONG_Z)
    fxp = send(xp, ALONG_X)
    zz = after(zz, xps, fxp)
    zs = other(zz)
    z2 = send(zz[:height], ALONG_Z)
    z2s = other(z2)
    xzz, xzs = send(zz, ALONG_X), send(zs, ALONG_X)
    fxzz = send(xzz, ALONG_X)
    xz2, xz2s = send(z2, ALONG_X), send(z2s, ALONG_X)

    left = left_panel_of(after(gathered, z2s), weights)

    def both(arrays, first_core):
        return [
            (array, half, dx, core)
            for array, dx in zip(arrays, (HERE, BACK, AHEAD, ACROSS))
            for half, core in ((0, first_core), (1, 1 - first_core))
        ]

    def alike(mine, swapped, x_mine, x_swapped, their_x, their_x_swapped, fx_mine, their_fx):
        return [
            (mine, 0, HERE, 0),
            (swapped, 0, HERE, 1),
            (x_mine, 0, BACK, 0),
            (x_swapped, 0, BACK, 1),
            (their_x, 0, AHEAD, 1),
            (their_x_swapped, 0, AHEAD, 0),
            (fx_mine, 0, ACROSS, 0),
            (their_fx, 0, ACROSS, 1),
        ]

    out = block_step(HERE, alike(p, ps, xp, xps, other(xp), other(xps), fxp, other(fxp)), left, gamma, None)
    their_fxzz = other(after(fxzz, out))
    out = block_step(BACK, both([zz, xzz, other(xzs), fxzz], 0), left, gamma, out)
    fxz2 = send(after(xz2, out), ALONG_X)
    out = block_step(AHEAD, both([after(zs, xz2s), xzs, other(xzz), their_fxzz], 1), left, gamma, out)
    their_fx = other(after(fxz2, out))
    return block_step(ACROSS, alike(z2, z2s, xz2, xz2s, other(xz2), other(xz2s), fxz2, their_fx), left, gamma, out)


def solution(mesh):
    placed = (P("row", "col"), P("row", "col"), P(), P("row", "col"))
    return jax.shard_map(
        per_device, mesh=mesh, in_specs=placed, out_specs=P("row", "col"), check_vma=False
    )
```

time: 139 us -> 115 us (0.83)
  starting transfers between devices: 64.7 us -> 48.3 us
  Pallas kernels: 25.9 us -> 18.5 us
  local copies, waits for them, and re-layouts: 7.38 us -> 5.53 us
    ppermute x24 -> x25, starting transfers between devices: 64.6 us -> 48.3 us  [send(): return lax.ppermute(value, AXES, way)]
    pallas_call x4, Pallas kernels: 24.2 us -> 17.7 us  [block_step(): pl.pallas_call(functools.partial(block_kernel, dz, places, len(arrays), h...]
    unnamed x40 -> x30, local copies, waits for them, and re-layouts: 7.36 us -> 5.51 us
    ppermute x24 -> x25, waiting for transfers between devices: 26.2 us -> 27 us  [send(): return lax.ppermute(value, AXES, way)]
  transfers between devices with their start and end apart: 25 -> 26, of which waited for: 7 -> 10; matrix products, arithmetic and copies ran while one was open for 1% -> 1% of each run, Pallas kernels for 14% -> 13%
where the time goes in v3:
time: 115 us
  starting transfers between devices  48.3 us (42%)
  waiting for transfers between devices  27 us (23%)
  Pallas kernels  18.5 us (16%)
  between operations  13.6 us (12%)
  local copies, waits for them, and re-layouts  5.53 us (5%)
  other arithmetic  1.99 us (2%)
    ppermute x25, starting transfers between devices, send(): return lax.ppermute(value, AXES, way)  48.3 us
    ppermute x25, waiting for transfers between devices, send(): return lax.ppermute(value, AXES, way)  27 us
    pallas_call x4, Pallas kernels, block_step(): pl.pallas_call(functools.partial(block_kernel, dz, places, len(arrays), h...  17.7 us
    unnamed x30, local copies, waits for them, and re-layouts  5.51 us
  transfers between devices with their start and end apart: 26, of which 10 were waited for; matrix products, arithmetic and copies ran while one was open for 1% of the time, Pallas kernels for 13%

profile of v3, /device:TPU:25, one launch (start us, length us, event | category | flops | bytes accessed | tf_op | source)
XLA Modules:
  0.0 114.9 jit_solution(4395670191149739919)
XLA Ops:
  7.5 0.9 copy-done.13
  8.4 10.0 %collective-permute-start.1 = (bf16[640,256]{1,0:T(8,128)(2,1)S(1)}, bf16[640,256]{1,0:T(8,128)(2,1)}, u32[]{:S(2)}, u32[]{:S(2)}) collective-permute-start(bf16[640,256]{1,0:T(8,128)(2,1)S(1)} %join_shard.1), channel_id=1, source_target_pairs={{0,0},{1,16},{2,32},{3,48},{4,8},{5,24},{6,40},{7,56},{8,160},{9,1... | collective-permute-start | bytes 983048 | tf_op jit(solution)/shard_map/ppermute | solution.py:45
  18.5 3.9 %collective-permute-done.1.refs_0_ = bf16[640,256]{1,0:T(8,128)(2,1)} collective-permute-done((bf16[640,256]{1,0:T(8,128)(2,1)S(1)}, bf16[640,256]{1,0:T(8,128)(2,1)}, u32[]{:S(2)}, u32[]{:S(2)}) %collective-permute-start.1) | collective-permute-done | bytes 327712 | tf_op jit(solution)/shard_map/ppermute | solution.py:45
  22.5 2.7 %collective-permute-start.2 = (bf16[640,256]{1,0:T(8,128)(2,1)}, bf16[640,256]{1,0:T(8,128)(2,1)S(1)}, u32[]{:S(2)}, u32[]{:S(2)}) collective-permute-start(bf16[640,256]{1,0:T(8,128)(2,1)} %collective-permute-done.1.refs_0_), channel_id=1, source_target_pairs={{0,8},{1,9},{2,10},{3,11},{4,12},{5,13},{6,14},{7,15},{8,0},{9,1},... | collective-permute-start | bytes 983048 | tf_op jit(solution)/shard_map/ppermute | solution.py:45
  26.6 0.9 pad_maximum_fusion
  27.6 8.6 %collective-permute-start.5 = (bf16[640,256]{1,0:T(8,128)(2,1)}, bf16[640,256]{1,0:T(8,128)(2,1)}, u32[]{:S(2)}, u32[]{:S(2)}) collective-permute-start(bf16[640,256]{1,0:T(8,128)(2,1)} %collective-permute-done.1.refs_0_), channel_id=1, source_target_pairs={{0,16},{1,17},{2,18},{3,19},{4,20},{5,21},{6,22},{7,23},{8,56},{9,... | collective-permute-start | bytes 983048 | tf_op jit(solution)/shard_map/ppermute | solution.py:45
  36.1 1.0 pad_maximum_fusion.1
  37.2 9.9 %collective-permute-start.3 = (bf16[1280,256]{1,0:T(8,128)(2,1)S(1)}, bf16[1280,256]{1,0:T(8,128)(2,1)S(1)}, u32[]{:S(2)}, u32[]{:S(2)}) collective-permute-start(bf16[1280,256]{1,0:T(8,128)(2,1)S(1)} %pad_maximum_fusion.1), channel_id=1, source_target_pairs={{0,64},{1,65},{2,66},{3,67},{4,68},{5,69},{6,70},{7,71},{8,200},{9... | collective-permute-start | bytes 1966088 | tf_op jit(solution)/shard_map/ppermute | solution.py:45
  47.2 6.4 %collective-permute-done.4.refs_3_ = bf16[640,256]{1,0:T(8,128)(2,1)} collective-permute-done((bf16[640,256]{1,0:T(8,128)(2,1)}, bf16[640,256]{1,0:T(8,128)(2,1)}, u32[]{:S(2)}, u32[]{:S(2)}) %collective-permute-start.4) | collective-permute-done | bytes 327712 | tf_op jit(solution)/shard_map/ppermute | solution.py:45
  53.6 3.6 %collective-permute-done.6.refs_6_ = bf16[640,256]{1,0:T(8,128)(2,1)} collective-permute-done((bf16[640,256]{1,0:T(8,128)(2,1)}, bf16[640,256]{1,0:T(8,128)(2,1)}, u32[]{:S(2)}, u32[]{:S(2)}) %collective-permute-start.6) | collective-permute-done | bytes 327712 | tf_op jit(solution)/shard_map/ppermute | solution.py:45
  57.2 3.3 %collective-permute-done.3.refs_0_ = bf16[1280,256]{1,0:T(8,128)(2,1)S(1)} collective-permute-done((bf16[1280,256]{1,0:T(8,128)(2,1)S(1)}, bf16[1280,256]{1,0:T(8,128)(2,1)S(1)}, u32[]{:S(2)}, u32[]{:S(2)}) %collective-permute-start.3) | collective-permute-done | bytes 655392 | tf_op jit(solution)/shard_map/ppermute | solution.py:45
  60.5 1.5 %collective-permute-start.13 = (bf16[1280,256]{1,0:T(8,128)(2,1)S(1)}, bf16[1280,256]{1,0:T(8,128)(2,1)}, u32[]{:S(2)}, u32[]{:S(2)}) collective-permute-start(bf16[1280,256]{1,0:T(8,128)(2,1)S(1)} %collective-permute-done.3.refs_0_), channel_id=1, source_target_pairs={{0,16},{1,17},{2,18},{3,19},{4,20},{5,21},{6,22},{7,23},{8,56},{9,... | collective-permute-start | bytes 1966088 | tf_op jit(solution)/shard_map/ppermute | solution.py:45
  62.9 4.0 %collective-permute-start.7 = (bf16[640,256]{1,0:T(8,128)(2,1)S(1)}, bf16[640,256]{1,0:T(8,128)(2,1)S(1)}, u32[]{:S(2)}, u32[]{:S(2)}) collective-permute-start(bf16[640,256]{1,0:T(8,128)(2,1)S(1)} %slice.3), channel_id=1, source_target_pairs={{0,64},{1,65},{2,66},{3,67},{4,68},{5,69},{6,70},{7,71},{8,200},{9... | collective-permute-start | bytes 983048 | tf_op jit(solution)/shard_map/ppermute | solution.py:45
  67.8 5.5 %collective-permute-done.7.refs_0_ = bf16[640,256]{1,0:T(8,128)(2,1)S(1)} collective-permute-done((bf16[640,256]{1,0:T(8,128)(2,1)S(1)}, bf16[640,256]{1,0:T(8,128)(2,1)S(1)}, u32[]{:S(2)}, u32[]{:S(2)}) %collective-permute-start.7) | collective-permute-done | bytes 327712 | tf_op jit(solution)/shard_map/ppermute | solution.py:45
  73.3 2.7 %collective-permute-start.17 = (bf16[1280,256]{1,0:T(8,128)(2,1)}, bf16[1280,256]{1,0:T(8,128)(2,1)}, u32[]{:S(2)}, u32[]{:S(2)}) collective-permute-start(bf16[1280,256]{1,0:T(8,128)(2,1)} %collective-permute-done.13.refs_1_), channel_id=1, source_target_pairs={{0,16},{1,17},{2,18},{3,19},{4,20},{5,21},{6,22},{7,23},{8,56},{9,... | collective-permute-start | bytes 1966088 | tf_op jit(solution)/shard_map/ppermute | solution.py:45
  77.4 2.6 %collective-permute-start.16 = (bf16[1280,256]{1,0:T(8,128)(2,1)}, bf16[1280,256]{1,0:T(8,128)(2,1)}, u32[]{:S(2)}, u32[]{:S(2)}) collective-permute-start(bf16[1280,256]{1,0:T(8,128)(2,1)} %collective-permute-done.15.refs_1_), channel_id=1, source_target_pairs={{0,8},{1,9},{2,10},{3,11},{4,12},{5,13},{6,14},{7,15},{8,0},{9,1},... | collective-permute-start | bytes 1966088 | tf_op jit(solution)/shard_map/ppermute | solution.py:45
  80.0 1.7 %copy-done.1 = bf16[8,640,256]{2,1,0:T(8,128)(2,1)S(1)} copy-done((bf16[8,640,256]{2,1,0:T(8,128)(2,1)S(1)}, bf16[8,640,256]{2,1,0:T(8,128)(2,1)}, u32[]{:S(2)}) %copy-start.1) | copy-done | bytes 2621464
  83.0 5.0 %block_step.4.refs_5_ = bf16[640,2560]{1,0:T(8,128)(2,1)} custom-call(bf16[8,640,256]{2,1,0:T(8,128)(2,1)S(1)} %weigh_left.1.left_ref, bf16[640,256]{1,0:T(8,128)(2,1)} %collective-permute-done.1.refs_0_, bf16[640,256]{1,0:T(8,128)(2,1)S(1)} %copy-done.5, bf16[640,256]{1,0:T(8,128)(2,1)} %collective-permute-done.5.refs_2_, ...), custom_call_target="tpu_custom_call" | custom-call | flops 409600 | bytes 409600 | tf_op jit(solution)/shard_map/block_step/pallas_call | solution.py:150
  88.5 2.4 %collective-permute-start.10 = (bf16[640,256]{1,0:T(8,128)(2,1)S(1)}, bf16[640,256]{1,0:T(8,128)(2,1)S(1)}, u32[]{:S(2)}, u32[]{:S(2)}) collective-permute-start(bf16[640,256]{1,0:T(8,128)(2,1)S(1)} %copy-done.11), channel_id=1, source_target_pairs={{0,16},{1,17},{2,18},{3,19},{4,20},{5,21},{6,22},{7,23},{8,56},{9,... | collective-permute-start | bytes 983048 | tf_op jit(solution)/shard_map/ppermute | solution.py:45
  90.9 4.9 %block_step.5.refs_5_ = bf16[640,2560]{1,0:T(8,128)(2,1)} custom-call(bf16[8,640,256]{2,1,0:T(8,128)(2,1)S(1)} %weigh_left.1.left_ref, bf16[1280,256]{1,0:T(8,128)(2,1)S(1)} %copy-done.3, bf16[1280,256]{1,0:T(8,128)(2,1)} %collective-permute-done.13.refs_1_, bf16[1280,256]{1,0:T(8,128)(2,1)} %collective-permute-done.16.refs_2_, ...), custom_call_target="tpu_custom_call", output_to_operand_aliasing={{}: (6, {})} | custom-call | flops 409600 | bytes 409600 | tf_op jit(solution)/shard_map/block_step/pallas_call | solution.py:150
  96.9 4.5 %block_step.6.refs_9_ = bf16[640,2560]{1,0:T(8,128)(2,1)} custom-call(bf16[8,640,256]{2,1,0:T(8,128)(2,1)S(1)} %weigh_left.1.left_ref, bf16[1280,256]{1,0:T(8,128)(2,1)S(1)} %copy-done.7, bf16[1280,256]{1,0:T(8,128)(2,1)} %collective-permute-done.15.refs_1_, bf16[1280,256]{1,0:T(8,128)(2,1)S(1)} %collective-permute-done.22.refs_2_, ...), custom_call_target="tpu_custom_call", output_to_operand_aliasing={{}: (6, {})} | custom-call | flops 409600 | bytes 409600 | tf_op jit(solution)/shard_map/block_step/pallas_call | solution.py:150
  102.1 1.3 %collective-permute-start.24 = (bf16[640,256]{1,0:T(8,128)(2,1)S(1)}, bf16[640,256]{1,0:T(8,128)(2,1)S(1)}, u32[]{:S(2)}, u32[]{:S(2)}) collective-permute-start(bf16[640,256]{1,0:T(8,128)(2,1)S(1)} %collective-permute-done.21.refs_6_), channel_id=1, source_target_pairs={{0,8},{1,9},{2,10},{3,11},{4,12},{5,13},{6,14},{7,15},{8,0},{9,1},... | collective-permute-start | bytes 983048 | tf_op jit(solution)/shard_map/ppermute | solution.py:45
  103.4 1.2 %collective-permute-done.24.refs_7_ = bf16[640,256]{1,0:T(8,128)(2,1)S(1)} collective-permute-done((bf16[640,256]{1,0:T(8,128)(2,1)S(1)}, bf16[640,256]{1,0:T(8,128)(2,1)S(1)}, u32[]{:S(2)}, u32[]{:S(2)}) %collective-permute-start.24) | collective-permute-done | bytes 327712 | tf_op jit(solution)/shard_map/ppermute | solution.py:45
  104.7 3.4 %block_step.7 = bf16[640,2560]{1,0:T(8,128)(2,1)} custom-call(bf16[8,640,256]{2,1,0:T(8,128)(2,1)S(1)} %weigh_left.1.left_ref, bf16[640,256]{1,0:T(8,128)(2,1)S(1)} %copy-done.9, bf16[640,256]{1,0:T(8,128)(2,1)S(1)} %copy-done.11, bf16[640,256]{1,0:T(8,128)(2,1)S(1)} %collective-permute-done.9.refs_2_, ...), custom_call_target="tpu_custom_call", output_to_operand_aliasing={{}: (10, {})} | custom-call | flops 409600 | bytes 409600 | tf_op jit(solution)/shard_map/block_step/pallas_call | solution.py:150
  (69 shorter events, 9.4 us)
Async XLA Ops:
  6.5 73.4 %all-gather.3.cloned.1.call-start = ((), (), s32[]{:S(2)}) async-start(), calls=%async_computation | async-start | bytes 3276800 | tf_op jit(solution)/shard_map/all_gather | solution.py:185
  8.4 14.0 %collective-permute-start.1 = (bf16[640,256]{1,0:T(8,128)(2,1)S(1)}, bf16[640,256]{1,0:T(8,128)(2,1)}, u32[]{:S(2)}, u32[]{:S(2)}) collective-permute-start(bf16[640,256]{1,0:T(8,128)(2,1)S(1)} %join_shard.1), channel_id=1, source_target_pairs={{0,0},{1,16},{2,32},{3,48},{4,8},{5,24},{6,40},{7,56},{8,160},{9,1... | collective-permute-start | bytes 983048 | tf_op jit(solution)/shard_map/ppermute | solution.py:45
  18.4 7.6 %collective-permute-start = (bf16[640,256]{1,0:T(8,128)(2,1)S(1)}, bf16[640,256]{1,0:T(8,128)(2,1)S(1)}, u32[]{:S(2)}, u32[]{:S(2)}) collective-permute-start(bf16[640,256]{1,0:T(8,128)(2,1)S(1)} %join_shard.1), channel_id=1, source_target_pairs={{0,4},{1,5},{2,6},{3,7},{4,0},{5,1},{6,2},{7,3},{8,12},{9,13},{10,... | collective-permute-start | bytes 983048 | tf_op jit(solution)/shard_map/ppermute | solution.py:45
  22.5 4.1 %collective-permute-start.2 = (bf16[640,256]{1,0:T(8,128)(2,1)}, bf16[640,256]{1,0:T(8,128)(2,1)S(1)}, u32[]{:S(2)}, u32[]{:S(2)}) collective-permute-start(bf16[640,256]{1,0:T(8,128)(2,1)} %collective-permute-done.1.refs_0_), channel_id=1, source_target_pairs={{0,8},{1,9},{2,10},{3,11},{4,12},{5,13},{6,14},{7,15},{8,0},{9,1},... | collective-permute-start | bytes 983048 | tf_op jit(solution)/shard_map/ppermute | solution.py:45
  27.6 19.6 %collective-permute-start.5 = (bf16[640,256]{1,0:T(8,128)(2,1)}, bf16[640,256]{1,0:T(8,128)(2,1)}, u32[]{:S(2)}, u32[]{:S(2)}) collective-permute-start(bf16[640,256]{1,0:T(8,128)(2,1)} %collective-permute-done.1.refs_0_), channel_id=1, source_target_pairs={{0,16},{1,17},{2,18},{3,19},{4,20},{5,21},{6,22},{7,23},{8,56},{9,... | collective-permute-start | bytes 983048 | tf_op jit(solution)/shard_map/ppermute | solution.py:45
  37.2 23.3 %collective-permute-start.3 = (bf16[1280,256]{1,0:T(8,128)(2,1)S(1)}, bf16[1280,256]{1,0:T(8,128)(2,1)S(1)}, u32[]{:S(2)}, u32[]{:S(2)}) collective-permute-start(bf16[1280,256]{1,0:T(8,128)(2,1)S(1)} %pad_maximum_fusion.1), channel_id=1, source_target_pairs={{0,64},{1,65},{2,66},{3,67},{4,68},{5,69},{6,70},{7,71},{8,200},{9... | collective-permute-start | bytes 1966088 | tf_op jit(solution)/shard_map/ppermute | solution.py:45
  47.1 6.4 %collective-permute-start.4 = (bf16[640,256]{1,0:T(8,128)(2,1)}, bf16[640,256]{1,0:T(8,128)(2,1)}, u32[]{:S(2)}, u32[]{:S(2)}) collective-permute-start(bf16[640,256]{1,0:T(8,128)(2,1)} %copy-done.4), channel_id=1, source_target_pairs={{0,16},{1,17},{2,18},{3,19},{4,20},{5,21},{6,22},{7,23},{8,56},{9,... | collective-permute-start | bytes 983048 | tf_op jit(solution)/shard_map/ppermute | solution.py:45
  47.1 10.0 %collective-permute-start.6 = (bf16[640,256]{1,0:T(8,128)(2,1)}, bf16[640,256]{1,0:T(8,128)(2,1)}, u32[]{:S(2)}, u32[]{:S(2)}) collective-permute-start(bf16[640,256]{1,0:T(8,128)(2,1)} %collective-permute-done.5.refs_2_), channel_id=1, source_target_pairs={{0,16},{1,17},{2,18},{3,19},{4,20},{5,21},{6,22},{7,23},{8,56},{9,... | collective-permute-start | bytes 983048 | tf_op jit(solution)/shard_map/ppermute | solution.py:45
  60.5 6.4 %collective-permute-start.14 = (bf16[1280,256]{1,0:T(8,128)(2,1)S(1)}, bf16[1280,256]{1,0:T(8,128)(2,1)S(1)}, u32[]{:S(2)}, u32[]{:S(2)}) collective-permute-start(bf16[1280,256]{1,0:T(8,128)(2,1)S(1)} %collective-permute-done.3.refs_0_), channel_id=1, source_target_pairs={{0,8},{1,9},{2,10},{3,11},{4,12},{5,13},{6,14},{7,15},{8,0},{9,1},... | collective-permute-start | bytes 1966088 | tf_op jit(solution)/shard_map/ppermute | solution.py:45
  60.5 12.8 %collective-permute-start.13 = (bf16[1280,256]{1,0:T(8,128)(2,1)S(1)}, bf16[1280,256]{1,0:T(8,128)(2,1)}, u32[]{:S(2)}, u32[]{:S(2)}) collective-permute-start(bf16[1280,256]{1,0:T(8,128)(2,1)S(1)} %collective-permute-done.3.refs_0_), channel_id=1, source_target_pairs={{0,16},{1,17},{2,18},{3,19},{4,20},{5,21},{6,22},{7,23},{8,56},{9,... | collective-permute-start | bytes 1966088 | tf_op jit(solution)/shard_map/ppermute | solution.py:45
  62.9 10.4 %collective-permute-start.7 = (bf16[640,256]{1,0:T(8,128)(2,1)S(1)}, bf16[640,256]{1,0:T(8,128)(2,1)S(1)}, u32[]{:S(2)}, u32[]{:S(2)}) collective-permute-start(bf16[640,256]{1,0:T(8,128)(2,1)S(1)} %slice.3), channel_id=1, source_target_pairs={{0,64},{1,65},{2,66},{3,67},{4,68},{5,69},{6,70},{7,71},{8,200},{9... | collective-permute-start | bytes 983048 | tf_op jit(solution)/shard_map/ppermute | solution.py:45
  66.9 10.4 %collective-permute-start.15 = (bf16[1280,256]{1,0:T(8,128)(2,1)S(1)}, bf16[1280,256]{1,0:T(8,128)(2,1)}, u32[]{:S(2)}, u32[]{:S(2)}) collective-permute-start(bf16[1280,256]{1,0:T(8,128)(2,1)S(1)} %collective-permute-done.14.refs_0_), channel_id=1, source_target_pairs={{0,16},{1,17},{2,18},{3,19},{4,20},{5,21},{6,22},{7,23},{8,56},{9,... | collective-permute-start | bytes 1966088 | tf_op jit(solution)/shard_map/ppermute | solution.py:45
  73.3 14.6 %collective-permute-start.17 = (bf16[1280,256]{1,0:T(8,128)(2,1)}, bf16[1280,256]{1,0:T(8,128)(2,1)}, u32[]{:S(2)}, u32[]{:S(2)}) collective-permute-start(bf16[1280,256]{1,0:T(8,128)(2,1)} %collective-permute-done.13.refs_1_), channel_id=1, source_target_pairs={{0,16},{1,17},{2,18},{3,19},{4,20},{5,21},{6,22},{7,23},{8,56},{9,... | collective-permute-start | bytes 1966088 | tf_op jit(solution)/shard_map/ppermute | solution.py:45
  76.0 6.5 %collective-permute-start.18 = (bf16[640,256]{1,0:T(8,128)(2,1)}, bf16[640,256]{1,0:T(8,128)(2,1)}, u32[]{:S(2)}, u32[]{:S(2)}) collective-permute-start(bf16[640,256]{1,0:T(8,128)(2,1)} %collective-permute-done.5.refs_2_), channel_id=1, source_target_pairs={{0,8},{1,9},{2,10},{3,11},{4,12},{5,13},{6,14},{7,15},{8,0},{9,1},... | collective-permute-start | bytes 983048 | tf_op jit(solution)/shard_map/ppermute | solution.py:45
  76.0 6.7 %collective-permute-start.19 = (bf16[640,256]{1,0:T(8,128)(2,1)}, bf16[640,256]{1,0:T(8,128)(2,1)}, u32[]{:S(2)}, u32[]{:S(2)}) collective-permute-start(bf16[640,256]{1,0:T(8,128)(2,1)} %collective-permute-done.4.refs_3_), channel_id=1, source_target_pairs={{0,8},{1,9},{2,10},{3,11},{4,12},{5,13},{6,14},{7,15},{8,0},{9,1},... | collective-permute-start | bytes 983048 | tf_op jit(solution)/shard_map/ppermute | solution.py:45
  76.5 6.4 %collective-permute-start.20 = (bf16[640,256]{1,0:T(8,128)(2,1)}, bf16[640,256]{1,0:T(8,128)(2,1)}, u32[]{:S(2)}, u32[]{:S(2)}) collective-permute-start(bf16[640,256]{1,0:T(8,128)(2,1)} %collective-permute-done.6.refs_6_), channel_id=1, source_target_pairs={{0,8},{1,9},{2,10},{3,11},{4,12},{5,13},{6,14},{7,15},{8,0},{9,1},... | collective-permute-start | bytes 983048 | tf_op jit(solution)/shard_map/ppermute | solution.py:45
  77.4 13.5 %collective-permute-start.16 = (bf16[1280,256]{1,0:T(8,128)(2,1)}, bf16[1280,256]{1,0:T(8,128)(2,1)}, u32[]{:S(2)}, u32[]{:S(2)}) collective-permute-start(bf16[1280,256]{1,0:T(8,128)(2,1)} %collective-permute-done.15.refs_1_), channel_id=1, source_target_pairs={{0,8},{1,9},{2,10},{3,11},{4,12},{5,13},{6,14},{7,15},{8,0},{9,1},... | collective-permute-start | bytes 1966088 | tf_op jit(solution)/shard_map/ppermute | solution.py:45
  82.7 13.1 %collective-permute-start.9 = (bf16[640,256]{1,0:T(8,128)(2,1)S(1)}, bf16[640,256]{1,0:T(8,128)(2,1)S(1)}, u32[]{:S(2)}, u32[]{:S(2)}) collective-permute-start(bf16[640,256]{1,0:T(8,128)(2,1)S(1)} %copy-done.9), channel_id=1, source_target_pairs={{0,16},{1,17},{2,18},{3,19},{4,20},{5,21},{6,22},{7,23},{8,56},{9,... | collective-permute-start | bytes 983048 | tf_op jit(solution)/shard_map/ppermute | solution.py:45
  82.7 14.2 %collective-permute-start.22 = (bf16[1280,256]{1,0:T(8,128)(2,1)}, bf16[1280,256]{1,0:T(8,128)(2,1)S(1)}, u32[]{:S(2)}, u32[]{:S(2)}) collective-permute-start(bf16[1280,256]{1,0:T(8,128)(2,1)} %collective-permute-done.13.refs_1_), channel_id=1, source_target_pairs={{0,8},{1,9},{2,10},{3,11},{4,12},{5,13},{6,14},{7,15},{8,0},{9,1},... | collective-permute-start | bytes 1966088 | tf_op jit(solution)/shard_map/ppermute | solution.py:45
  87.9 8.9 %collective-permute-start.23 = (bf16[1280,256]{1,0:T(8,128)(2,1)}, bf16[1280,256]{1,0:T(8,128)(2,1)S(1)}, u32[]{:S(2)}, u32[]{:S(2)}) collective-permute-start(bf16[1280,256]{1,0:T(8,128)(2,1)} %collective-permute-done.17.refs_3_), channel_id=1, source_target_pairs={{0,8},{1,9},{2,10},{3,11},{4,12},{5,13},{6,14},{7,15},{8,0},{9,1},... | collective-permute-start | bytes 1966088 | tf_op jit(solution)/shard_map/ppermute | solution.py:45
  88.5 7.5 %collective-permute-start.10 = (bf16[640,256]{1,0:T(8,128)(2,1)S(1)}, bf16[640,256]{1,0:T(8,128)(2,1)S(1)}, u32[]{:S(2)}, u32[]{:S(2)}) collective-permute-start(bf16[640,256]{1,0:T(8,128)(2,1)S(1)} %copy-done.11), channel_id=1, source_target_pairs={{0,16},{1,17},{2,18},{3,19},{4,20},{5,21},{6,22},{7,23},{8,56},{9,... | collective-permute-start | bytes 983048 | tf_op jit(solution)/shard_map/ppermute | solution.py:45
  95.8 6.3 %collective-permute-start.21 = (bf16[640,256]{1,0:T(8,128)(2,1)S(1)}, bf16[640,256]{1,0:T(8,128)(2,1)S(1)}, u32[]{:S(2)}, u32[]{:S(2)}) collective-permute-start(bf16[640,256]{1,0:T(8,128)(2,1)S(1)} %collective-permute-done.9.refs_2_), channel_id=1, source_target_pairs={{0,16},{1,17},{2,18},{3,19},{4,20},{5,21},{6,22},{7,23},{8,56},{9,... | collective-permute-start | bytes 983048 | tf_op jit(solution)/shard_map/ppermute | solution.py:45
  95.9 7.5 %collective-permute-start.11 = (bf16[640,256]{1,0:T(8,128)(2,1)S(1)}, bf16[640,256]{1,0:T(8,128)(2,1)S(1)}, u32[]{:S(2)}, u32[]{:S(2)}) collective-permute-start(bf16[640,256]{1,0:T(8,128)(2,1)S(1)} %collective-permute-done.9.refs_2_), channel_id=1, source_target_pairs={{0,8},{1,9},{2,10},{3,11},{4,12},{5,13},{6,14},{7,15},{8,0},{9,1},... | collective-permute-start | bytes 983048 | tf_op jit(solution)/shard_map/ppermute | solution.py:45
  96.0 7.4 %collective-permute-start.12 = (bf16[640,256]{1,0:T(8,128)(2,1)S(1)}, bf16[640,256]{1,0:T(8,128)(2,1)S(1)}, u32[]{:S(2)}, u32[]{:S(2)}) collective-permute-start(bf16[640,256]{1,0:T(8,128)(2,1)S(1)} %collective-permute-done.10.refs_3_), channel_id=1, source_target_pairs={{0,8},{1,9},{2,10},{3,11},{4,12},{5,13},{6,14},{7,15},{8,0},{9,1},... | collective-permute-start | bytes 983048 | tf_op jit(solution)/shard_map/ppermute | solution.py:45
  (17 other events, 168.5 us)
Sparse Core Ops, SparseCore 0:
  27.7 46.9 all-gather.2

commit v4 on v3

--- a/solution.py
+++ b/solution.py
@@ -53,50 +53,66 @@
     return lax.optimization_barrier((value, *earlier))[0]
 
 
-def weigh(panel_ref, weights_ref, out_ref):
-    half = panel_ref.shape[-1] // 2
+def weigh(own_ref, other_ref, weights_ref, out_ref):
+    half = own_ref.shape[-1] // 2
     k = pl.program_id(0)
-    side = rem(lax.div(lax.axis_index("col"), jnp.int32(Y)) + k, ZL)
-    weights = weights_ref[side * Y + lax.div(k, jnp.int32(ZL))]
-    panel = panel_ref[...].astype(jnp.float32)
-    out_ref[:, :half] = (panel[:, half:] * weights).astype(jnp.bfloat16)
-    out_ref[:, half:] = (panel[:, :half] * weights).astype(jnp.bfloat16)
-
-
-def left_panel_of(gathered, weights):
-    parts, height, width = gathered.shape
+    away, y = lax.div(k, jnp.int32(Y)), rem(k, Y)
+    side = rem(lax.div(lax.axis_index("col"), jnp.int32(Y)) + away, ZL)
+    weights = weights_ref[side * Y + y]
+
+    def put(panel_ref):
+        panel = panel_ref[...].astype(jnp.float32)
+        out_ref[:, :half] = (panel[:, half:] * weights).astype(jnp.bfloat16)
+        out_ref[:, half:] = (panel[:, :half] * weights).astype(jnp.bfloat16)
+
+    pl.when(away == 0)(lambda: put(own_ref))
+    pl.when(away == 1)(lambda: put(other_ref))
+
+
+def left_panel_of(own, others, weights):
+    side, height, width = own.shape
+    parts = ZL * side
     return pl.pallas_call(
         weigh,
         grid=(parts,),
         in_specs=[
-            pl.BlockSpec((None, height, width), lambda k: (k, 0, 0)),
+            pl.BlockSpec((None, height, width), lambda k: (jnp.minimum(k, side - 1), 0, 0)),
+            pl.BlockSpec((None, height, width), lambda k: (jnp.maximum(k - side, 0), 0, 0)),
             pl.BlockSpec((parts, 1, width // 2), lambda k: (0, 0, 0)),
         ],
         out_specs=pl.BlockSpec((None, height, width), lambda k: (k, 0, 0)),
         out_shape=jax.ShapeDtypeStruct((parts, height, width), jnp.bfloat16),
         compiler_params=pltpu.CompilerParams(vmem_limit_bytes=8 * 2**20),
-        cost_estimate=pl.CostEstimate(
-            flops=parts * height * width, bytes_accessed=4 * parts * height * width, transcendentals=0
-        ),
+        cost_estimate=pl.CostEstimate(flops=height, bytes_accessed=height * width, transcendentals=0),
         name="weigh_left",
-    )(gathered, weights.reshape(parts, 1, width // 2))
+    )(own, others, weights.reshape(parts, 1, width // 2))
 
 
 def rem(value, length):
     return lax.rem(value, jnp.int32(length))
 
 
-def join(left_ref, right_ref, out_ref):
+def join(left_ref, right_ref, out_ref, sems):
     half = left_ref.shape[-1]
-    out_ref[:, :half] = left_ref[...]
-    out_ref[:, half:] = right_ref[...]
+    copies = [
+        pltpu.make_async_copy(left_ref, out_ref.at[:, pl.ds(0, half)], sems.at[0]),
+        pltpu.make_async_copy(right_ref, out_ref.at[:, pl.ds(half, half)], sems.at[1]),
+    ]
+    for copy in copies:
+        copy.start()
+    for copy in copies:
+        copy.wait()
 
 
 def side_by_side(first, second):
     height, width = first.shape
+    anywhere = pl.BlockSpec(memory_space=pl.ANY)
     return pl.pallas_call(
         join,
+        in_specs=[anywhere, anywhere],
+        out_specs=anywhere,
         out_shape=jax.ShapeDtypeStruct((height, 2 * width), first.dtype),
+        scratch_shapes=[pltpu.SemaphoreType.DMA((2,))],
         compiler_params=pltpu.CompilerParams(vmem_limit_bytes=4 * 2**20),
         name="join_shard",
     )(first, second)
@@ -116,7 +132,7 @@
     left, right = [], []
     for array, skip, dx, other_core in places:
         zl, y = rem(core + other_core, CORE), rem(x + dx[0] + dx[1] * way + 2 * X - 2 * high, X)
-        left.append(left_ref[y * ZL + rem(zl + lax.div(col, jnp.int32(Y)), ZL)])
+        left.append(left_ref[rem(zl + lax.div(col, jnp.int32(Y)), ZL) * Y + y])
         right.append(arrays[array][skip * height : (skip + 1) * height, :])
     commutator = lax.dot_general(
         jnp.concatenate(left, 1),
@@ -175,26 +191,27 @@
 def per_device(eta_ladder, gamma_ladder, occupation, gamma):
     weights = 1.0 - 0.5 * occupation.astype(jnp.float32)
     shard = side_by_side(gamma_ladder, eta_ladder)
-    height, width = shard.shape
+    height = shard.shape[0]
+    alike_y = [[zl * Y + y for y in range(Y)] for zl in range(ZL)]
+    own = lax.all_gather(shard, "col", axis_index_groups=alike_y)
     other_zl = send(shard, OTHER_ZL)
 
     p = send(shard, TO_HOME)
     ps = other(p)
-    sides = jnp.stack([shard, after(other_zl, ps)])
-    alike_y = [[zl * Y + y for y in range(Y)] for zl in range(ZL)]
-    gathered = lax.all_gather(sides, "col", axis_index_groups=alike_y).reshape(ZL * Y, height, width)
     xp, xps = send(p, ALONG_X), send(ps, ALONG_X)
+    others = lax.all_gather(after(other_zl, own, xps), "col", axis_index_groups=alike_y)
     zz = send(jnp.concatenate([p, ps], 0), ALONG_Z)
     fxp = send(xp, ALONG_X)
     zz = after(zz, xps, fxp)
     zs = other(zz)
     z2 = send(zz[:height], ALONG_Z)
+    xzz, xzs = send(zz, ALONG_X), send(zs, ALONG_X)
+    z2 = after(z2, xzz)
     z2s = other(z2)
-    xzz, xzs = send(zz, ALONG_X), send(zs, ALONG_X)
     fxzz = send(xzz, ALONG_X)
     xz2, xz2s = send(z2, ALONG_X), send(z2s, ALONG_X)
 
-    left = left_panel_of(after(gathered, z2s), weights)
+    left = left_panel_of(own, after(others, z2s), weights)
 
     def both(arrays, first_core):
         return [

time: 115 us -> 119 us (1.035); the launches traced: 115 us -> 117 us
  waiting for transfers between devices: 27 us -> 29.8 us
  starting transfers between devices: 48.3 us -> 50.8 us
  other arithmetic: 1.99 us -> 0.05 us
    ppermute x25, waiting for transfers between devices: 27 us -> 29.8 us  [send(): return lax.ppermute(value, AXES, way)]
    ppermute x25, starting transfers between devices: 48.3 us -> 50.7 us  [send(): return lax.ppermute(value, AXES, way)]
    pallas_call x4, Pallas kernels: 17.7 us -> 16.1 us  [block_step(): pl.pallas_call(functools.partial(block_kernel, dz, places, len(arrays), h...]
  transfers between devices with their start and end apart: 26 -> 27, of which waited for: 10 -> 7; matrix products, arithmetic and copies ran while one was open for 1% -> 0% of each run, Pallas kernels for 13% -> 12%
where the time goes in v4:
time: 119 us; the launch traced here: 117 us
  starting transfers between devices  50.8 us (43%)
  waiting for transfers between devices  29.8 us (25%)
  Pallas kernels  17.7 us (15%)
  between operations  13.6 us (11%)
  local copies, waits for them, and re-layouts  5.32 us (4%)
    ppermute x25, starting transfers between devices, send(): return lax.ppermute(value, AXES, way)  50.7 us
    ppermute x25, waiting for transfers between devices, send(): return lax.ppermute(value, AXES, way)  29.8 us
    pallas_call x4, Pallas kernels, block_step(): pl.pallas_call(functools.partial(block_kernel, dz, places, len(arrays), h...  16.1 us
    unnamed x30, local copies, waits for them, and re-layouts  5.3 us
  transfers between devices with their start and end apart: 27, of which 7 were waited for; matrix products, arithmetic and copies ran while one was open for 0% of the time, Pallas kernels for 12%

profile of v4, /device:TPU:25, one launch (start us, length us, event | category | flops | bytes accessed | tf_op | source)
XLA Modules:
  0.0 117.3 jit_solution(16425083173163264765)
XLA Ops:
  9.2 10.0 %collective-permute-start.1 = (bf16[640,256]{1,0:T(8,128)(2,1)}, bf16[640,256]{1,0:T(8,128)(2,1)S(1)}, u32[]{:S(2)}, u32[]{:S(2)}) collective-permute-start(bf16[640,256]{1,0:T(8,128)(2,1)} %join_shard.1), channel_id=1, source_target_pairs={{0,0},{1,16},{2,32},{3,48},{4,8},{5,24},{6,40},{7,56},{8,160},{9,1... | collective-permute-start | bytes 983048 | tf_op jit(solution)/shard_map/ppermute | solution.py:45
  19.2 4.4 %collective-permute-done.1.refs_0_ = bf16[640,256]{1,0:T(8,128)(2,1)S(1)} collective-permute-done((bf16[640,256]{1,0:T(8,128)(2,1)}, bf16[640,256]{1,0:T(8,128)(2,1)S(1)}, u32[]{:S(2)}, u32[]{:S(2)}) %collective-permute-start.1) | collective-permute-done | bytes 327712 | tf_op jit(solution)/shard_map/ppermute | solution.py:45
  23.6 2.4 %collective-permute-start.2 = (bf16[640,256]{1,0:T(8,128)(2,1)S(1)}, bf16[640,256]{1,0:T(8,128)(2,1)S(1)}, u32[]{:S(2)}, u32[]{:S(2)}) collective-permute-start(bf16[640,256]{1,0:T(8,128)(2,1)S(1)} %collective-permute-done.1.refs_0_), channel_id=1, source_target_pairs={{0,8},{1,9},{2,10},{3,11},{4,12},{5,13},{6,14},{7,15},{8,0},{9,1},... | collective-permute-start | bytes 983048 | tf_op jit(solution)/shard_map/ppermute | solution.py:45
  26.0 5.9 %collective-permute-start = (bf16[640,256]{1,0:T(8,128)(2,1)}, bf16[640,256]{1,0:T(8,128)(2,1)S(1)}, u32[]{:S(2)}, u32[]{:S(2)}) collective-permute-start(bf16[640,256]{1,0:T(8,128)(2,1)} %join_shard.1), channel_id=1, source_target_pairs={{0,4},{1,5},{2,6},{3,7},{4,0},{5,1},{6,2},{7,3},{8,12},{9,13},{10,... | collective-permute-start | bytes 983048 | tf_op jit(solution)/shard_map/ppermute | solution.py:45
  31.9 3.8 %collective-permute-start.3 = (bf16[640,256]{1,0:T(8,128)(2,1)S(1)}, bf16[640,256]{1,0:T(8,128)(2,1)S(1)}, u32[]{:S(2)}, u32[]{:S(2)}) collective-permute-start(bf16[640,256]{1,0:T(8,128)(2,1)S(1)} %collective-permute-done.2.refs_1_), channel_id=1, source_target_pairs={{0,16},{1,17},{2,18},{3,19},{4,20},{5,21},{6,22},{7,23},{8,56},{9,... | collective-permute-start | bytes 983048 | tf_op jit(solution)/shard_map/ppermute | solution.py:45
  35.7 8.6 %collective-permute-start.4 = (bf16[1280,256]{1,0:T(8,128)(2,1)S(1)}, bf16[1280,256]{1,0:T(8,128)(2,1)S(1)}, u32[]{:S(2)}, u32[]{:S(2)}) collective-permute-start(bf16[1280,256]{1,0:T(8,128)(2,1)S(1)} %pad_maximum_fusion), channel_id=1, source_target_pairs={{0,64},{1,65},{2,66},{3,67},{4,68},{5,69},{6,70},{7,71},{8,200},{9... | collective-permute-start | bytes 1966088 | tf_op jit(solution)/shard_map/ppermute | solution.py:45
  45.2 7.7 %collective-permute-done.6.refs_6_ = bf16[640,256]{1,0:T(8,128)(2,1)} collective-permute-done((bf16[640,256]{1,0:T(8,128)(2,1)S(1)}, bf16[640,256]{1,0:T(8,128)(2,1)}, u32[]{:S(2)}, u32[]{:S(2)}) %collective-permute-start.6) | collective-permute-done | bytes 327712 | tf_op jit(solution)/shard_map/ppermute | solution.py:45
  53.0 5.9 %collective-permute-done.4.refs_0_ = bf16[1280,256]{1,0:T(8,128)(2,1)S(1)} collective-permute-done((bf16[1280,256]{1,0:T(8,128)(2,1)S(1)}, bf16[1280,256]{1,0:T(8,128)(2,1)S(1)}, u32[]{:S(2)}, u32[]{:S(2)}) %collective-permute-start.4) | collective-permute-done | bytes 655392 | tf_op jit(solution)/shard_map/ppermute | solution.py:45
  58.9 4.2 %collective-permute-start.14 = (bf16[1280,256]{1,0:T(8,128)(2,1)S(1)}, bf16[1280,256]{1,0:T(8,128)(2,1)S(1)}, u32[]{:S(2)}, u32[]{:S(2)}) collective-permute-start(bf16[1280,256]{1,0:T(8,128)(2,1)S(1)} %collective-permute-done.4.refs_0_), channel_id=1, source_target_pairs={{0,8},{1,9},{2,10},{3,11},{4,12},{5,13},{6,14},{7,15},{8,0},{9,1},... | collective-permute-start | bytes 1966088 | tf_op jit(solution)/shard_map/ppermute | solution.py:45
  63.1 2.4 %collective-permute-start.8 = (bf16[1280,256]{1,0:T(8,128)(2,1)S(1)}, bf16[1280,256]{1,0:T(8,128)(2,1)S(1)}, u32[]{:S(2)}, u32[]{:S(2)}) collective-permute-start(bf16[1280,256]{1,0:T(8,128)(2,1)S(1)} %collective-permute-done.4.refs_0_), channel_id=1, source_target_pairs={{0,16},{1,17},{2,18},{3,19},{4,20},{5,21},{6,22},{7,23},{8,56},{9,... | collective-permute-start | bytes 1966088 | tf_op jit(solution)/shard_map/ppermute | solution.py:45
  65.6 1.6 %collective-permute-start.15 = (bf16[1280,256]{1,0:T(8,128)(2,1)S(1)}, bf16[1280,256]{1,0:T(8,128)(2,1)S(1)}, u32[]{:S(2)}, u32[]{:S(2)}) collective-permute-start(bf16[1280,256]{1,0:T(8,128)(2,1)S(1)} %collective-permute-done.14.refs_0_), channel_id=1, source_target_pairs={{0,16},{1,17},{2,18},{3,19},{4,20},{5,21},{6,22},{7,23},{8,56},{9,... | collective-permute-start | bytes 1966088 | tf_op jit(solution)/shard_map/ppermute | solution.py:45
  67.2 6.9 %collective-permute-done.7.refs_0_ = bf16[640,256]{1,0:T(8,128)(2,1)S(1)} collective-permute-done((bf16[640,256]{1,0:T(8,128)(2,1)S(1)}, bf16[640,256]{1,0:T(8,128)(2,1)S(1)}, u32[]{:S(2)}, u32[]{:S(2)}) %collective-permute-start.7) | collective-permute-done | bytes 327712 | tf_op jit(solution)/shard_map/ppermute | solution.py:45
  74.9 1.6 %collective-permute-start.17 = (bf16[1280,256]{1,0:T(8,128)(2,1)S(1)}, bf16[1280,256]{1,0:T(8,128)(2,1)}, u32[]{:S(2)}, u32[]{:S(2)}) collective-permute-start(bf16[1280,256]{1,0:T(8,128)(2,1)S(1)} %collective-permute-done.8.refs_1_), channel_id=1, source_target_pairs={{0,16},{1,17},{2,18},{3,19},{4,20},{5,21},{6,22},{7,23},{8,56},{9,... | collective-permute-start | bytes 1966088 | tf_op jit(solution)/shard_map/ppermute | solution.py:45
  77.2 2.9 %collective-permute-done.15.refs_1_ = bf16[1280,256]{1,0:T(8,128)(2,1)S(1)} collective-permute-done((bf16[1280,256]{1,0:T(8,128)(2,1)S(1)}, bf16[1280,256]{1,0:T(8,128)(2,1)S(1)}, u32[]{:S(2)}, u32[]{:S(2)}) %collective-permute-start.15) | collective-permute-done | bytes 655392 | tf_op jit(solution)/shard_map/ppermute | solution.py:45
  80.1 1.9 %collective-permute-start.16 = (bf16[1280,256]{1,0:T(8,128)(2,1)S(1)}, bf16[1280,256]{1,0:T(8,128)(2,1)}, u32[]{:S(2)}, u32[]{:S(2)}) collective-permute-start(bf16[1280,256]{1,0:T(8,128)(2,1)S(1)} %collective-permute-done.15.refs_1_), channel_id=1, source_target_pairs={{0,8},{1,9},{2,10},{3,11},{4,12},{5,13},{6,14},{7,15},{8,0},{9,1},... | collective-permute-start | bytes 1966088 | tf_op jit(solution)/shard_map/ppermute | solution.py:45
  82.0 1.3 %copy-done.1 = bf16[2560,256]{1,0:T(8,128)(2,1)S(1)} copy-done((bf16[2560,256]{1,0:T(8,128)(2,1)S(1)}, bf16[2560,256]{1,0:T(8,128)(2,1)}, u32[]{:S(2)}) %copy-start.1) | copy-done | bytes 1310744
  83.3 1.3 %copy-done.2 = bf16[2560,256]{1,0:T(8,128)(2,1)S(1)} copy-done((bf16[2560,256]{1,0:T(8,128)(2,1)S(1)}, bf16[2560,256]{1,0:T(8,128)(2,1)}, u32[]{:S(2)}) %copy-start.2) | copy-done | bytes 1310744
  86.9 4.7 %block_step.4.refs_5_ = bf16[640,2560]{1,0:T(8,128)(2,1)} custom-call(bf16[8,640,256]{2,1,0:T(8,128)(2,1)S(1)} %weigh_left.1.left_ref, bf16[640,256]{1,0:T(8,128)(2,1)S(1)} %collective-permute-done.1.refs_0_, bf16[640,256]{1,0:T(8,128)(2,1)S(1)} %collective-permute-done.2.refs_1_, bf16[640,256]{1,0:T(8,128)(2,1)S(1)} %copy-done.4, ...), custom_call_target="tpu_custom_call" | custom-call | flops 409600 | bytes 409600 | tf_op jit(solution)/shard_map/block_step/pallas_call | solution.py:166
  92.2 1.3 %collective-permute-start.11 = (bf16[640,256]{1,0:T(8,128)(2,1)S(1)}, bf16[640,256]{1,0:T(8,128)(2,1)S(1)}, u32[]{:S(2)}, u32[]{:S(2)}) collective-permute-start(bf16[640,256]{1,0:T(8,128)(2,1)S(1)} %copy-done.10), channel_id=1, source_target_pairs={{0,16},{1,17},{2,18},{3,19},{4,20},{5,21},{6,22},{7,23},{8,56},{9,... | collective-permute-start | bytes 983048 | tf_op jit(solution)/shard_map/ppermute | solution.py:45
  93.5 4.7 %block_step.5.refs_5_ = bf16[640,2560]{1,0:T(8,128)(2,1)} custom-call(bf16[8,640,256]{2,1,0:T(8,128)(2,1)S(1)} %weigh_left.1.left_ref, bf16[1280,256]{1,0:T(8,128)(2,1)S(1)} %collective-permute-done.4.refs_0_, bf16[1280,256]{1,0:T(8,128)(2,1)S(1)} %collective-permute-done.8.refs_1_, ...), custom_call_target="tpu_custom_call", output_to_operand_aliasing={{}: (6, {})} | custom-call | flops 409600 | bytes 409600 | tf_op jit(solution)/shard_map/block_step/pallas_call | solution.py:166
  99.1 1.4 %collective-permute-start.13 = (bf16[640,256]{1,0:T(8,128)(2,1)S(1)}, bf16[640,256]{1,0:T(8,128)(2,1)S(1)}, u32[]{:S(2)}, u32[]{:S(2)}) collective-permute-start(bf16[640,256]{1,0:T(8,128)(2,1)S(1)} %collective-permute-done.11.refs_3_), channel_id=1, source_target_pairs={{0,8},{1,9},{2,10},{3,11},{4,12},{5,13},{6,14},{7,15},{8,0},{9,1},... | collective-permute-start | bytes 983048 | tf_op jit(solution)/shard_map/ppermute | solution.py:45
  100.6 3.4 %block_step.6.refs_9_ = bf16[640,2560]{1,0:T(8,128)(2,1)} custom-call(bf16[8,640,256]{2,1,0:T(8,128)(2,1)S(1)} %weigh_left.1.left_ref, bf16[1280,256]{1,0:T(8,128)(2,1)S(1)} %collective-permute-done.14.refs_0_, bf16[1280,256]{1,0:T(8,128)(2,1)S(1)} %collective-permute-done.15.refs_1_, ...), custom_call_target="tpu_custom_call", output_to_operand_aliasing={{}: (6, {})} | custom-call | flops 409600 | bytes 409600 | tf_op jit(solution)/shard_map/block_step/pallas_call | solution.py:166
  104.5 1.3 %collective-permute-start.24 = (bf16[640,256]{1,0:T(8,128)(2,1)S(1)}, bf16[640,256]{1,0:T(8,128)(2,1)S(1)}, u32[]{:S(2)}, u32[]{:S(2)}) collective-permute-start(bf16[640,256]{1,0:T(8,128)(2,1)S(1)} %collective-permute-done.21.refs_6_), channel_id=1, source_target_pairs={{0,8},{1,9},{2,10},{3,11},{4,12},{5,13},{6,14},{7,15},{8,0},{9,1},... | collective-permute-start | bytes 983048 | tf_op jit(solution)/shard_map/ppermute | solution.py:45
  107.0 3.4 %block_step.7 = bf16[640,2560]{1,0:T(8,128)(2,1)} custom-call(bf16[8,640,256]{2,1,0:T(8,128)(2,1)S(1)} %weigh_left.1.left_ref, bf16[640,256]{1,0:T(8,128)(2,1)S(1)} %copy-done.8, bf16[640,256]{1,0:T(8,128)(2,1)S(1)} %copy-done.10, bf16[640,256]{1,0:T(8,128)(2,1)S(1)} %collective-permute-done.10.refs_2_, ...), custom_call_target="tpu_custom_call", output_to_operand_aliasing={{}: (10, {})} | custom-call | flops 409600 | bytes 409600 | tf_op jit(solution)/shard_map/block_step/pallas_call | solution.py:166
  (71 shorter events, 10.5 us)
Async XLA Ops:
  6.5 37.8 %all-gather.5.cloned.1.call-start = ((), (), s32[]{:S(2)}) async-start(), calls=%async_computation | async-start | bytes 1638400 | tf_op jit(solution)/shard_map/all_gather | solution.py:196
  9.1 72.8 %all-gather.7.cloned.1.call-start = ((), (), s32[]{:S(2)}) async-start(), calls=%async_computation.1 | async-start | bytes 1638400 | tf_op jit(solution)/shard_map/all_gather | solution.py:202
  9.2 14.4 %collective-permute-start.1 = (bf16[640,256]{1,0:T(8,128)(2,1)}, bf16[640,256]{1,0:T(8,128)(2,1)S(1)}, u32[]{:S(2)}, u32[]{:S(2)}) collective-permute-start(bf16[640,256]{1,0:T(8,128)(2,1)} %join_shard.1), channel_id=1, source_target_pairs={{0,0},{1,16},{2,32},{3,48},{4,8},{5,24},{6,40},{7,56},{8,160},{9,1... | collective-permute-start | bytes 983048 | tf_op jit(solution)/shard_map/ppermute | solution.py:45
  23.6 8.3 %collective-permute-start.2 = (bf16[640,256]{1,0:T(8,128)(2,1)S(1)}, bf16[640,256]{1,0:T(8,128)(2,1)S(1)}, u32[]{:S(2)}, u32[]{:S(2)}) collective-permute-start(bf16[640,256]{1,0:T(8,128)(2,1)S(1)} %collective-permute-done.1.refs_0_), channel_id=1, source_target_pairs={{0,8},{1,9},{2,10},{3,11},{4,12},{5,13},{6,14},{7,15},{8,0},{9,1},... | collective-permute-start | bytes 983048 | tf_op jit(solution)/shard_map/ppermute | solution.py:45
  26.0 18.4 %collective-permute-start = (bf16[640,256]{1,0:T(8,128)(2,1)}, bf16[640,256]{1,0:T(8,128)(2,1)S(1)}, u32[]{:S(2)}, u32[]{:S(2)}) collective-permute-start(bf16[640,256]{1,0:T(8,128)(2,1)} %join_shard.1), channel_id=1, source_target_pairs={{0,4},{1,5},{2,6},{3,7},{4,0},{5,1},{6,2},{7,3},{8,12},{9,13},{10,... | collective-permute-start | bytes 983048 | tf_op jit(solution)/shard_map/ppermute | solution.py:45
  31.9 13.2 %collective-permute-start.5 = (bf16[640,256]{1,0:T(8,128)(2,1)S(1)}, bf16[640,256]{1,0:T(8,128)(2,1)S(1)}, u32[]{:S(2)}, u32[]{:S(2)}) collective-permute-start(bf16[640,256]{1,0:T(8,128)(2,1)S(1)} %collective-permute-done.1.refs_0_), channel_id=1, source_target_pairs={{0,16},{1,17},{2,18},{3,19},{4,20},{5,21},{6,22},{7,23},{8,56},{9,... | collective-permute-start | bytes 983048 | tf_op jit(solution)/shard_map/ppermute | solution.py:45
  31.9 12.4 %collective-permute-start.3 = (bf16[640,256]{1,0:T(8,128)(2,1)S(1)}, bf16[640,256]{1,0:T(8,128)(2,1)S(1)}, u32[]{:S(2)}, u32[]{:S(2)}) collective-permute-start(bf16[640,256]{1,0:T(8,128)(2,1)S(1)} %collective-permute-done.2.refs_1_), channel_id=1, source_target_pairs={{0,16},{1,17},{2,18},{3,19},{4,20},{5,21},{6,22},{7,23},{8,56},{9,... | collective-permute-start | bytes 983048 | tf_op jit(solution)/shard_map/ppermute | solution.py:45
  35.7 23.2 %collective-permute-start.4 = (bf16[1280,256]{1,0:T(8,128)(2,1)S(1)}, bf16[1280,256]{1,0:T(8,128)(2,1)S(1)}, u32[]{:S(2)}, u32[]{:S(2)}) collective-permute-start(bf16[1280,256]{1,0:T(8,128)(2,1)S(1)} %pad_maximum_fusion), channel_id=1, source_target_pairs={{0,64},{1,65},{2,66},{3,67},{4,68},{5,69},{6,70},{7,71},{8,200},{9... | collective-permute-start | bytes 1966088 | tf_op jit(solution)/shard_map/ppermute | solution.py:45
  45.1 7.8 %collective-permute-start.6 = (bf16[640,256]{1,0:T(8,128)(2,1)S(1)}, bf16[640,256]{1,0:T(8,128)(2,1)}, u32[]{:S(2)}, u32[]{:S(2)}) collective-permute-start(bf16[640,256]{1,0:T(8,128)(2,1)S(1)} %collective-permute-done.5.refs_2_), channel_id=1, source_target_pairs={{0,16},{1,17},{2,18},{3,19},{4,20},{5,21},{6,22},{7,23},{8,56},{9,... | collective-permute-start | bytes 983048 | tf_op jit(solution)/shard_map/ppermute | solution.py:45
  58.9 6.7 %collective-permute-start.14 = (bf16[1280,256]{1,0:T(8,128)(2,1)S(1)}, bf16[1280,256]{1,0:T(8,128)(2,1)S(1)}, u32[]{:S(2)}, u32[]{:S(2)}) collective-permute-start(bf16[1280,256]{1,0:T(8,128)(2,1)S(1)} %collective-permute-done.4.refs_0_), channel_id=1, source_target_pairs={{0,8},{1,9},{2,10},{3,11},{4,12},{5,13},{6,14},{7,15},{8,0},{9,1},... | collective-permute-start | bytes 1966088 | tf_op jit(solution)/shard_map/ppermute | solution.py:45
  63.1 11.1 %collective-permute-start.8 = (bf16[1280,256]{1,0:T(8,128)(2,1)S(1)}, bf16[1280,256]{1,0:T(8,128)(2,1)S(1)}, u32[]{:S(2)}, u32[]{:S(2)}) collective-permute-start(bf16[1280,256]{1,0:T(8,128)(2,1)S(1)} %collective-permute-done.4.refs_0_), channel_id=1, source_target_pairs={{0,16},{1,17},{2,18},{3,19},{4,20},{5,21},{6,22},{7,23},{8,56},{9,... | collective-permute-start | bytes 1966088 | tf_op jit(solution)/shard_map/ppermute | solution.py:45
  65.5 8.6 %collective-permute-start.7 = (bf16[640,256]{1,0:T(8,128)(2,1)S(1)}, bf16[640,256]{1,0:T(8,128)(2,1)S(1)}, u32[]{:S(2)}, u32[]{:S(2)}) collective-permute-start(bf16[640,256]{1,0:T(8,128)(2,1)S(1)} %slice.3), channel_id=1, source_target_pairs={{0,64},{1,65},{2,66},{3,67},{4,68},{5,69},{6,70},{7,71},{8,200},{9... | collective-permute-start | bytes 983048 | tf_op jit(solution)/shard_map/ppermute | solution.py:45
  65.6 14.4 %collective-permute-start.15 = (bf16[1280,256]{1,0:T(8,128)(2,1)S(1)}, bf16[1280,256]{1,0:T(8,128)(2,1)S(1)}, u32[]{:S(2)}, u32[]{:S(2)}) collective-permute-start(bf16[1280,256]{1,0:T(8,128)(2,1)S(1)} %collective-permute-done.14.refs_0_), channel_id=1, source_target_pairs={{0,16},{1,17},{2,18},{3,19},{4,20},{5,21},{6,22},{7,23},{8,56},{9,... | collective-permute-start | bytes 1966088 | tf_op jit(solution)/shard_map/ppermute | solution.py:45
  74.9 16.7 %collective-permute-start.17 = (bf16[1280,256]{1,0:T(8,128)(2,1)S(1)}, bf16[1280,256]{1,0:T(8,128)(2,1)}, u32[]{:S(2)}, u32[]{:S(2)}) collective-permute-start(bf16[1280,256]{1,0:T(8,128)(2,1)S(1)} %collective-permute-done.8.refs_1_), channel_id=1, source_target_pairs={{0,16},{1,17},{2,18},{3,19},{4,20},{5,21},{6,22},{7,23},{8,56},{9,... | collective-permute-start | bytes 1966088 | tf_op jit(solution)/shard_map/ppermute | solution.py:45
  76.6 8.9 %collective-permute-start.18 = (bf16[640,256]{1,0:T(8,128)(2,1)}, bf16[640,256]{1,0:T(8,128)(2,1)}, u32[]{:S(2)}, u32[]{:S(2)}) collective-permute-start(bf16[640,256]{1,0:T(8,128)(2,1)} %copy-done.3), channel_id=1, source_target_pairs={{0,8},{1,9},{2,10},{3,11},{4,12},{5,13},{6,14},{7,15},{8,0},{9,1},... | collective-permute-start | bytes 983048 | tf_op jit(solution)/shard_map/ppermute | solution.py:45
  76.6 10.3 %collective-permute-start.19 = (bf16[640,256]{1,0:T(8,128)(2,1)}, bf16[640,256]{1,0:T(8,128)(2,1)}, u32[]{:S(2)}, u32[]{:S(2)}) collective-permute-start(bf16[640,256]{1,0:T(8,128)(2,1)} %copy-done.5), channel_id=1, source_target_pairs={{0,8},{1,9},{2,10},{3,11},{4,12},{5,13},{6,14},{7,15},{8,0},{9,1},... | collective-permute-start | bytes 983048 | tf_op jit(solution)/shard_map/ppermute | solution.py:45
  77.1 9.8 %collective-permute-start.20 = (bf16[640,256]{1,0:T(8,128)(2,1)}, bf16[640,256]{1,0:T(8,128)(2,1)}, u32[]{:S(2)}, u32[]{:S(2)}) collective-permute-start(bf16[640,256]{1,0:T(8,128)(2,1)} %collective-permute-done.6.refs_6_), channel_id=1, source_target_pairs={{0,8},{1,9},{2,10},{3,11},{4,12},{5,13},{6,14},{7,15},{8,0},{9,1},... | collective-permute-start | bytes 983048 | tf_op jit(solution)/shard_map/ppermute | solution.py:45
  80.1 13.4 %collective-permute-start.16 = (bf16[1280,256]{1,0:T(8,128)(2,1)S(1)}, bf16[1280,256]{1,0:T(8,128)(2,1)}, u32[]{:S(2)}, u32[]{:S(2)}) collective-permute-start(bf16[1280,256]{1,0:T(8,128)(2,1)S(1)} %collective-permute-done.15.refs_1_), channel_id=1, source_target_pairs={{0,8},{1,9},{2,10},{3,11},{4,12},{5,13},{6,14},{7,15},{8,0},{9,1},... | collective-permute-start | bytes 1966088 | tf_op jit(solution)/shard_map/ppermute | solution.py:45
  85.6 12.6 %collective-permute-start.10 = (bf16[640,256]{1,0:T(8,128)(2,1)S(1)}, bf16[640,256]{1,0:T(8,128)(2,1)S(1)}, u32[]{:S(2)}, u32[]{:S(2)}) collective-permute-start(bf16[640,256]{1,0:T(8,128)(2,1)S(1)} %copy-done.8), channel_id=1, source_target_pairs={{0,16},{1,17},{2,18},{3,19},{4,20},{5,21},{6,22},{7,23},{8,56},{9,... | collective-permute-start | bytes 983048 | tf_op jit(solution)/shard_map/ppermute | solution.py:45
  86.9 13.7 %collective-permute-start.22 = (bf16[1280,256]{1,0:T(8,128)(2,1)S(1)}, bf16[1280,256]{1,0:T(8,128)(2,1)S(1)}, u32[]{:S(2)}, u32[]{:S(2)}) collective-permute-start(bf16[1280,256]{1,0:T(8,128)(2,1)S(1)} %collective-permute-done.8.refs_1_), channel_id=1, source_target_pairs={{0,8},{1,9},{2,10},{3,11},{4,12},{5,13},{6,14},{7,15},{8,0},{9,1},... | collective-permute-start | bytes 1966088 | tf_op jit(solution)/shard_map/ppermute | solution.py:45
  91.6 9.0 %collective-permute-start.23 = (bf16[1280,256]{1,0:T(8,128)(2,1)}, bf16[1280,256]{1,0:T(8,128)(2,1)S(1)}, u32[]{:S(2)}, u32[]{:S(2)}) collective-permute-start(bf16[1280,256]{1,0:T(8,128)(2,1)} %collective-permute-done.17.refs_3_), channel_id=1, source_target_pairs={{0,8},{1,9},{2,10},{3,11},{4,12},{5,13},{6,14},{7,15},{8,0},{9,1},... | collective-permute-start | bytes 1966088 | tf_op jit(solution)/shard_map/ppermute | solution.py:45
  92.2 6.9 %collective-permute-start.11 = (bf16[640,256]{1,0:T(8,128)(2,1)S(1)}, bf16[640,256]{1,0:T(8,128)(2,1)S(1)}, u32[]{:S(2)}, u32[]{:S(2)}) collective-permute-start(bf16[640,256]{1,0:T(8,128)(2,1)S(1)} %copy-done.10), channel_id=1, source_target_pairs={{0,16},{1,17},{2,18},{3,19},{4,20},{5,21},{6,22},{7,23},{8,56},{9,... | collective-permute-start | bytes 983048 | tf_op jit(solution)/shard_map/ppermute | solution.py:45
  98.7 7.0 %collective-permute-start.12 = (bf16[640,256]{1,0:T(8,128)(2,1)S(1)}, bf16[640,256]{1,0:T(8,128)(2,1)S(1)}, u32[]{:S(2)}, u32[]{:S(2)}) collective-permute-start(bf16[640,256]{1,0:T(8,128)(2,1)S(1)} %collective-permute-done.10.refs_2_), channel_id=1, source_target_pairs={{0,8},{1,9},{2,10},{3,11},{4,12},{5,13},{6,14},{7,15},{8,0},{9,1},... | collective-permute-start | bytes 983048 | tf_op jit(solution)/shard_map/ppermute | solution.py:45
  99.1 6.7 %collective-permute-start.13 = (bf16[640,256]{1,0:T(8,128)(2,1)S(1)}, bf16[640,256]{1,0:T(8,128)(2,1)S(1)}, u32[]{:S(2)}, u32[]{:S(2)}) collective-permute-start(bf16[640,256]{1,0:T(8,128)(2,1)S(1)} %collective-permute-done.11.refs_3_), channel_id=1, source_target_pairs={{0,8},{1,9},{2,10},{3,11},{4,12},{5,13},{6,14},{7,15},{8,0},{9,1},... | collective-permute-start | bytes 983048 | tf_op jit(solution)/shard_map/ppermute | solution.py:45
  (18 other events, 130.4 us)
Sparse Core Ops, SparseCore 0:
  9.3 28.8 all-gather.4
  45.2 32.3 all-gather.6

commit v5 on v4

--- a/solution.py
+++ b/solution.py
@@ -118,45 +118,66 @@
     )(first, second)
 
 
-def block_kernel(dz, places, operands, height, left_ref, *refs):
+def block_kernel(blocks, operands, height, left_ref, *refs):
     arrays, gamma_ref = refs[:operands], refs[operands]
     out_ref, old, new, sems = refs[-4:]
     row, col = lax.axis_index("row"), lax.axis_index("col")
     zh, x, core = lax.div(row, jnp.int32(X * CORE)), rem(lax.div(row, jnp.int32(CORE)), X), rem(row, CORE)
     way = 2 * core - 1
-    turn = rem(zh + dz[0] + dz[1] * way + 2 * ZH - lax.div(col, jnp.int32(2)), ZH)
-    low, high = rem(turn, 2), lax.div(turn, jnp.int32(2))
-    columns = pl.ds(pl.multiple_of((low * 2 + high) * height, 128), height)
-    come = pltpu.make_async_copy(gamma_ref.at[:, columns], old, sems.at[0])
-    come.start()
+
+    def turn_of(dz):
+        turn = rem(zh + dz[0] + dz[1] * way + 2 * ZH - lax.div(col, jnp.int32(2)), ZH)
+        return rem(turn, 2), lax.div(turn, jnp.int32(2))
+
+    columns, coming = [], []
+    for index, (dz, _) in enumerate(blocks):
+        low, high = turn_of(dz)
+        columns.append(pl.ds(pl.multiple_of((low * 2 + high) * height, 128), height))
+        here = old.at[:, pl.ds(index * height, height)]
+        coming.append(pltpu.make_async_copy(gamma_ref.at[:, columns[index]], here, sems.at[index]))
+        coming[index].start()
+    high = turn_of(blocks[0][0])[1]
     left, right = [], []
-    for array, skip, dx, other_core in places:
+    for place in range(len(blocks[0][1])):
+        _, _, dx, other_core = blocks[0][1][place]
         zl, y = rem(core + other_core, CORE), rem(x + dx[0] + dx[1] * way + 2 * X - 2 * high, X)
         left.append(left_ref[rem(zl + lax.div(col, jnp.int32(Y)), ZL) * Y + y])
-        right.append(arrays[array][skip * height : (skip + 1) * height, :])
-    commutator = lax.dot_general(
-        jnp.concatenate(left, 1),
-        jnp.concatenate(right, 1),
-        (((1,), (1,)), ((), ())),
-        preferred_element_type=jnp.float32,
-    )
-    come.wait()
-    new[...] = (old[...].astype(jnp.float32) + euler_step * commutator).astype(jnp.bfloat16)
-    go = pltpu.make_async_copy(new, out_ref.at[:, columns], sems.at[1])
-    go.start()
-    go.wait()
-
-
-def block_step(dz, pieces, left, gamma, out):
+        halves = [(arrays[pieces[place][0]], pieces[place][1]) for _, pieces in blocks]
+        right.append(jnp.concatenate([array[skip * height : (skip + 1) * height, :] for array, skip in halves], 0))
+    left, right = jnp.concatenate(left, 1), jnp.concatenate(right, 1)
+    total = len(blocks) * height
+    going = []
+    for first in range(0, total, 512):
+        last = min(first + 512, total)
+        commutator = lax.dot_general(
+            left, right[first:last], (((1,), (1,)), ((), ())), preferred_element_type=jnp.float32
+        )
+        if first == 0:
+            for copy in coming:
+                copy.wait()
+        new[:, first:last] = (old[:, first:last].astype(jnp.float32) + euler_step * commutator).astype(jnp.bfloat16)
+        while (len(going) + 1) * height <= last:
+            index = len(going)
+            there = out_ref.at[:, columns[index]]
+            going.append(pltpu.make_async_copy(new.at[:, pl.ds(index * height, height)], there, sems.at[len(blocks) + index]))
+            going[index].start()
+    for copy in going:
+        copy.wait()
+
+
+def block_step(blocks, left, gamma, out):
     arrays = []
-    places = []
-    for array, skip, dx, core in pieces:
-        known = [index for index, had in enumerate(arrays) if had is array]
-        if not known:
-            known = [len(arrays)]
-            arrays.append(array)
-        places.append((known[0], skip, dx, core))
-    height, count, width = left.shape[1], len(pieces), arrays[0].shape[-1]
+    placed = []
+    for dz, pieces in blocks:
+        places = []
+        for array, skip, dx, core in pieces:
+            known = [index for index, had in enumerate(arrays) if had is array]
+            if not known:
+                known = [len(arrays)]
+                arrays.append(array)
+            places.append((known[0], skip, dx, core))
+        placed.append((dz, places))
+    height, width = left.shape[1], left.shape[0] * left.shape[2]
     anywhere = pl.BlockSpec(memory_space=pl.ANY)
     operands = [left, *arrays, gamma]
     aliases = {}
@@ -164,7 +185,7 @@
         aliases = {len(operands): 0}
         operands.append(out)
     return pl.pallas_call(
-        functools.partial(block_kernel, dz, places, len(arrays), height),
+        functools.partial(block_kernel, placed, len(arrays), height),
         in_specs=[
             *[pl.BlockSpec(memory_space=pltpu.VMEM)] * (1 + len(arrays)),
             *[anywhere] * (len(operands) - 1 - len(arrays)),
@@ -173,14 +194,12 @@
         out_shape=jax.ShapeDtypeStruct(gamma.shape, gamma.dtype),
         input_output_aliases=aliases,
         scratch_shapes=[
-            pltpu.VMEM((height, height), jnp.bfloat16),
-            pltpu.VMEM((height, height), jnp.bfloat16),
-            pltpu.SemaphoreType.DMA((2,)),
+            pltpu.VMEM((height, len(blocks) * height), jnp.bfloat16),
+            pltpu.VMEM((height, len(blocks) * height), jnp.bfloat16),
+            pltpu.SemaphoreType.DMA((2 * len(blocks),)),
         ],
-        compiler_params=pltpu.CompilerParams(vmem_limit_bytes=20 * 2**20),
-        cost_estimate=pl.CostEstimate(
-            flops=height * height, bytes_accessed=height * height, transcendentals=0
-        ),
+        compiler_params=pltpu.CompilerParams(vmem_limit_bytes=28 * 2**20),
+        cost_estimate=pl.CostEstimate(flops=height * height, bytes_accessed=height * height, transcendentals=0),
         name="block_step",
     )(*operands)
 
@@ -194,51 +213,45 @@
     height = shard.shape[0]
     alike_y = [[zl * Y + y for y in range(Y)] for zl in range(ZL)]
     own = lax.all_gather(shard, "col", axis_index_groups=alike_y)
+
+    p = send(shard, TO_HOME)
     other_zl = send(shard, OTHER_ZL)
-
-    p = send(shard, TO_HOME)
-    ps = other(p)
-    xp, xps = send(p, ALONG_X), send(ps, ALONG_X)
-    others = lax.all_gather(after(other_zl, own, xps), "col", axis_index_groups=alike_y)
-    zz = send(jnp.concatenate([p, ps], 0), ALONG_Z)
-    fxp = send(xp, ALONG_X)
-    zz = after(zz, xps, fxp)
+    p = after(p, other_zl)
+    p = jnp.concatenate([p, other(p)], 0)
+    xp = send(p, ALONG_X)
+    others = lax.all_gather(after(other_zl, own, xp), "col", axis_index_groups=alike_y)
+    fxp = send(xp[:height], ALONG_X)
+    zz = after(send(p, ALONG_Z), fxp)
     zs = other(zz)
     z2 = send(zz[:height], ALONG_Z)
     xzz, xzs = send(zz, ALONG_X), send(zs, ALONG_X)
-    z2 = after(z2, xzz)
-    z2s = other(z2)
     fxzz = send(xzz, ALONG_X)
-    xz2, xz2s = send(z2, ALONG_X), send(z2s, ALONG_X)
-
-    left = left_panel_of(own, after(others, z2s), weights)
-
-    def both(arrays, first_core):
-        return [
-            (array, half, dx, core)
-            for array, dx in zip(arrays, (HERE, BACK, AHEAD, ACROSS))
-            for half, core in ((0, first_core), (1, 1 - first_core))
-        ]
-
-    def alike(mine, swapped, x_mine, x_swapped, their_x, their_x_swapped, fx_mine, their_fx):
-        return [
-            (mine, 0, HERE, 0),
-            (swapped, 0, HERE, 1),
-            (x_mine, 0, BACK, 0),
-            (x_swapped, 0, BACK, 1),
-            (their_x, 0, AHEAD, 1),
-            (their_x_swapped, 0, AHEAD, 0),
-            (fx_mine, 0, ACROSS, 0),
-            (their_fx, 0, ACROSS, 1),
-        ]
-
-    out = block_step(HERE, alike(p, ps, xp, xps, other(xp), other(xps), fxp, other(fxp)), left, gamma, None)
-    their_fxzz = other(after(fxzz, out))
-    out = block_step(BACK, both([zz, xzz, other(xzs), fxzz], 0), left, gamma, out)
-    fxz2 = send(after(xz2, out), ALONG_X)
-    out = block_step(AHEAD, both([after(zs, xz2s), xzs, other(xzz), their_fxzz], 1), left, gamma, out)
-    their_fx = other(after(fxz2, out))
-    return block_step(ACROSS, alike(z2, z2s, xz2, xz2s, other(xz2), other(xz2s), fxz2, their_fx), left, gamma, out)
+    z2 = jnp.concatenate([z2, other(z2)], 0)
+    xz2 = send(z2, ALONG_X)
+
+    left = left_panel_of(own, after(others, z2), weights)
+
+    def pieces(here, back, ahead, across, first_cores):
+        parts = [(here, HERE), (back, BACK), (ahead, AHEAD), (across, ACROSS)]
+        out = []
+        for (arrays, dx), first_core in zip(parts, first_cores):
+            arrays = arrays if isinstance(arrays, tuple) else (arrays, arrays)
+            halves = [0, 0] if arrays[0] is not arrays[1] else [0, 1]
+            order = [0, 1] if first_core == 0 else [1, 0]
+            out.append([(arrays[i], halves[i], dx, core) for core, i in enumerate(order)])
+        return out
+
+    def flat_list(groups, turned):
+        order = [3, 2, 1, 0] if turned else [0, 1, 2, 3]
+        return [piece for index in order for piece in groups[index]]
+
+    near = flat_list(pieces(zz, xzz, other(xzs), fxzz, (0, 0, 0, 0)), False)
+    far = flat_list(pieces(zs, xzs, other(xzz), other(fxzz), (1, 1, 1, 1)), True)
+    out = block_step([(BACK, near), (AHEAD, far)], left, gamma, None)
+    fxz2 = send(xz2[:height], ALONG_X)
+    same = flat_list(pieces(p, xp, other(xp), (fxp, other(fxp)), (0, 0, 1, 0)), False)
+    last = flat_list(pieces(z2, xz2, other(xz2), (fxz2, other(after(fxz2, out))), (0, 0, 1, 0)), True)
+    return block_step([(HERE, same), (ACROSS, last)], left, gamma, out)
 
 
 def solution(mesh):

time: 119 us -> 134 us (1.13)
  waiting for transfers between devices: 29.8 us -> 43.8 us
  local copies, waits for them, and re-layouts: 5.32 us -> 10.5 us
  starting transfers between devices: 50.8 us -> 47.2 us
    ppermute x25 -> x21, waiting for transfers between devices: 29.8 us -> 43.8 us  [send(): return lax.ppermute(value, AXES, way)]
    ppermute x25 -> x21, starting transfers between devices: 50.7 us -> 47.1 us  [send(): return lax.ppermute(value, AXES, way)]
    unnamed x30 -> x48, local copies, waits for them, and re-layouts: 5.3 us -> 8.65 us
    slice x0 -> x2, local copies, waits for them, and re-layouts: none -> 1.77 us  [the longest x1 1.74 us: per_device(): fxz2 = send(xz2[:height], ALONG_X)]
    pallas_call x4 -> x2, Pallas kernels: 16.1 us -> 16.7 us  [block_step(): pl.pallas_call(functools.partial(block_kernel, placed, len(arrays), heigh...]
  transfers between devices with their start and end apart: 27 -> 23, of which waited for: 7 -> 8; matrix products, arithmetic and copies ran while one was open for 0% -> 1% of each run, Pallas kernels for 12% -> 7%
where the time goes in v5:
time: 134 us; the launch traced here: 133 us
  starting transfers between devices  47.2 us (35%)
  waiting for transfers between devices  43.8 us (33%)
  Pallas kernels  18.3 us (14%)
  between operations  13.6 us (10%)
  local copies, waits for them, and re-layouts  10.5 us (8%)
    ppermute x21, starting transfers between devices, send(): return lax.ppermute(value, AXES, way)  47.1 us
    ppermute x21, waiting for transfers between devices, send(): return lax.ppermute(value, AXES, way)  43.8 us
    pallas_call x2, Pallas kernels, block_step(): pl.pallas_call(functools.partial(block_kernel, placed, len(arrays), heigh...  16.7 us
    unnamed x48, local copies, waits for them, and re-layouts  8.65 us
  transfers between devices with their start and end apart: 23, of which 8 were waited for; matrix products, arithmetic and copies ran while one was open for 1% of the time, Pallas kernels for 7%

profile of v5, /device:TPU:25, one launch (start us, length us, event | category | flops | bytes accessed | tf_op | source)
XLA Modules:
  0.0 133.4 jit_solution(18142593659822793680)
XLA Ops:
  9.2 1.7 %collective-permute-start = (bf16[640,256]{1,0:T(8,128)(2,1)}, bf16[640,256]{1,0:T(8,128)(2,1)S(1)}, u32[]{:S(2)}, u32[]{:S(2)}) collective-permute-start(bf16[640,256]{1,0:T(8,128)(2,1)} %join_shard.1), channel_id=1, source_target_pairs={{0,4},{1,5},{2,6},{3,7},{4,0},{5,1},{6,2},{7,3},{8,12},{9,13},{10,... | collective-permute-start | bytes 983048 | tf_op jit(solution)/shard_map/ppermute | solution.py:45
  10.9 9.3 %collective-permute-start.1 = (bf16[640,256]{1,0:T(8,128)(2,1)}, bf16[640,256]{1,0:T(8,128)(2,1)S(1)}, u32[]{:S(2)}, u32[]{:S(2)}) collective-permute-start(bf16[640,256]{1,0:T(8,128)(2,1)} %join_shard.1), channel_id=1, source_target_pairs={{0,0},{1,16},{2,32},{3,48},{4,8},{5,24},{6,40},{7,56},{8,160},{9,1... | collective-permute-start | bytes 983048 | tf_op jit(solution)/shard_map/ppermute | solution.py:45
  20.3 7.5 %collective-permute-done.1 = bf16[640,256]{1,0:T(8,128)(2,1)S(1)} collective-permute-done((bf16[640,256]{1,0:T(8,128)(2,1)}, bf16[640,256]{1,0:T(8,128)(2,1)S(1)}, u32[]{:S(2)}, u32[]{:S(2)}) %collective-permute-start.1) | collective-permute-done | bytes 327712 | tf_op jit(solution)/shard_map/ppermute | solution.py:45
  27.8 1.6 %collective-permute-done.2 = bf16[640,256]{1,0:T(8,128)(2,1)S(1)} collective-permute-done((bf16[640,256]{1,0:T(8,128)(2,1)S(1)}, bf16[640,256]{1,0:T(8,128)(2,1)S(1)}, u32[]{:S(2)}, u32[]{:S(2)}) %collective-permute-start.2) | collective-permute-done | bytes 327712 | tf_op jit(solution)/shard_map/ppermute | solution.py:45
  29.5 2.1 %collective-permute-start.3 = (bf16[1280,256]{1,0:T(8,128)(2,1)S(1)}, bf16[1280,256]{1,0:T(8,128)(2,1)S(1)}, u32[]{:S(2)}, u32[]{:S(2)}) collective-permute-start(bf16[1280,256]{1,0:T(8,128)(2,1)S(1)} %constant_dynamic-update-slice_fusion.refs_0_), channel_id=1, source_target_pairs={{0,16},{1,17},{2,18},{3,19},{4,20},{5,21},{6,22},{7,23},{8,56},{9,... | collective-permute-start | bytes 1966088 | tf_op jit(solution)/shard_map/ppermute | solution.py:45
  31.6 14.9 %collective-permute-start.4 = (bf16[1280,256]{1,0:T(8,128)(2,1)S(1)}, bf16[1280,256]{1,0:T(8,128)(2,1)S(1)}, u32[]{:S(2)}, u32[]{:S(2)}) collective-permute-start(bf16[1280,256]{1,0:T(8,128)(2,1)S(1)} %constant_dynamic-update-slice_fusion.refs_0_), channel_id=1, source_target_pairs={{0,64},{1,65},{2,66},{3,67},{4,68},{5,69},{6,70},{7,71},{8,200},{9... | collective-permute-start | bytes 1966088 | tf_op jit(solution)/shard_map/ppermute | solution.py:45
  48.4 10.9 %collective-permute-done.4.refs_0_ = bf16[1280,256]{1,0:T(8,128)(2,1)S(1)} collective-permute-done((bf16[1280,256]{1,0:T(8,128)(2,1)S(1)}, bf16[1280,256]{1,0:T(8,128)(2,1)S(1)}, u32[]{:S(2)}, u32[]{:S(2)}) %collective-permute-start.4) | collective-permute-done | bytes 655392 | tf_op jit(solution)/shard_map/ppermute | solution.py:45
  59.5 5.9 %collective-permute-start.6 = (bf16[640,256]{1,0:T(8,128)(2,1)S(1)}, bf16[640,256]{1,0:T(8,128)(2,1)S(1)}, u32[]{:S(2)}, u32[]{:S(2)}) collective-permute-start(bf16[640,256]{1,0:T(8,128)(2,1)S(1)} %slice.10), channel_id=1, source_target_pairs={{0,64},{1,65},{2,66},{3,67},{4,68},{5,69},{6,70},{7,71},{8,200},{9... | collective-permute-start | bytes 983048 | tf_op jit(solution)/shard_map/ppermute | solution.py:45
  65.4 6.2 %collective-permute-done.6 = bf16[640,256]{1,0:T(8,128)(2,1)S(1)} collective-permute-done((bf16[640,256]{1,0:T(8,128)(2,1)S(1)}, bf16[640,256]{1,0:T(8,128)(2,1)S(1)}, u32[]{:S(2)}, u32[]{:S(2)}) %collective-permute-start.6) | collective-permute-done | bytes 327712 | tf_op jit(solution)/shard_map/ppermute | solution.py:45
  71.6 1.1 collective-permute-start.7
  72.7 2.9 %collective-permute-start.16 = (bf16[1280,256]{1,0:T(8,128)(2,1)S(1)}, bf16[1280,256]{1,0:T(8,128)(2,1)}, u32[]{:S(2)}, u32[]{:S(2)}) collective-permute-start(bf16[1280,256]{1,0:T(8,128)(2,1)S(1)} %collective-permute-done.12.refs_1_), channel_id=1, source_target_pairs={{0,16},{1,17},{2,18},{3,19},{4,20},{5,21},{6,22},{7,23},{8,56},{9,... | collective-permute-start | bytes 1966088 | tf_op jit(solution)/shard_map/ppermute | solution.py:45
  75.8 1.2 collective-permute-start.10
  78.5 4.7 %collective-permute-done.16.refs_3_ = bf16[1280,256]{1,0:T(8,128)(2,1)} collective-permute-done((bf16[1280,256]{1,0:T(8,128)(2,1)S(1)}, bf16[1280,256]{1,0:T(8,128)(2,1)}, u32[]{:S(2)}, u32[]{:S(2)}) %collective-permute-start.16) | collective-permute-done | bytes 655392 | tf_op jit(solution)/shard_map/ppermute | solution.py:45
  83.2 1.5 %collective-permute-start.17 = (bf16[1280,256]{1,0:T(8,128)(2,1)}, bf16[1280,256]{1,0:T(8,128)(2,1)}, u32[]{:S(2)}, u32[]{:S(2)}) collective-permute-start(bf16[1280,256]{1,0:T(8,128)(2,1)} %collective-permute-done.16.refs_3_), channel_id=1, source_target_pairs={{0,8},{1,9},{2,10},{3,11},{4,12},{5,13},{6,14},{7,15},{8,0},{9,1},... | collective-permute-start | bytes 1966088 | tf_op jit(solution)/shard_map/ppermute | solution.py:45
  84.7 5.5 %collective-permute-done.14.refs_6_ = bf16[1280,256]{1,0:T(8,128)(2,1)} collective-permute-done((bf16[1280,256]{1,0:T(8,128)(2,1)S(1)}, bf16[1280,256]{1,0:T(8,128)(2,1)}, u32[]{:S(2)}, u32[]{:S(2)}) %collective-permute-start.14) | collective-permute-done | bytes 655392 | tf_op jit(solution)/shard_map/ppermute | solution.py:45
  90.2 1.5 %collective-permute-start.15 = (bf16[1280,256]{1,0:T(8,128)(2,1)}, bf16[1280,256]{1,0:T(8,128)(2,1)}, u32[]{:S(2)}, u32[]{:S(2)}) collective-permute-start(bf16[1280,256]{1,0:T(8,128)(2,1)} %collective-permute-done.14.refs_6_), channel_id=1, source_target_pairs={{0,8},{1,9},{2,10},{3,11},{4,12},{5,13},{6,14},{7,15},{8,0},{9,1},... | collective-permute-start | bytes 1966088 | tf_op jit(solution)/shard_map/ppermute | solution.py:45
  91.7 5.5 %collective-permute-done.10.refs_8_ = bf16[1280,256]{1,0:T(8,128)(2,1)} collective-permute-done((bf16[1280,256]{1,0:T(8,128)(2,1)S(1)}, bf16[1280,256]{1,0:T(8,128)(2,1)}, u32[]{:S(2)}, u32[]{:S(2)}) %collective-permute-start.10) | collective-permute-done | bytes 655392 | tf_op jit(solution)/shard_map/ppermute | solution.py:45
  97.2 1.7 %slice.13 = bf16[640,256]{1,0:T(8,128)(2,1)} slice(bf16[1280,256]{1,0:T(8,128)(2,1)} %collective-permute-done.10.refs_8_), slice={[0:640], [0:256]} | slice | bytes 655360 | tf_op jit(solution)/shard_map/slice | solution.py:251
  99.0 3.2 %collective-permute-start.11 = (bf16[640,256]{1,0:T(8,128)(2,1)}, bf16[640,256]{1,0:T(8,128)(2,1)}, u32[]{:S(2)}, u32[]{:S(2)}) collective-permute-start(bf16[640,256]{1,0:T(8,128)(2,1)} %slice.13), channel_id=1, source_target_pairs={{0,16},{1,17},{2,18},{3,19},{4,20},{5,21},{6,22},{7,23},{8,56},{9,... | collective-permute-start | bytes 983048 | tf_op jit(solution)/shard_map/ppermute | solution.py:45
  103.6 1.4 %copy-done.9 = bf16[2560,256]{1,0:T(8,128)(2,1)S(1)} copy-done((bf16[2560,256]{1,0:T(8,128)(2,1)S(1)}, bf16[2560,256]{1,0:T(8,128)(2,1)}, u32[]{:S(2)}) %copy-start.9) | copy-done | bytes 1310744
  104.9 1.3 copy-done.10
  107.8 8.4 %block_step.2.refs_11_ = bf16[640,2560]{1,0:T(8,128)(2,1)} custom-call(bf16[8,640,256]{2,1,0:T(8,128)(2,1)S(1)} %weigh_left.1.left_ref, bf16[1280,256]{1,0:T(8,128)(2,1)S(1)} %copy-done.2, bf16[1280,256]{1,0:T(8,128)(2,1)S(1)} %copy-done.12, bf16[1280,256]{1,0:T(8,128)(2,1)} %collective-permute-done.15.refs_2_, ...), custom_call_target="tpu_custom_call" | custom-call | flops 409600 | bytes 409600 | tf_op jit(solution)/shard_map/block_step/pallas_call | solution.py:187
  116.4 1.8 %collective-permute-done.19.refs_6_ = bf16[640,256]{1,0:T(8,128)(2,1)S(1)} collective-permute-done((bf16[640,256]{1,0:T(8,128)(2,1)}, bf16[640,256]{1,0:T(8,128)(2,1)S(1)}, u32[]{:S(2)}, u32[]{:S(2)}) %collective-permute-start.19) | collective-permute-done | bytes 327712 | tf_op jit(solution)/shard_map/ppermute | solution.py:45
  118.2 8.3 %block_step.3 = bf16[640,2560]{1,0:T(8,128)(2,1)} custom-call(bf16[8,640,256]{2,1,0:T(8,128)(2,1)S(1)} %weigh_left.1.left_ref, bf16[1280,256]{1,0:T(8,128)(2,1)S(1)} %copy-done.6, bf16[1280,256]{1,0:T(8,128)(2,1)S(1)} %copy-done.4, bf16[1280,256]{1,0:T(8,128)(2,1)} %collective-permute-done.8.refs_2_, ...), custom_call_target="tpu_custom_call", output_to_operand_aliasing={{}: (12, {})} | custom-call | flops 409600 | bytes 409600 | tf_op jit(solution)/shard_map/block_step/pallas_call | solution.py:187
  (82 shorter events, 9.5 us)
Async XLA Ops:
  6.5 41.8 %all-gather.5.cloned.1.call-start = ((), (), s32[]{:S(2)}) async-start(), calls=%async_computation | async-start | bytes 1638400 | tf_op jit(solution)/shard_map/all_gather | solution.py:215
  8.4 95.2 %copy-start.22 = (s32[1024]{0:T(1024)S(1)}, s32[1024]{0:T(1024)}, u32[]{:S(2)}) copy-start(s32[1024]{0:T(1024)} %param.6) | copy-start | bytes 12292
  9.1 94.4 %all-gather.7.cloned.1.call-start = ((), (), s32[]{:S(2)}) async-start(), calls=%async_computation.1 | async-start | bytes 1638400 | tf_op jit(solution)/shard_map/all_gather | solution.py:222
  9.2 11.1 %collective-permute-start = (bf16[640,256]{1,0:T(8,128)(2,1)}, bf16[640,256]{1,0:T(8,128)(2,1)S(1)}, u32[]{:S(2)}, u32[]{:S(2)}) collective-permute-start(bf16[640,256]{1,0:T(8,128)(2,1)} %join_shard.1), channel_id=1, source_target_pairs={{0,4},{1,5},{2,6},{3,7},{4,0},{5,1},{6,2},{7,3},{8,12},{9,13},{10,... | collective-permute-start | bytes 983048 | tf_op jit(solution)/shard_map/ppermute | solution.py:45
  10.9 16.9 %collective-permute-start.1 = (bf16[640,256]{1,0:T(8,128)(2,1)}, bf16[640,256]{1,0:T(8,128)(2,1)S(1)}, u32[]{:S(2)}, u32[]{:S(2)}) collective-permute-start(bf16[640,256]{1,0:T(8,128)(2,1)} %join_shard.1), channel_id=1, source_target_pairs={{0,0},{1,16},{2,32},{3,48},{4,8},{5,24},{6,40},{7,56},{8,160},{9,1... | collective-permute-start | bytes 983048 | tf_op jit(solution)/shard_map/ppermute | solution.py:45
  27.8 1.6 %collective-permute-start.2 = (bf16[640,256]{1,0:T(8,128)(2,1)S(1)}, bf16[640,256]{1,0:T(8,128)(2,1)S(1)}, u32[]{:S(2)}, u32[]{:S(2)}) collective-permute-start(bf16[640,256]{1,0:T(8,128)(2,1)S(1)} %collective-permute-done.1), channel_id=1, source_target_pairs={{0,8},{1,9},{2,10},{3,11},{4,12},{5,13},{6,14},{7,15},{8,0},{9,1},... | collective-permute-start | bytes 983048 | tf_op jit(solution)/shard_map/ppermute | solution.py:45
  29.5 17.9 %collective-permute-start.3 = (bf16[1280,256]{1,0:T(8,128)(2,1)S(1)}, bf16[1280,256]{1,0:T(8,128)(2,1)S(1)}, u32[]{:S(2)}, u32[]{:S(2)}) collective-permute-start(bf16[1280,256]{1,0:T(8,128)(2,1)S(1)} %constant_dynamic-update-slice_fusion.refs_0_), channel_id=1, source_target_pairs={{0,16},{1,17},{2,18},{3,19},{4,20},{5,21},{6,22},{7,23},{8,56},{9,... | collective-permute-start | bytes 1966088 | tf_op jit(solution)/shard_map/ppermute | solution.py:45
  31.6 27.7 %collective-permute-start.4 = (bf16[1280,256]{1,0:T(8,128)(2,1)S(1)}, bf16[1280,256]{1,0:T(8,128)(2,1)S(1)}, u32[]{:S(2)}, u32[]{:S(2)}) collective-permute-start(bf16[1280,256]{1,0:T(8,128)(2,1)S(1)} %constant_dynamic-update-slice_fusion.refs_0_), channel_id=1, source_target_pairs={{0,64},{1,65},{2,66},{3,67},{4,68},{5,69},{6,70},{7,71},{8,200},{9... | collective-permute-start | bytes 1966088 | tf_op jit(solution)/shard_map/ppermute | solution.py:45
  48.2 11.1 %collective-permute-start.5 = (bf16[640,256]{1,0:T(8,128)(2,1)S(1)}, bf16[640,256]{1,0:T(8,128)(2,1)S(1)}, u32[]{:S(2)}, u32[]{:S(2)}) collective-permute-start(bf16[640,256]{1,0:T(8,128)(2,1)S(1)} %slice.12), channel_id=1, source_target_pairs={{0,16},{1,17},{2,18},{3,19},{4,20},{5,21},{6,22},{7,23},{8,56},{9,... | collective-permute-start | bytes 983048 | tf_op jit(solution)/shard_map/ppermute | solution.py:45
  59.3 13.4 %collective-permute-start.12 = (bf16[1280,256]{1,0:T(8,128)(2,1)S(1)}, bf16[1280,256]{1,0:T(8,128)(2,1)S(1)}, u32[]{:S(2)}, u32[]{:S(2)}) collective-permute-start(bf16[1280,256]{1,0:T(8,128)(2,1)S(1)} %collective-permute-done.4.refs_0_), channel_id=1, source_target_pairs={{0,16},{1,17},{2,18},{3,19},{4,20},{5,21},{6,22},{7,23},{8,56},{9,... | collective-permute-start | bytes 1966088 | tf_op jit(solution)/shard_map/ppermute | solution.py:45
  59.3 16.3 %collective-permute-start.13 = (bf16[1280,256]{1,0:T(8,128)(2,1)S(1)}, bf16[1280,256]{1,0:T(8,128)(2,1)S(1)}, u32[]{:S(2)}, u32[]{:S(2)}) collective-permute-start(bf16[1280,256]{1,0:T(8,128)(2,1)S(1)} %collective-permute-done.4.refs_0_), channel_id=1, source_target_pairs={{0,8},{1,9},{2,10},{3,11},{4,12},{5,13},{6,14},{7,15},{8,0},{9,1},... | collective-permute-start | bytes 1966088 | tf_op jit(solution)/shard_map/ppermute | solution.py:45
  59.5 12.0 %collective-permute-start.6 = (bf16[640,256]{1,0:T(8,128)(2,1)S(1)}, bf16[640,256]{1,0:T(8,128)(2,1)S(1)}, u32[]{:S(2)}, u32[]{:S(2)}) collective-permute-start(bf16[640,256]{1,0:T(8,128)(2,1)S(1)} %slice.10), channel_id=1, source_target_pairs={{0,64},{1,65},{2,66},{3,67},{4,68},{5,69},{6,70},{7,71},{8,200},{9... | collective-permute-start | bytes 983048 | tf_op jit(solution)/shard_map/ppermute | solution.py:45
  71.6 4.2 %collective-permute-start.7 = (bf16[640,256]{1,0:T(8,128)(2,1)S(1)}, bf16[640,256]{1,0:T(8,128)(2,1)S(1)}, u32[]{:S(2)}, u32[]{:S(2)}) collective-permute-start(bf16[640,256]{1,0:T(8,128)(2,1)S(1)} %collective-permute-done.6), channel_id=1, source_target_pairs={{0,8},{1,9},{2,10},{3,11},{4,12},{5,13},{6,14},{7,15},{8,0},{9,1},... | collective-permute-start | bytes 983048 | tf_op jit(solution)/shard_map/ppermute | solution.py:45
  72.7 10.5 %collective-permute-start.16 = (bf16[1280,256]{1,0:T(8,128)(2,1)S(1)}, bf16[1280,256]{1,0:T(8,128)(2,1)}, u32[]{:S(2)}, u32[]{:S(2)}) collective-permute-start(bf16[1280,256]{1,0:T(8,128)(2,1)S(1)} %collective-permute-done.12.refs_1_), channel_id=1, source_target_pairs={{0,16},{1,17},{2,18},{3,19},{4,20},{5,21},{6,22},{7,23},{8,56},{9,... | collective-permute-start | bytes 1966088 | tf_op jit(solution)/shard_map/ppermute | solution.py:45
  75.6 14.5 %collective-permute-start.14 = (bf16[1280,256]{1,0:T(8,128)(2,1)S(1)}, bf16[1280,256]{1,0:T(8,128)(2,1)}, u32[]{:S(2)}, u32[]{:S(2)}) collective-permute-start(bf16[1280,256]{1,0:T(8,128)(2,1)S(1)} %collective-permute-done.13.refs_7_), channel_id=1, source_target_pairs={{0,16},{1,17},{2,18},{3,19},{4,20},{5,21},{6,22},{7,23},{8,56},{9,... | collective-permute-start | bytes 1966088 | tf_op jit(solution)/shard_map/ppermute | solution.py:45
  75.8 21.4 %collective-permute-start.10 = (bf16[1280,256]{1,0:T(8,128)(2,1)S(1)}, bf16[1280,256]{1,0:T(8,128)(2,1)}, u32[]{:S(2)}, u32[]{:S(2)}) collective-permute-start(bf16[1280,256]{1,0:T(8,128)(2,1)S(1)} %constant_dynamic-update-slice_fusion.2.refs_9_), channel_id=1, source_target_pairs={{0,16},{1,17},{2,18},{3,19},{4,20},{5,21},{6,22},{7,23},{8,56},{9,... | collective-permute-start | bytes 1966088 | tf_op jit(solution)/shard_map/ppermute | solution.py:45
  77.9 24.3 %collective-permute-start.18 = (bf16[1280,256]{1,0:T(8,128)(2,1)S(1)}, bf16[1280,256]{1,0:T(8,128)(2,1)S(1)}, u32[]{:S(2)}, u32[]{:S(2)}) collective-permute-start(bf16[1280,256]{1,0:T(8,128)(2,1)S(1)} %collective-permute-done.12.refs_1_), channel_id=1, source_target_pairs={{0,8},{1,9},{2,10},{3,11},{4,12},{5,13},{6,14},{7,15},{8,0},{9,1},... | collective-permute-start | bytes 1966088 | tf_op jit(solution)/shard_map/ppermute | solution.py:45
  83.2 24.0 %collective-permute-start.17 = (bf16[1280,256]{1,0:T(8,128)(2,1)}, bf16[1280,256]{1,0:T(8,128)(2,1)}, u32[]{:S(2)}, u32[]{:S(2)}) collective-permute-start(bf16[1280,256]{1,0:T(8,128)(2,1)} %collective-permute-done.16.refs_3_), channel_id=1, source_target_pairs={{0,8},{1,9},{2,10},{3,11},{4,12},{5,13},{6,14},{7,15},{8,0},{9,1},... | collective-permute-start | bytes 1966088 | tf_op jit(solution)/shard_map/ppermute | solution.py:45
  90.2 17.1 %collective-permute-start.15 = (bf16[1280,256]{1,0:T(8,128)(2,1)}, bf16[1280,256]{1,0:T(8,128)(2,1)}, u32[]{:S(2)}, u32[]{:S(2)}) collective-permute-start(bf16[1280,256]{1,0:T(8,128)(2,1)} %collective-permute-done.14.refs_6_), channel_id=1, source_target_pairs={{0,8},{1,9},{2,10},{3,11},{4,12},{5,13},{6,14},{7,15},{8,0},{9,1},... | collective-permute-start | bytes 1966088 | tf_op jit(solution)/shard_map/ppermute | solution.py:45
  99.0 17.3 %collective-permute-start.11 = (bf16[640,256]{1,0:T(8,128)(2,1)}, bf16[640,256]{1,0:T(8,128)(2,1)}, u32[]{:S(2)}, u32[]{:S(2)}) collective-permute-start(bf16[640,256]{1,0:T(8,128)(2,1)} %slice.13), channel_id=1, source_target_pairs={{0,16},{1,17},{2,18},{3,19},{4,20},{5,21},{6,22},{7,23},{8,56},{9,... | collective-permute-start | bytes 983048 | tf_op jit(solution)/shard_map/ppermute | solution.py:45
  102.2 14.2 %collective-permute-start.8 = (bf16[1280,256]{1,0:T(8,128)(2,1)}, bf16[1280,256]{1,0:T(8,128)(2,1)}, u32[]{:S(2)}, u32[]{:S(2)}) collective-permute-start(bf16[1280,256]{1,0:T(8,128)(2,1)} %copy-done.3), channel_id=1, source_target_pairs={{0,8},{1,9},{2,10},{3,11},{4,12},{5,13},{6,14},{7,15},{8,0},{9,1},... | collective-permute-start | bytes 1966088 | tf_op jit(solution)/shard_map/ppermute | solution.py:45
  103.0 13.4 %collective-permute-start.20 = (bf16[1280,256]{1,0:T(8,128)(2,1)}, bf16[1280,256]{1,0:T(8,128)(2,1)}, u32[]{:S(2)}, u32[]{:S(2)}) collective-permute-start(bf16[1280,256]{1,0:T(8,128)(2,1)} %collective-permute-done.10.refs_8_), channel_id=1, source_target_pairs={{0,8},{1,9},{2,10},{3,11},{4,12},{5,13},{6,14},{7,15},{8,0},{9,1},... | collective-permute-start | bytes 1966088 | tf_op jit(solution)/shard_map/ppermute | solution.py:45
  107.2 9.2 %collective-permute-start.9 = (bf16[640,256]{1,0:T(8,128)(2,1)S(1)}, bf16[640,256]{1,0:T(8,128)(2,1)S(1)}, u32[]{:S(2)}, u32[]{:S(2)}) collective-permute-start(bf16[640,256]{1,0:T(8,128)(2,1)S(1)} %copy-done.18), channel_id=1, source_target_pairs={{0,8},{1,9},{2,10},{3,11},{4,12},{5,13},{6,14},{7,15},{8,0},{9,1},... | collective-permute-start | bytes 983048 | tf_op jit(solution)/shard_map/ppermute | solution.py:45
  116.3 1.9 %collective-permute-start.19 = (bf16[640,256]{1,0:T(8,128)(2,1)}, bf16[640,256]{1,0:T(8,128)(2,1)S(1)}, u32[]{:S(2)}, u32[]{:S(2)}) collective-permute-start(bf16[640,256]{1,0:T(8,128)(2,1)} %collective-permute-done.11.refs_5_), channel_id=1, source_target_pairs={{0,8},{1,9},{2,10},{3,11},{4,12},{5,13},{6,14},{7,15},{8,0},{9,1},... | collective-permute-start | bytes 983048 | tf_op jit(solution)/shard_map/ppermute | solution.py:45
  (22 other events, 193.5 us)
Sparse Core Ops, SparseCore 0:
  9.3 29.5 all-gather.4
  48.5 29.8 all-gather.6

commit v6 on v5

--- a/solution.py
+++ b/solution.py
@@ -120,7 +120,7 @@
 
 def block_kernel(blocks, operands, height, left_ref, *refs):
     arrays, gamma_ref = refs[:operands], refs[operands]
-    out_ref, old, new, sems = refs[-4:]
+    out_ref, right, total, old, new, sems = refs[-6:]
     row, col = lax.axis_index("row"), lax.axis_index("col")
     zh, x, core = lax.div(row, jnp.int32(X * CORE)), rem(lax.div(row, jnp.int32(CORE)), X), rem(row, CORE)
     way = 2 * core - 1
@@ -129,38 +129,61 @@
         turn = rem(zh + dz[0] + dz[1] * way + 2 * ZH - lax.div(col, jnp.int32(2)), ZH)
         return rem(turn, 2), lax.div(turn, jnp.int32(2))
 
-    columns, coming = [], []
+    count, width = len(blocks[0][1]), arrays[0].shape[-1]
+    phases = 2
+    arriving = [[] for _ in range(phases)]
+    for place in range(count):
+        for index, (_, pieces) in enumerate(blocks):
+            array, skip = pieces[place][:2]
+            arriving[place * phases // count].append(
+                pltpu.make_async_copy(
+                    arrays[array].at[pl.ds(skip * height, height), :],
+                    right.at[pl.ds(index * height, height), pl.ds(place * width, width)],
+                    sems.at[place * len(blocks) + index],
+                )
+            )
+    columns = []
     for index, (dz, _) in enumerate(blocks):
         low, high = turn_of(dz)
         columns.append(pl.ds(pl.multiple_of((low * 2 + high) * height, 128), height))
         here = old.at[:, pl.ds(index * height, height)]
-        coming.append(pltpu.make_async_copy(gamma_ref.at[:, columns[index]], here, sems.at[index]))
-        coming[index].start()
+        copy = pltpu.make_async_copy(gamma_ref.at[:, columns[index]], here, sems.at[count * len(blocks) + index])
+        arriving[-1].append(copy)
+    for copies in arriving:
+        for copy in copies:
+            copy.start()
     high = turn_of(blocks[0][0])[1]
-    left, right = [], []
-    for place in range(len(blocks[0][1])):
+    left = []
+    for place in range(count):
         _, _, dx, other_core = blocks[0][1][place]
         zl, y = rem(core + other_core, CORE), rem(x + dx[0] + dx[1] * way + 2 * X - 2 * high, X)
         left.append(left_ref[rem(zl + lax.div(col, jnp.int32(Y)), ZL) * Y + y])
-        halves = [(arrays[pieces[place][0]], pieces[place][1]) for _, pieces in blocks]
-        right.append(jnp.concatenate([array[skip * height : (skip + 1) * height, :] for array, skip in halves], 0))
-    left, right = jnp.concatenate(left, 1), jnp.concatenate(right, 1)
-    total = len(blocks) * height
+    all_columns = len(blocks) * height
     going = []
-    for first in range(0, total, 512):
-        last = min(first + 512, total)
-        commutator = lax.dot_general(
-            left, right[first:last], (((1,), (1,)), ((), ())), preferred_element_type=jnp.float32
-        )
-        if first == 0:
-            for copy in coming:
-                copy.wait()
-        new[:, first:last] = (old[:, first:last].astype(jnp.float32) + euler_step * commutator).astype(jnp.bfloat16)
-        while (len(going) + 1) * height <= last:
-            index = len(going)
-            there = out_ref.at[:, columns[index]]
-            going.append(pltpu.make_async_copy(new.at[:, pl.ds(index * height, height)], there, sems.at[len(blocks) + index]))
-            going[index].start()
+    for phase, copies in enumerate(arriving):
+        for copy in copies:
+            copy.wait()
+        depth = count // phases
+        mine = jnp.concatenate(left[phase * depth : (phase + 1) * depth], 1)
+        for first in range(0, all_columns, 512):
+            last = min(first + 512, all_columns)
+            commutator = lax.dot_general(
+                mine,
+                right[first:last, phase * depth * width : (phase + 1) * depth * width],
+                (((1,), (1,)), ((), ())),
+                preferred_element_type=jnp.float32,
+            )
+            if phase > 0:
+                commutator = total[:, first:last] + commutator
+            if phase < phases - 1:
+                total[:, first:last] = commutator
+                continue
+            new[:, first:last] = (old[:, first:last].astype(jnp.float32) + euler_step * commutator).astype(jnp.bfloat16)
+            while (len(going) + 1) * height <= last:
+                index = len(going)
+                there, sem = out_ref.at[:, columns[index]], sems.at[(count + 1) * len(blocks) + index]
+                going.append(pltpu.make_async_copy(new.at[:, pl.ds(index * height, height)], there, sem))
+                going[index].start()
     for copy in going:
         copy.wait()
 
@@ -187,16 +210,18 @@
     return pl.pallas_call(
         functools.partial(block_kernel, placed, len(arrays), height),
         in_specs=[
-            *[pl.BlockSpec(memory_space=pltpu.VMEM)] * (1 + len(arrays)),
-            *[anywhere] * (len(operands) - 1 - len(arrays)),
+            pl.BlockSpec(memory_space=pltpu.VMEM),
+            *[anywhere] * (len(operands) - 1),
         ],
         out_specs=anywhere,
         out_shape=jax.ShapeDtypeStruct(gamma.shape, gamma.dtype),
         input_output_aliases=aliases,
         scratch_shapes=[
+            pltpu.VMEM((len(blocks) * height, width), jnp.bfloat16),
+            pltpu.VMEM((height, len(blocks) * height), jnp.float32),
             pltpu.VMEM((height, len(blocks) * height), jnp.bfloat16),
             pltpu.VMEM((height, len(blocks) * height), jnp.bfloat16),
-            pltpu.SemaphoreType.DMA((2 * len(blocks),)),
+            pltpu.SemaphoreType.DMA(((len(blocks[0][1]) + 2) * len(blocks),)),
         ],
         compiler_params=pltpu.CompilerParams(vmem_limit_bytes=28 * 2**20),
         cost_estimate=pl.CostEstimate(flops=height * height, bytes_accessed=height * height, transcendentals=0),
@@ -217,41 +242,42 @@
     p = send(shard, TO_HOME)
     other_zl = send(shard, OTHER_ZL)
     p = after(p, other_zl)
-    p = jnp.concatenate([p, other(p)], 0)
-    xp = send(p, ALONG_X)
+    ps = other(p)
+    za, zb = send(p, ALONG_Z), send(ps, ALONG_Z)
+    xp, xps = send(p, ALONG_X), send(ps, ALONG_X)
     others = lax.all_gather(after(other_zl, own, xp), "col", axis_index_groups=alike_y)
-    fxp = send(xp[:height], ALONG_X)
-    zz = after(send(p, ALONG_Z), fxp)
+    fxp = send(after(xp, xps), ALONG_X)
+    z2 = send(za, ALONG_Z)
+    zz = jnp.concatenate([za, after(zb, xps, fxp)], 0)
     zs = other(zz)
-    z2 = send(zz[:height], ALONG_Z)
     xzz, xzs = send(zz, ALONG_X), send(zs, ALONG_X)
-    fxzz = send(xzz, ALONG_X)
-    z2 = jnp.concatenate([z2, other(z2)], 0)
-    xz2 = send(z2, ALONG_X)
-
-    left = left_panel_of(own, after(others, z2), weights)
-
-    def pieces(here, back, ahead, across, first_cores):
-        parts = [(here, HERE), (back, BACK), (ahead, AHEAD), (across, ACROSS)]
-        out = []
-        for (arrays, dx), first_core in zip(parts, first_cores):
-            arrays = arrays if isinstance(arrays, tuple) else (arrays, arrays)
-            halves = [0, 0] if arrays[0] is not arrays[1] else [0, 1]
-            order = [0, 1] if first_core == 0 else [1, 0]
-            out.append([(arrays[i], halves[i], dx, core) for core, i in enumerate(order)])
-        return out
-
-    def flat_list(groups, turned):
-        order = [3, 2, 1, 0] if turned else [0, 1, 2, 3]
-        return [piece for index in order for piece in groups[index]]
-
-    near = flat_list(pieces(zz, xzz, other(xzs), fxzz, (0, 0, 0, 0)), False)
-    far = flat_list(pieces(zs, xzs, other(xzz), other(fxzz), (1, 1, 1, 1)), True)
-    out = block_step([(BACK, near), (AHEAD, far)], left, gamma, None)
-    fxz2 = send(xz2[:height], ALONG_X)
-    same = flat_list(pieces(p, xp, other(xp), (fxp, other(fxp)), (0, 0, 1, 0)), False)
-    last = flat_list(pieces(z2, xz2, other(xz2), (fxz2, other(after(fxz2, out))), (0, 0, 1, 0)), True)
-    return block_step([(HERE, same), (ACROSS, last)], left, gamma, out)
+    fxzz = send(after(xzz, z2), ALONG_X)
+    z2s = other(z2)
+    xz2, xz2s = send(z2, ALONG_X), send(z2s, ALONG_X)
+
+    left = left_panel_of(own, after(others, z2s), weights)
+
+    def singles(here, back, ahead, across):
+        return list(zip((*here, *back, *ahead, *across), [0] * 8, [HERE] * 2 + [BACK] * 2 + [AHEAD] * 2 + [ACROSS] * 2, [0, 1] * 4))
+
+    def pairs_of(arrays, first_core):
+        return [
+            (array, core ^ first_core, dx, core)
+            for array, dx in zip(arrays, (HERE, BACK, AHEAD, ACROSS))
+            for core in (0, 1)
+        ]
+
+    def turned(pieces):
+        return [piece for index in (3, 2, 1, 0) for piece in pieces[2 * index : 2 * index + 2]]
+
+    fxz2 = send(xz2, ALONG_X)
+    near = pairs_of([zz, xzz, other(xzs), fxzz], 0)
+    far = pairs_of([zs, xzs, other(xzz), other(after(fxzz, xz2, xz2s))], 1)
+    out = block_step([(BACK, near), (AHEAD, turned(far))], left, gamma, None)
+    their_fxz2 = other(after(fxz2, out))
+    same = singles((p, ps), (xp, xps), (other(xps), other(xp)), (fxp, other(fxp)))
+    last = singles((z2, z2s), (xz2, xz2s), (other(xz2s), other(xz2)), (fxz2, their_fxz2))
+    return block_step([(HERE, same), (ACROSS, turned(last))], left, gamma, out)
 
 
 def solution(mesh):

time: 134 us -> 133 us (level); the launches traced: 133 us -> 131 us
  Pallas kernels: 18.3 us -> 15.2 us
  local copies, waits for them, and re-layouts: 10.5 us -> 12.5 us
  waiting for transfers between devices: 43.8 us -> 42.2 us
    pallas_call x2, Pallas kernels: 16.7 us -> 13.7 us  [block_step(): pl.pallas_call(functools.partial(block_kernel, placed, len(arrays), heigh...]
    unnamed x48 -> x51, local copies, waits for them, and re-layouts: 8.65 us -> 10.7 us
    slice x3 -> x0, local copies, waits for them, and re-layouts: 1.79 us -> none  [the longest x1 1.74 us: per_device(): fxz2 = send(xz2[:height], ALONG_X)]
    concatenate x2 -> x1, local copies, waits for them, and re-layouts: 0.05 us -> 1.72 us  [per_device(): zz = jnp.concatenate([za, after(zb, xps, fxp)], 0)]
    ppermute x21 -> x26, waiting for transfers between devices: 43.8 us -> 42.2 us  [send(): return lax.ppermute(value, AXES, way)]
    ppermute x21 -> x26, starting transfers between devices: 47.1 us -> 46.5 us  [send(): return lax.ppermute(value, AXES, way)]
  transfers between devices with their start and end apart: 23 -> 28, of which waited for: 8 -> 8; matrix products, arithmetic and copies ran while one was open for 1% -> 2% of each run, Pallas kernels for 7% -> 6%
where the time goes in v6:
time: 133 us; the launch traced here: 131 us
  starting transfers between devices  46.6 us (35%)
  waiting for transfers between devices  42.2 us (32%)
  Pallas kernels  15.2 us (11%)
  between operations  13.6 us (10%)
  local copies, waits for them, and re-layouts  12.5 us (9%)
    ppermute x26, starting transfers between devices, send(): return lax.ppermute(value, AXES, way)  46.5 us
    ppermute x26, waiting for transfers between devices, send(): return lax.ppermute(value, AXES, way)  42.2 us
    pallas_call x2, Pallas kernels, block_step(): pl.pallas_call(functools.partial(block_kernel, placed, len(arrays), heigh...  13.7 us
    unnamed x51, local copies, waits for them, and re-layouts  10.7 us
  transfers between devices with their start and end apart: 28, of which 8 were waited for; matrix products, arithmetic and copies ran while one was open for 2% of the time, Pallas kernels for 6%

profile of v6, /device:TPU:25, one launch (start us, length us, event | category | flops | bytes accessed | tf_op | source)
XLA Modules:
  0.0 130.8 jit_solution(15560731369856367334)
XLA Ops:
  9.2 1.7 %collective-permute-start = (bf16[640,256]{1,0:T(8,128)(2,1)}, bf16[640,256]{1,0:T(8,128)(2,1)S(1)}, u32[]{:S(2)}, u32[]{:S(2)}) collective-permute-start(bf16[640,256]{1,0:T(8,128)(2,1)} %join_shard.1), channel_id=1, source_target_pairs={{0,4},{1,5},{2,6},{3,7},{4,0},{5,1},{6,2},{7,3},{8,12},{9,13},{10,... | collective-permute-start | bytes 983048 | tf_op jit(solution)/shard_map/ppermute | solution.py:45
  10.9 9.3 %collective-permute-start.1 = (bf16[640,256]{1,0:T(8,128)(2,1)}, bf16[640,256]{1,0:T(8,128)(2,1)S(1)}, u32[]{:S(2)}, u32[]{:S(2)}) collective-permute-start(bf16[640,256]{1,0:T(8,128)(2,1)} %join_shard.1), channel_id=1, source_target_pairs={{0,0},{1,16},{2,32},{3,48},{4,8},{5,24},{6,40},{7,56},{8,160},{9,1... | collective-permute-start | bytes 983048 | tf_op jit(solution)/shard_map/ppermute | solution.py:45
  20.3 7.5 %collective-permute-done.1.refs_0_ = bf16[640,256]{1,0:T(8,128)(2,1)S(1)} collective-permute-done((bf16[640,256]{1,0:T(8,128)(2,1)}, bf16[640,256]{1,0:T(8,128)(2,1)S(1)}, u32[]{:S(2)}, u32[]{:S(2)}) %collective-permute-start.1) | collective-permute-done | bytes 327712 | tf_op jit(solution)/shard_map/ppermute | solution.py:45
  27.8 2.4 %collective-permute-start.2 = (bf16[640,256]{1,0:T(8,128)(2,1)S(1)}, bf16[640,256]{1,0:T(8,128)(2,1)S(1)}, u32[]{:S(2)}, u32[]{:S(2)}) collective-permute-start(bf16[640,256]{1,0:T(8,128)(2,1)S(1)} %collective-permute-done.1.refs_0_), channel_id=1, source_target_pairs={{0,16},{1,17},{2,18},{3,19},{4,20},{5,21},{6,22},{7,23},{8,56},{9,... | collective-permute-start | bytes 983048 | tf_op jit(solution)/shard_map/ppermute | solution.py:45
  30.3 1.2 collective-permute-start.7
  31.5 14.9 %collective-permute-start.3 = (bf16[640,256]{1,0:T(8,128)(2,1)S(1)}, bf16[640,256]{1,0:T(8,128)(2,1)S(1)}, u32[]{:S(2)}, u32[]{:S(2)}) collective-permute-start(bf16[640,256]{1,0:T(8,128)(2,1)S(1)} %collective-permute-done.1.refs_0_), channel_id=1, source_target_pairs={{0,64},{1,65},{2,66},{3,67},{4,68},{5,69},{6,70},{7,71},{8,200},{9... | collective-permute-start | bytes 983048 | tf_op jit(solution)/shard_map/ppermute | solution.py:45
  48.0 5.5 %collective-permute-done.3 = bf16[640,256]{1,0:T(8,128)(2,1)S(1)} collective-permute-done((bf16[640,256]{1,0:T(8,128)(2,1)S(1)}, bf16[640,256]{1,0:T(8,128)(2,1)S(1)}, u32[]{:S(2)}, u32[]{:S(2)}) %collective-permute-start.3) | collective-permute-done | bytes 327712 | tf_op jit(solution)/shard_map/ppermute | solution.py:45
  55.0 2.0 %collective-permute-done.14 = bf16[640,256]{1,0:T(8,128)(2,1)S(1)} collective-permute-done((bf16[640,256]{1,0:T(8,128)(2,1)S(1)}, bf16[640,256]{1,0:T(8,128)(2,1)S(1)}, u32[]{:S(2)}, u32[]{:S(2)}) %collective-permute-start.14) | collective-permute-done | bytes 327712 | tf_op jit(solution)/shard_map/ppermute | solution.py:45
  57.8 1.7 %constant_dynamic-update-slice_fusion.refs_0_ = bf16[1280,256]{1,0:T(8,128)(2,1)} fusion(bf16[1280,256]{1,0:T(8,128)(2,1)} %constant_dynamic-update-slice_fusion.1, bf16[640,256]{1,0:T(8,128)(2,1)} %copy-done.24), kind=kLoop, calls=%fused_computation | loop fusion | bytes 655360 | tf_op jit(solution)/shard_map/concatenate | solution.py:251
  59.5 1.4 %collective-permute-start.15 = (bf16[1280,256]{1,0:T(8,128)(2,1)}, bf16[1280,256]{1,0:T(8,128)(2,1)}, u32[]{:S(2)}, u32[]{:S(2)}) collective-permute-start(bf16[1280,256]{1,0:T(8,128)(2,1)} %constant_dynamic-update-slice_fusion.refs_0_), channel_id=1, source_target_pairs={{0,16},{1,17},{2,18},{3,19},{4,20},{5,21},{6,22},{7,23},{8,56},{9,... | collective-permute-start | bytes 1966088 | tf_op jit(solution)/shard_map/ppermute | solution.py:45
  60.9 1.0 collective-permute-start.16
  61.9 3.6 %collective-permute-start.4 = (bf16[640,256]{1,0:T(8,128)(2,1)}, bf16[640,256]{1,0:T(8,128)(2,1)S(1)}, u32[]{:S(2)}, u32[]{:S(2)}) collective-permute-start(bf16[640,256]{1,0:T(8,128)(2,1)} %copy-done.23), channel_id=1, source_target_pairs={{0,64},{1,65},{2,66},{3,67},{4,68},{5,69},{6,70},{7,71},{8,200},{9... | collective-permute-start | bytes 983048 | tf_op jit(solution)/shard_map/ppermute | solution.py:45
  65.5 7.7 %collective-permute-done.4.refs_14_ = bf16[640,256]{1,0:T(8,128)(2,1)S(1)} collective-permute-done((bf16[640,256]{1,0:T(8,128)(2,1)}, bf16[640,256]{1,0:T(8,128)(2,1)S(1)}, u32[]{:S(2)}, u32[]{:S(2)}) %collective-permute-start.4) | collective-permute-done | bytes 327712 | tf_op jit(solution)/shard_map/ppermute | solution.py:45
  74.0 2.8 %collective-permute-start.19 = (bf16[1280,256]{1,0:T(8,128)(2,1)}, bf16[1280,256]{1,0:T(8,128)(2,1)}, u32[]{:S(2)}, u32[]{:S(2)}) collective-permute-start(bf16[1280,256]{1,0:T(8,128)(2,1)} %collective-permute-done.15.refs_1_), channel_id=1, source_target_pairs={{0,16},{1,17},{2,18},{3,19},{4,20},{5,21},{6,22},{7,23},{8,56},{9,... | collective-permute-start | bytes 1966088 | tf_op jit(solution)/shard_map/ppermute | solution.py:45
  79.9 1.1 collective-permute-start.22
  81.0 14.1 %collective-permute-done.12.refs_12_ = bf16[640,256]{1,0:T(8,128)(2,1)} collective-permute-done((bf16[640,256]{1,0:T(8,128)(2,1)S(1)}, bf16[640,256]{1,0:T(8,128)(2,1)}, u32[]{:S(2)}, u32[]{:S(2)}) %collective-permute-start.12) | collective-permute-done | bytes 327712 | tf_op jit(solution)/shard_map/ppermute | solution.py:45
  95.1 3.5 %collective-permute-done.20.refs_13_ = bf16[640,256]{1,0:T(8,128)(2,1)S(1)} collective-permute-done((bf16[640,256]{1,0:T(8,128)(2,1)S(1)}, bf16[640,256]{1,0:T(8,128)(2,1)S(1)}, u32[]{:S(2)}, u32[]{:S(2)}) %collective-permute-start.20) | collective-permute-done | bytes 327712 | tf_op jit(solution)/shard_map/ppermute | solution.py:45
  98.6 1.5 %collective-permute-start.21 = (bf16[1280,256]{1,0:T(8,128)(2,1)}, bf16[1280,256]{1,0:T(8,128)(2,1)}, u32[]{:S(2)}, u32[]{:S(2)}) collective-permute-start(bf16[1280,256]{1,0:T(8,128)(2,1)} %collective-permute-done.19.refs_3_), channel_id=1, source_target_pairs={{0,8},{1,9},{2,10},{3,11},{4,12},{5,13},{6,14},{7,15},{8,0},{9,1},... | collective-permute-start | bytes 1966088 | tf_op jit(solution)/shard_map/ppermute | solution.py:45
  100.8 1.7 %collective-permute-start.13 = (bf16[640,256]{1,0:T(8,128)(2,1)}, bf16[640,256]{1,0:T(8,128)(2,1)}, u32[]{:S(2)}, u32[]{:S(2)}) collective-permute-start(bf16[640,256]{1,0:T(8,128)(2,1)} %collective-permute-done.12.refs_12_), channel_id=1, source_target_pairs={{0,16},{1,17},{2,18},{3,19},{4,20},{5,21},{6,22},{7,23},{8,56},{9,... | collective-permute-start | bytes 983048 | tf_op jit(solution)/shard_map/ppermute | solution.py:45
  103.1 1.4 %copy-done.2 = bf16[2560,256]{1,0:T(8,128)(2,1)S(1)} copy-done((bf16[2560,256]{1,0:T(8,128)(2,1)S(1)}, bf16[2560,256]{1,0:T(8,128)(2,1)}, u32[]{:S(2)}) %copy-start.2) | copy-done | bytes 1310744
  104.5 1.3 %copy-done.3 = bf16[2560,256]{1,0:T(8,128)(2,1)S(1)} copy-done((bf16[2560,256]{1,0:T(8,128)(2,1)S(1)}, bf16[2560,256]{1,0:T(8,128)(2,1)}, u32[]{:S(2)}) %copy-start.3) | copy-done | bytes 1310744
  107.8 7.1 %block_step.2.refs_17_ = bf16[640,2560]{1,0:T(8,128)(2,1)} custom-call(bf16[8,640,256]{2,1,0:T(8,128)(2,1)S(1)} %weigh_left.1.left_ref, bf16[1280,256]{1,0:T(8,128)(2,1)S(1)} %copy-done.1, bf16[1280,256]{1,0:T(8,128)(2,1)} %collective-permute-done.15.refs_1_, bf16[1280,256]{1,0:T(8,128)(2,1)} %collective-permute-done.18.refs_2_, ...), custom_call_target="tpu_custom_call" | custom-call | flops 409600 | bytes 409600 | tf_op jit(solution)/shard_map/block_step/pallas_call | solution.py:210
  115.5 1.1 collective-permute-done.24.refs_10_
  117.4 6.6 %block_step.3 = bf16[640,2560]{1,0:T(8,128)(2,1)} custom-call(bf16[8,640,256]{2,1,0:T(8,128)(2,1)S(1)} %weigh_left.1.left_ref, bf16[640,256]{1,0:T(8,128)(2,1)S(1)} %copy-done.7, bf16[640,256]{1,0:T(8,128)(2,1)S(1)} %copy-done.9, bf16[640,256]{1,0:T(8,128)(2,1)S(1)} %copy-done.11, bf16[640,256]{1,0:T(8,128)(2,1)S(1)} %copy-done.13, ...), custom_call_target="tpu_custom_call", output_to_operand_aliasing={{}: (18, {})} | custom-call | flops 409600 | bytes 409600 | tf_op jit(solution)/shard_map/block_step/pallas_call | solution.py:210
  (91 shorter events, 15.0 us)
Async XLA Ops:
  6.5 51.2 %all-gather.5.cloned.1.call-start = ((), (), s32[]{:S(2)}) async-start(), calls=%async_computation | async-start | bytes 1638400 | tf_op jit(solution)/shard_map/all_gather | solution.py:240
  9.2 94.0 %all-gather.7.cloned.1.call-start = ((), (), s32[]{:S(2)}) async-start(), calls=%async_computation.1 | async-start | bytes 1638400 | tf_op jit(solution)/shard_map/all_gather | solution.py:248
  9.2 11.1 %collective-permute-start = (bf16[640,256]{1,0:T(8,128)(2,1)}, bf16[640,256]{1,0:T(8,128)(2,1)S(1)}, u32[]{:S(2)}, u32[]{:S(2)}) collective-permute-start(bf16[640,256]{1,0:T(8,128)(2,1)} %join_shard.1), channel_id=1, source_target_pairs={{0,4},{1,5},{2,6},{3,7},{4,0},{5,1},{6,2},{7,3},{8,12},{9,13},{10,... | collective-permute-start | bytes 983048 | tf_op jit(solution)/shard_map/ppermute | solution.py:45
  10.9 16.9 %collective-permute-start.1 = (bf16[640,256]{1,0:T(8,128)(2,1)}, bf16[640,256]{1,0:T(8,128)(2,1)S(1)}, u32[]{:S(2)}, u32[]{:S(2)}) collective-permute-start(bf16[640,256]{1,0:T(8,128)(2,1)} %join_shard.1), channel_id=1, source_target_pairs={{0,0},{1,16},{2,32},{3,48},{4,8},{5,24},{6,40},{7,56},{8,160},{9,1... | collective-permute-start | bytes 983048 | tf_op jit(solution)/shard_map/ppermute | solution.py:45
  27.8 20.1 %collective-permute-start.2 = (bf16[640,256]{1,0:T(8,128)(2,1)S(1)}, bf16[640,256]{1,0:T(8,128)(2,1)S(1)}, u32[]{:S(2)}, u32[]{:S(2)}) collective-permute-start(bf16[640,256]{1,0:T(8,128)(2,1)S(1)} %collective-permute-done.1.refs_0_), channel_id=1, source_target_pairs={{0,16},{1,17},{2,18},{3,19},{4,20},{5,21},{6,22},{7,23},{8,56},{9,... | collective-permute-start | bytes 983048 | tf_op jit(solution)/shard_map/ppermute | solution.py:45
  30.3 17.6 %collective-permute-start.7 = (bf16[640,256]{1,0:T(8,128)(2,1)S(1)}, bf16[640,256]{1,0:T(8,128)(2,1)S(1)}, u32[]{:S(2)}, u32[]{:S(2)}) collective-permute-start(bf16[640,256]{1,0:T(8,128)(2,1)S(1)} %collective-permute-done.6.refs_1_), channel_id=1, source_target_pairs={{0,16},{1,17},{2,18},{3,19},{4,20},{5,21},{6,22},{7,23},{8,56},{9,... | collective-permute-start | bytes 983048 | tf_op jit(solution)/shard_map/ppermute | solution.py:45
  31.5 22.0 %collective-permute-start.3 = (bf16[640,256]{1,0:T(8,128)(2,1)S(1)}, bf16[640,256]{1,0:T(8,128)(2,1)S(1)}, u32[]{:S(2)}, u32[]{:S(2)}) collective-permute-start(bf16[640,256]{1,0:T(8,128)(2,1)S(1)} %collective-permute-done.1.refs_0_), channel_id=1, source_target_pairs={{0,64},{1,65},{2,66},{3,67},{4,68},{5,69},{6,70},{7,71},{8,200},{9... | collective-permute-start | bytes 983048 | tf_op jit(solution)/shard_map/ppermute | solution.py:45
  47.1 9.9 %collective-permute-start.14 = (bf16[640,256]{1,0:T(8,128)(2,1)S(1)}, bf16[640,256]{1,0:T(8,128)(2,1)S(1)}, u32[]{:S(2)}, u32[]{:S(2)}) collective-permute-start(bf16[640,256]{1,0:T(8,128)(2,1)S(1)} %collective-permute-done.6.refs_1_), channel_id=1, source_target_pairs={{0,64},{1,65},{2,66},{3,67},{4,68},{5,69},{6,70},{7,71},{8,200},{9... | collective-permute-start | bytes 983048 | tf_op jit(solution)/shard_map/ppermute | solution.py:45
  47.9 9.8 %collective-permute-start.10 = (bf16[640,256]{1,0:T(8,128)(2,1)S(1)}, bf16[640,256]{1,0:T(8,128)(2,1)}, u32[]{:S(2)}, u32[]{:S(2)}) collective-permute-start(bf16[640,256]{1,0:T(8,128)(2,1)S(1)} %collective-permute-done.2.refs_2_), channel_id=1, source_target_pairs={{0,16},{1,17},{2,18},{3,19},{4,20},{5,21},{6,22},{7,23},{8,56},{9,... | collective-permute-start | bytes 983048 | tf_op jit(solution)/shard_map/ppermute | solution.py:45
  59.5 14.5 %collective-permute-start.15 = (bf16[1280,256]{1,0:T(8,128)(2,1)}, bf16[1280,256]{1,0:T(8,128)(2,1)}, u32[]{:S(2)}, u32[]{:S(2)}) collective-permute-start(bf16[1280,256]{1,0:T(8,128)(2,1)} %constant_dynamic-update-slice_fusion.refs_0_), channel_id=1, source_target_pairs={{0,16},{1,17},{2,18},{3,19},{4,20},{5,21},{6,22},{7,23},{8,56},{9,... | collective-permute-start | bytes 1966088 | tf_op jit(solution)/shard_map/ppermute | solution.py:45
  60.9 15.9 %collective-permute-start.16 = (bf16[1280,256]{1,0:T(8,128)(2,1)}, bf16[1280,256]{1,0:T(8,128)(2,1)S(1)}, u32[]{:S(2)}, u32[]{:S(2)}) collective-permute-start(bf16[1280,256]{1,0:T(8,128)(2,1)} %constant_dynamic-update-slice_fusion.refs_0_), channel_id=1, source_target_pairs={{0,8},{1,9},{2,10},{3,11},{4,12},{5,13},{6,14},{7,15},{8,0},{9,1},... | collective-permute-start | bytes 1966088 | tf_op jit(solution)/shard_map/ppermute | solution.py:45
  61.9 11.3 %collective-permute-start.4 = (bf16[640,256]{1,0:T(8,128)(2,1)}, bf16[640,256]{1,0:T(8,128)(2,1)S(1)}, u32[]{:S(2)}, u32[]{:S(2)}) collective-permute-start(bf16[640,256]{1,0:T(8,128)(2,1)} %copy-done.23), channel_id=1, source_target_pairs={{0,64},{1,65},{2,66},{3,67},{4,68},{5,69},{6,70},{7,71},{8,200},{9... | collective-permute-start | bytes 983048 | tf_op jit(solution)/shard_map/ppermute | solution.py:45
  74.0 24.6 %collective-permute-start.19 = (bf16[1280,256]{1,0:T(8,128)(2,1)}, bf16[1280,256]{1,0:T(8,128)(2,1)}, u32[]{:S(2)}, u32[]{:S(2)}) collective-permute-start(bf16[1280,256]{1,0:T(8,128)(2,1)} %collective-permute-done.15.refs_1_), channel_id=1, source_target_pairs={{0,16},{1,17},{2,18},{3,19},{4,20},{5,21},{6,22},{7,23},{8,56},{9,... | collective-permute-start | bytes 1966088 | tf_op jit(solution)/shard_map/ppermute | solution.py:45
  76.8 23.2 %collective-permute-start.17 = (bf16[1280,256]{1,0:T(8,128)(2,1)S(1)}, bf16[1280,256]{1,0:T(8,128)(2,1)}, u32[]{:S(2)}, u32[]{:S(2)}) collective-permute-start(bf16[1280,256]{1,0:T(8,128)(2,1)S(1)} %collective-permute-done.16.refs_7_), channel_id=1, source_target_pairs={{0,16},{1,17},{2,18},{3,19},{4,20},{5,21},{6,22},{7,23},{8,56},{9,... | collective-permute-start | bytes 1966088 | tf_op jit(solution)/shard_map/ppermute | solution.py:45
  77.7 17.3 %collective-permute-start.12 = (bf16[640,256]{1,0:T(8,128)(2,1)S(1)}, bf16[640,256]{1,0:T(8,128)(2,1)}, u32[]{:S(2)}, u32[]{:S(2)}) collective-permute-start(bf16[640,256]{1,0:T(8,128)(2,1)S(1)} %collective-permute-done.4.refs_14_), channel_id=1, source_target_pairs={{0,16},{1,17},{2,18},{3,19},{4,20},{5,21},{6,22},{7,23},{8,56},{9,... | collective-permute-start | bytes 983048 | tf_op jit(solution)/shard_map/ppermute | solution.py:45
  78.6 20.0 %collective-permute-start.20 = (bf16[640,256]{1,0:T(8,128)(2,1)S(1)}, bf16[640,256]{1,0:T(8,128)(2,1)S(1)}, u32[]{:S(2)}, u32[]{:S(2)}) collective-permute-start(bf16[640,256]{1,0:T(8,128)(2,1)S(1)} %collective-permute-done.5.refs_15_), channel_id=1, source_target_pairs={{0,16},{1,17},{2,18},{3,19},{4,20},{5,21},{6,22},{7,23},{8,56},{9,... | collective-permute-start | bytes 983048 | tf_op jit(solution)/shard_map/ppermute | solution.py:45
  79.9 26.8 %collective-permute-start.22 = (bf16[1280,256]{1,0:T(8,128)(2,1)}, bf16[1280,256]{1,0:T(8,128)(2,1)}, u32[]{:S(2)}, u32[]{:S(2)}) collective-permute-start(bf16[1280,256]{1,0:T(8,128)(2,1)} %collective-permute-done.15.refs_1_), channel_id=1, source_target_pairs={{0,8},{1,9},{2,10},{3,11},{4,12},{5,13},{6,14},{7,15},{8,0},{9,1},... | collective-permute-start | bytes 1966088 | tf_op jit(solution)/shard_map/ppermute | solution.py:45
  98.6 8.7 %collective-permute-start.21 = (bf16[1280,256]{1,0:T(8,128)(2,1)}, bf16[1280,256]{1,0:T(8,128)(2,1)}, u32[]{:S(2)}, u32[]{:S(2)}) collective-permute-start(bf16[1280,256]{1,0:T(8,128)(2,1)} %collective-permute-done.19.refs_3_), channel_id=1, source_target_pairs={{0,8},{1,9},{2,10},{3,11},{4,12},{5,13},{6,14},{7,15},{8,0},{9,1},... | collective-permute-start | bytes 1966088 | tf_op jit(solution)/shard_map/ppermute | solution.py:45
  100.0 7.4 %collective-permute-start.18 = (bf16[1280,256]{1,0:T(8,128)(2,1)}, bf16[1280,256]{1,0:T(8,128)(2,1)}, u32[]{:S(2)}, u32[]{:S(2)}) collective-permute-start(bf16[1280,256]{1,0:T(8,128)(2,1)} %collective-permute-done.17.refs_6_), channel_id=1, source_target_pairs={{0,8},{1,9},{2,10},{3,11},{4,12},{5,13},{6,14},{7,15},{8,0},{9,1},... | collective-permute-start | bytes 1966088 | tf_op jit(solution)/shard_map/ppermute | solution.py:45
  100.8 14.2 %collective-permute-start.13 = (bf16[640,256]{1,0:T(8,128)(2,1)}, bf16[640,256]{1,0:T(8,128)(2,1)}, u32[]{:S(2)}, u32[]{:S(2)}) collective-permute-start(bf16[640,256]{1,0:T(8,128)(2,1)} %collective-permute-done.12.refs_12_), channel_id=1, source_target_pairs={{0,16},{1,17},{2,18},{3,19},{4,20},{5,21},{6,22},{7,23},{8,56},{9,... | collective-permute-start | bytes 983048 | tf_op jit(solution)/shard_map/ppermute | solution.py:45
  102.4 12.7 %collective-permute-start.9 = (bf16[640,256]{1,0:T(8,128)(2,1)}, bf16[640,256]{1,0:T(8,128)(2,1)}, u32[]{:S(2)}, u32[]{:S(2)}) collective-permute-start(bf16[640,256]{1,0:T(8,128)(2,1)} %copy-done.10), channel_id=1, source_target_pairs={{0,8},{1,9},{2,10},{3,11},{4,12},{5,13},{6,14},{7,15},{8,0},{9,1},... | collective-permute-start | bytes 983048 | tf_op jit(solution)/shard_map/ppermute | solution.py:45
  106.8 8.7 %collective-permute-start.8 = (bf16[640,256]{1,0:T(8,128)(2,1)S(1)}, bf16[640,256]{1,0:T(8,128)(2,1)S(1)}, u32[]{:S(2)}, u32[]{:S(2)}) collective-permute-start(bf16[640,256]{1,0:T(8,128)(2,1)S(1)} %copy-done.13), channel_id=1, source_target_pairs={{0,8},{1,9},{2,10},{3,11},{4,12},{5,13},{6,14},{7,15},{8,0},{9,1},... | collective-permute-start | bytes 983048 | tf_op jit(solution)/shard_map/ppermute | solution.py:45
  107.3 8.2 %collective-permute-start.11 = (bf16[640,256]{1,0:T(8,128)(2,1)}, bf16[640,256]{1,0:T(8,128)(2,1)S(1)}, u32[]{:S(2)}, u32[]{:S(2)}) collective-permute-start(bf16[640,256]{1,0:T(8,128)(2,1)} %collective-permute-done.10.refs_6_), channel_id=1, source_target_pairs={{0,8},{1,9},{2,10},{3,11},{4,12},{5,13},{6,14},{7,15},{8,0},{9,1},... | collective-permute-start | bytes 983048 | tf_op jit(solution)/shard_map/ppermute | solution.py:45
  107.4 8.1 %collective-permute-start.25 = (bf16[640,256]{1,0:T(8,128)(2,1)}, bf16[640,256]{1,0:T(8,128)(2,1)S(1)}, u32[]{:S(2)}, u32[]{:S(2)}) collective-permute-start(bf16[640,256]{1,0:T(8,128)(2,1)} %collective-permute-done.12.refs_12_), channel_id=1, source_target_pairs={{0,8},{1,9},{2,10},{3,11},{4,12},{5,13},{6,14},{7,15},{8,0},{9,1},... | collective-permute-start | bytes 983048 | tf_op jit(solution)/shard_map/ppermute | solution.py:45
  (29 other events, 170.0 us)
Sparse Core Ops, SparseCore 0:
  9.3 29.5 all-gather.4
  57.9 26.7 all-gather.6

commit v7 on v6

--- a/solution.py
+++ b/solution.py
@@ -25,9 +25,9 @@
     return ((((zh % ZH) * X + x % X) * CORE + core % CORE) * ZL + zl % ZL) * Y + y % Y
 
 
-def home(zh, x, core, zl, y):
+def home(zh, x, core, zl, y, step=0):
     group = zh * 2 + x // 2
-    return flat(zh + 2 * core + x % 2, y + 2 * core, zl, group // Y, group % Y)
+    return flat(zh + 2 * core + x % 2 + step, y + 2 * core + step, zl, group // Y, group % Y)
 
 
 def pairs(target):
@@ -35,6 +35,7 @@
 
 
 TO_HOME = pairs(home)
+TO_SECOND = pairs(lambda *device: home(*device, step=2))
 ALONG_Z = pairs(lambda zh, x, core, zl, y: flat(zh + 1 - 2 * core, x, core, zl, y))
 ALONG_X = pairs(lambda zh, x, core, zl, y: flat(zh, x + 1 - 2 * core, core, zl, y))
 OTHER_ZL = pairs(lambda zh, x, core, zl, y: flat(zh, x, core, zl + 1, y))
@@ -239,45 +240,44 @@
     alike_y = [[zl * Y + y for y in range(Y)] for zl in range(ZL)]
     own = lax.all_gather(shard, "col", axis_index_groups=alike_y)
 
-    p = send(shard, TO_HOME)
+    p, p2 = send(shard, TO_HOME), send(shard, TO_SECOND)
     other_zl = send(shard, OTHER_ZL)
-    p = after(p, other_zl)
+    p = jnp.concatenate([p, after(p2, other_zl)], 0)
     ps = other(p)
-    za, zb = send(p, ALONG_Z), send(ps, ALONG_Z)
     xp, xps = send(p, ALONG_X), send(ps, ALONG_X)
-    others = lax.all_gather(after(other_zl, own, xp), "col", axis_index_groups=alike_y)
-    fxp = send(after(xp, xps), ALONG_X)
-    z2 = send(za, ALONG_Z)
-    zz = jnp.concatenate([za, after(zb, xps, fxp)], 0)
+    fxp = send(xp, ALONG_X)
+    zz = after(send(p, ALONG_Z), xps)
+    others = lax.all_gather(after(other_zl, own, ps), "col", axis_index_groups=alike_y)
     zs = other(zz)
     xzz, xzs = send(zz, ALONG_X), send(zs, ALONG_X)
-    fxzz = send(after(xzz, z2), ALONG_X)
-    z2s = other(z2)
-    xz2, xz2s = send(z2, ALONG_X), send(z2s, ALONG_X)
-
-    left = left_panel_of(own, after(others, z2s), weights)
-
-    def singles(here, back, ahead, across):
-        return list(zip((*here, *back, *ahead, *across), [0] * 8, [HERE] * 2 + [BACK] * 2 + [AHEAD] * 2 + [ACROSS] * 2, [0, 1] * 4))
-
-    def pairs_of(arrays, first_core):
-        return [
-            (array, core ^ first_core, dx, core)
-            for array, dx in zip(arrays, (HERE, BACK, AHEAD, ACROSS))
-            for core in (0, 1)
-        ]
-
-    def turned(pieces):
-        return [piece for index in (3, 2, 1, 0) for piece in pieces[2 * index : 2 * index + 2]]
-
-    fxz2 = send(xz2, ALONG_X)
-    near = pairs_of([zz, xzz, other(xzs), fxzz], 0)
-    far = pairs_of([zs, xzs, other(xzz), other(after(fxzz, xz2, xz2s))], 1)
-    out = block_step([(BACK, near), (AHEAD, turned(far))], left, gamma, None)
-    their_fxz2 = other(after(fxz2, out))
-    same = singles((p, ps), (xp, xps), (other(xps), other(xp)), (fxp, other(fxp)))
-    last = singles((z2, z2s), (xz2, xz2s), (other(xz2s), other(xz2)), (fxz2, their_fxz2))
-    return block_step([(HERE, same), (ACROSS, turned(last))], left, gamma, out)
+    fxzz = send(xzz, ALONG_X)
+    left = left_panel_of(own, others, weights)
+
+    def places(entries, half):
+        return [(array, half ^ turn, (dx[0] + 2 * (half ^ turn), dx[1]), core) for array, turn, dx, core in entries]
+
+    alike = [
+        (p, 0, HERE, 0),
+        (ps, 0, HERE, 1),
+        (xp, 0, BACK, 0),
+        (xps, 0, BACK, 1),
+        (other(xp), 0, AHEAD, 1),
+        (other(xps), 0, AHEAD, 0),
+        (fxp, 0, ACROSS, 0),
+        (other(fxp), 0, ACROSS, 1),
+    ]
+    out = block_step([(HERE, places(alike, 0)), (ACROSS, places(alike, 1))], left, gamma, None)
+    between = [
+        (zz, 0, HERE, 0),
+        (zs, 1, HERE, 1),
+        (xzz, 0, BACK, 0),
+        (xzs, 1, BACK, 1),
+        (other(xzz), 1, AHEAD, 1),
+        (other(xzs), 0, AHEAD, 0),
+        (fxzz, 0, ACROSS, 0),
+        (other(after(fxzz, out)), 1, ACROSS, 1),
+    ]
+    return block_step([(BACK, places(between, 0)), (AHEAD, places(between, 1))], left, gamma, out)
 
 
 def solution(mesh):

time: 133 us -> 138 us (1.038); the launches traced: 131 us -> 138 us
  starting transfers between devices: 46.6 us -> 61.8 us
  local copies, waits for them, and re-layouts: 12.5 us -> 7.1 us
  waiting for transfers between devices: 42.2 us -> 38.6 us
    ppermute x26 -> x18, starting transfers between devices: 46.5 us -> 61.8 us  [send(): return lax.ppermute(value, AXES, way)]
    unnamed x51 -> x13, local copies, waits for them, and re-layouts: 10.7 us -> 5.23 us
    ppermute x26 -> x18, waiting for transfers between devices: 42.2 us -> 38.6 us  [send(): return lax.ppermute(value, AXES, way)]
  transfers between devices with their start and end apart: 28 -> 20, of which waited for: 8 -> 8; matrix products, arithmetic and copies ran while one was open for 2% -> 2% of each run, Pallas kernels for 6% -> 6%
where the time goes in v7:
time: 138 us
  starting transfers between devices  61.8 us (45%)
  waiting for transfers between devices  38.6 us (28%)
  Pallas kernels  15.9 us (12%)
  between operations  13.5 us (10%)
  local copies, waits for them, and re-layouts  7.1 us (5%)
    ppermute x18, starting transfers between devices, send(): return lax.ppermute(value, AXES, way)  61.8 us
    ppermute x18, waiting for transfers between devices, send(): return lax.ppermute(value, AXES, way)  38.6 us
    pallas_call x2, Pallas kernels, block_step(): pl.pallas_call(functools.partial(block_kernel, placed, len(arrays), heigh...  14.4 us
    unnamed x13, local copies, waits for them, and re-layouts  5.23 us
  transfers between devices with their start and end apart: 20, of which 8 were waited for; matrix products, arithmetic and copies ran while one was open for 2% of the time, Pallas kernels for 6%

profile of v7, /device:TPU:25, one launch (start us, length us, event | category | flops | bytes accessed | tf_op | source)
XLA Modules:
  0.0 137.6 jit_solution(18086638379952430270)
XLA Ops:
  6.5 0.9 copy-done.3
  7.5 0.9 copy-done.4
  9.2 1.7 %collective-permute-start = (bf16[640,256]{1,0:T(8,128)(2,1)}, bf16[640,256]{1,0:T(8,128)(2,1)}, u32[]{:S(2)}, u32[]{:S(2)}) collective-permute-start(bf16[640,256]{1,0:T(8,128)(2,1)} %join_shard.1), channel_id=1, source_target_pairs={{0,4},{1,5},{2,6},{3,7},{4,0},{5,1},{6,2},{7,3},{8,12},{9,13},{10,... | collective-permute-start | bytes 983048 | tf_op jit(solution)/shard_map/ppermute | solution.py:46
  10.9 4.9 %collective-permute-start.2 = (bf16[640,256]{1,0:T(8,128)(2,1)}, bf16[640,256]{1,0:T(8,128)(2,1)S(1)}, u32[]{:S(2)}, u32[]{:S(2)}) collective-permute-start(bf16[640,256]{1,0:T(8,128)(2,1)} %join_shard.1), channel_id=1, source_target_pairs={{0,160},{1,176},{2,128},{3,144},{4,168},{5,184},{6,136},{7,152},{8... | collective-permute-start | bytes 983048 | tf_op jit(solution)/shard_map/ppermute | solution.py:46
  15.8 6.5 %collective-permute-start.1 = (bf16[640,256]{1,0:T(8,128)(2,1)}, bf16[640,256]{1,0:T(8,128)(2,1)S(1)}, u32[]{:S(2)}, u32[]{:S(2)}) collective-permute-start(bf16[640,256]{1,0:T(8,128)(2,1)} %join_shard.1), channel_id=1, source_target_pairs={{0,0},{1,16},{2,32},{3,48},{4,8},{5,24},{6,40},{7,56},{8,160},{9,1... | collective-permute-start | bytes 983048 | tf_op jit(solution)/shard_map/ppermute | solution.py:46
  22.3 7.8 %collective-permute-done.2 = bf16[640,256]{1,0:T(8,128)(2,1)S(1)} collective-permute-done((bf16[640,256]{1,0:T(8,128)(2,1)}, bf16[640,256]{1,0:T(8,128)(2,1)S(1)}, u32[]{:S(2)}, u32[]{:S(2)}) %collective-permute-start.2) | collective-permute-done | bytes 327712 | tf_op jit(solution)/shard_map/ppermute | solution.py:46
  30.1 1.4 collective-permute-done.1
  32.2 1.9 %constant_dynamic-update-slice_fusion.refs_0_ = bf16[1280,256]{1,0:T(8,128)(2,1)} fusion(bf16[1280,256]{1,0:T(8,128)(2,1)} %constant_dynamic-update-slice_fusion.1, bf16[640,256]{1,0:T(8,128)(2,1)} %copy-done.5), kind=kLoop, calls=%fused_computation | loop fusion | bytes 655360 | tf_op jit(solution)/shard_map/concatenate | solution.py:245
  34.1 4.2 %collective-permute-start.3 = (bf16[1280,256]{1,0:T(8,128)(2,1)}, bf16[1280,256]{1,0:T(8,128)(2,1)}, u32[]{:S(2)}, u32[]{:S(2)}) collective-permute-start(bf16[1280,256]{1,0:T(8,128)(2,1)} %constant_dynamic-update-slice_fusion.refs_0_), channel_id=1, source_target_pairs={{0,8},{1,9},{2,10},{3,11},{4,12},{5,13},{6,14},{7,15},{8,0},{9,1},... | collective-permute-start | bytes 1966088 | tf_op jit(solution)/shard_map/ppermute | solution.py:46
  38.3 24.8 %collective-permute-start.4 = (bf16[1280,256]{1,0:T(8,128)(2,1)}, bf16[1280,256]{1,0:T(8,128)(2,1)}, u32[]{:S(2)}, u32[]{:S(2)}) collective-permute-start(bf16[1280,256]{1,0:T(8,128)(2,1)} %constant_dynamic-update-slice_fusion.refs_0_), channel_id=1, source_target_pairs={{0,64},{1,65},{2,66},{3,67},{4,68},{5,69},{6,70},{7,71},{8,200},{9... | collective-permute-start | bytes 1966088 | tf_op jit(solution)/shard_map/ppermute | solution.py:46
  63.1 9.9 %collective-permute-start.5 = (bf16[1280,256]{1,0:T(8,128)(2,1)}, bf16[1280,256]{1,0:T(8,128)(2,1)}, u32[]{:S(2)}, u32[]{:S(2)}) collective-permute-start(bf16[1280,256]{1,0:T(8,128)(2,1)} %collective-permute-done.3.refs_1_), channel_id=1, source_target_pairs={{0,16},{1,17},{2,18},{3,19},{4,20},{5,21},{6,22},{7,23},{8,56},{9,... | collective-permute-start | bytes 1966088 | tf_op jit(solution)/shard_map/ppermute | solution.py:46
  73.1 1.2 collective-permute-done.4.refs_0_
  74.3 6.6 %collective-permute-done.5.refs_3_ = bf16[1280,256]{1,0:T(8,128)(2,1)} collective-permute-done((bf16[1280,256]{1,0:T(8,128)(2,1)}, bf16[1280,256]{1,0:T(8,128)(2,1)}, u32[]{:S(2)}, u32[]{:S(2)}) %collective-permute-start.5) | collective-permute-done | bytes 655392 | tf_op jit(solution)/shard_map/ppermute | solution.py:46
  80.8 7.0 %collective-permute-done.12.refs_2_ = bf16[1280,256]{1,0:T(8,128)(2,1)} collective-permute-done((bf16[1280,256]{1,0:T(8,128)(2,1)}, bf16[1280,256]{1,0:T(8,128)(2,1)}, u32[]{:S(2)}, u32[]{:S(2)}) %collective-permute-start.12) | collective-permute-done | bytes 655392 | tf_op jit(solution)/shard_map/ppermute | solution.py:46
  87.8 3.4 %collective-permute-start.15 = (bf16[1280,256]{1,0:T(8,128)(2,1)}, bf16[1280,256]{1,0:T(8,128)(2,1)}, u32[]{:S(2)}, u32[]{:S(2)}) collective-permute-start(bf16[1280,256]{1,0:T(8,128)(2,1)} %collective-permute-done.12.refs_2_), channel_id=1, source_target_pairs={{0,16},{1,17},{2,18},{3,19},{4,20},{5,21},{6,22},{7,23},{8,56},{9,... | collective-permute-start | bytes 1966088 | tf_op jit(solution)/shard_map/ppermute | solution.py:46
  91.4 2.2 %collective-permute-start.14 = (bf16[1280,256]{1,0:T(8,128)(2,1)}, bf16[1280,256]{1,0:T(8,128)(2,1)}, u32[]{:S(2)}, u32[]{:S(2)}) collective-permute-start(bf16[1280,256]{1,0:T(8,128)(2,1)} %collective-permute-done.5.refs_3_), channel_id=1, source_target_pairs={{0,8},{1,9},{2,10},{3,11},{4,12},{5,13},{6,14},{7,15},{8,0},{9,1},... | collective-permute-start | bytes 1966088 | tf_op jit(solution)/shard_map/ppermute | solution.py:46
  93.5 5.6 %collective-permute-done.15.refs_6_ = bf16[1280,256]{1,0:T(8,128)(2,1)} collective-permute-done((bf16[1280,256]{1,0:T(8,128)(2,1)}, bf16[1280,256]{1,0:T(8,128)(2,1)}, u32[]{:S(2)}, u32[]{:S(2)}) %collective-permute-start.15) | collective-permute-done | bytes 655392 | tf_op jit(solution)/shard_map/ppermute | solution.py:46
  99.1 7.0 %collective-permute-done.7.refs_2_ = bf16[1280,256]{1,0:T(8,128)(2,1)} collective-permute-done((bf16[1280,256]{1,0:T(8,128)(2,1)}, bf16[1280,256]{1,0:T(8,128)(2,1)}, u32[]{:S(2)}, u32[]{:S(2)}) %collective-permute-start.7) | collective-permute-done | bytes 655392 | tf_op jit(solution)/shard_map/ppermute | solution.py:46
  106.1 3.1 %collective-permute-start.11 = (bf16[1280,256]{1,0:T(8,128)(2,1)}, bf16[1280,256]{1,0:T(8,128)(2,1)}, u32[]{:S(2)}, u32[]{:S(2)}) collective-permute-start(bf16[1280,256]{1,0:T(8,128)(2,1)} %collective-permute-done.7.refs_2_), channel_id=1, source_target_pairs={{0,16},{1,17},{2,18},{3,19},{4,20},{5,21},{6,22},{7,23},{8,56},{9,... | collective-permute-start | bytes 1966088 | tf_op jit(solution)/shard_map/ppermute | solution.py:46
  109.9 1.3 copy-done.1
  111.3 1.3 copy-done.2
  114.0 7.2 %block_step.2.refs_9_ = bf16[640,2560]{1,0:T(8,128)(2,1)} custom-call(bf16[8,640,256]{2,1,0:T(8,128)(2,1)S(1)} %weigh_left.1.left_ref, bf16[1280,256]{1,0:T(8,128)(2,1)} %constant_dynamic-update-slice_fusion.refs_0_, bf16[1280,256]{1,0:T(8,128)(2,1)} %collective-permute-done.3.refs_1_, bf16[1280,256]{1,0:T(8,128)(2,1)} %collective-permute-done.12.refs_2_, ...), custom_call_target="tpu_custom_call" | custom-call | flops 409600 | bytes 409600 | tf_op jit(solution)/shard_map/block_step/pallas_call | solution.py:211
  121.6 2.0 %collective-permute-done.17.refs_7_ = bf16[1280,256]{1,0:T(8,128)(2,1)S(1)} collective-permute-done((bf16[1280,256]{1,0:T(8,128)(2,1)}, bf16[1280,256]{1,0:T(8,128)(2,1)S(1)}, u32[]{:S(2)}, u32[]{:S(2)}) %collective-permute-start.17) | collective-permute-done | bytes 655392 | tf_op jit(solution)/shard_map/ppermute | solution.py:46
  123.6 7.2 %block_step.3 = bf16[640,2560]{1,0:T(8,128)(2,1)} custom-call(bf16[8,640,256]{2,1,0:T(8,128)(2,1)S(1)} %weigh_left.1.left_ref, bf16[1280,256]{1,0:T(8,128)(2,1)} %collective-permute-done.4.refs_0_, bf16[1280,256]{1,0:T(8,128)(2,1)} %collective-permute-done.6.refs_1_, ...), custom_call_target="tpu_custom_call", output_to_operand_aliasing={{}: (10, {})} | custom-call | flops 409600 | bytes 409600 | tf_op jit(solution)/shard_map/block_step/pallas_call | solution.py:211
  (37 shorter events, 4.2 us)
Async XLA Ops:
  6.5 56.5 %all-gather.5.cloned.1.call-start = ((), (), s32[]{:S(2)}) async-start(), calls=%async_computation | async-start | bytes 1638400 | tf_op jit(solution)/shard_map/all_gather | solution.py:241
  9.1 100.8 %all-gather.7.cloned.1.call-start = ((), (), s32[]{:S(2)}) async-start(), calls=%async_computation.1 | async-start | bytes 1638400 | tf_op jit(solution)/shard_map/all_gather | solution.py:250
  9.2 13.1 %collective-permute-start = (bf16[640,256]{1,0:T(8,128)(2,1)}, bf16[640,256]{1,0:T(8,128)(2,1)}, u32[]{:S(2)}, u32[]{:S(2)}) collective-permute-start(bf16[640,256]{1,0:T(8,128)(2,1)} %join_shard.1), channel_id=1, source_target_pairs={{0,4},{1,5},{2,6},{3,7},{4,0},{5,1},{6,2},{7,3},{8,12},{9,13},{10,... | collective-permute-start | bytes 983048 | tf_op jit(solution)/shard_map/ppermute | solution.py:46
  10.9 19.2 %collective-permute-start.2 = (bf16[640,256]{1,0:T(8,128)(2,1)}, bf16[640,256]{1,0:T(8,128)(2,1)S(1)}, u32[]{:S(2)}, u32[]{:S(2)}) collective-permute-start(bf16[640,256]{1,0:T(8,128)(2,1)} %join_shard.1), channel_id=1, source_target_pairs={{0,160},{1,176},{2,128},{3,144},{4,168},{5,184},{6,136},{7,152},{8... | collective-permute-start | bytes 983048 | tf_op jit(solution)/shard_map/ppermute | solution.py:46
  15.8 15.7 %collective-permute-start.1 = (bf16[640,256]{1,0:T(8,128)(2,1)}, bf16[640,256]{1,0:T(8,128)(2,1)S(1)}, u32[]{:S(2)}, u32[]{:S(2)}) collective-permute-start(bf16[640,256]{1,0:T(8,128)(2,1)} %join_shard.1), channel_id=1, source_target_pairs={{0,0},{1,16},{2,32},{3,48},{4,8},{5,24},{6,40},{7,56},{8,160},{9,1... | collective-permute-start | bytes 983048 | tf_op jit(solution)/shard_map/ppermute | solution.py:46
  30.1 1.4 copy-start.5
  32.2 81.8 %copy-start = (bf16[640,2560]{1,0:T(8,128)(2,1)S(1)}, bf16[640,2560]{1,0:T(8,128)(2,1)}, u32[]{:S(2)}) copy-start(bf16[640,2560]{1,0:T(8,128)(2,1)} %refs_8_.3) | copy-start | bytes 9830404
  34.1 29.0 %collective-permute-start.3 = (bf16[1280,256]{1,0:T(8,128)(2,1)}, bf16[1280,256]{1,0:T(8,128)(2,1)}, u32[]{:S(2)}, u32[]{:S(2)}) collective-permute-start(bf16[1280,256]{1,0:T(8,128)(2,1)} %constant_dynamic-update-slice_fusion.refs_0_), channel_id=1, source_target_pairs={{0,8},{1,9},{2,10},{3,11},{4,12},{5,13},{6,14},{7,15},{8,0},{9,1},... | collective-permute-start | bytes 1966088 | tf_op jit(solution)/shard_map/ppermute | solution.py:46
  38.3 36.0 %collective-permute-start.4 = (bf16[1280,256]{1,0:T(8,128)(2,1)}, bf16[1280,256]{1,0:T(8,128)(2,1)}, u32[]{:S(2)}, u32[]{:S(2)}) collective-permute-start(bf16[1280,256]{1,0:T(8,128)(2,1)} %constant_dynamic-update-slice_fusion.refs_0_), channel_id=1, source_target_pairs={{0,64},{1,65},{2,66},{3,67},{4,68},{5,69},{6,70},{7,71},{8,200},{9... | collective-permute-start | bytes 1966088 | tf_op jit(solution)/shard_map/ppermute | solution.py:46
  63.1 17.7 %collective-permute-start.5 = (bf16[1280,256]{1,0:T(8,128)(2,1)}, bf16[1280,256]{1,0:T(8,128)(2,1)}, u32[]{:S(2)}, u32[]{:S(2)}) collective-permute-start(bf16[1280,256]{1,0:T(8,128)(2,1)} %collective-permute-done.3.refs_1_), channel_id=1, source_target_pairs={{0,16},{1,17},{2,18},{3,19},{4,20},{5,21},{6,22},{7,23},{8,56},{9,... | collective-permute-start | bytes 1966088 | tf_op jit(solution)/shard_map/ppermute | solution.py:46
  73.0 14.9 %collective-permute-start.12 = (bf16[1280,256]{1,0:T(8,128)(2,1)}, bf16[1280,256]{1,0:T(8,128)(2,1)}, u32[]{:S(2)}, u32[]{:S(2)}) collective-permute-start(bf16[1280,256]{1,0:T(8,128)(2,1)} %constant_dynamic-update-slice_fusion.refs_0_), channel_id=1, source_target_pairs={{0,16},{1,17},{2,18},{3,19},{4,20},{5,21},{6,22},{7,23},{8,56},{9,... | collective-permute-start | bytes 1966088 | tf_op jit(solution)/shard_map/ppermute | solution.py:46
  80.8 10.5 %collective-permute-start.6 = (bf16[1280,256]{1,0:T(8,128)(2,1)}, bf16[1280,256]{1,0:T(8,128)(2,1)}, u32[]{:S(2)}, u32[]{:S(2)}) collective-permute-start(bf16[1280,256]{1,0:T(8,128)(2,1)} %collective-permute-done.4.refs_0_), channel_id=1, source_target_pairs={{0,8},{1,9},{2,10},{3,11},{4,12},{5,13},{6,14},{7,15},{8,0},{9,1},... | collective-permute-start | bytes 1966088 | tf_op jit(solution)/shard_map/ppermute | solution.py:46
  87.8 11.3 %collective-permute-start.15 = (bf16[1280,256]{1,0:T(8,128)(2,1)}, bf16[1280,256]{1,0:T(8,128)(2,1)}, u32[]{:S(2)}, u32[]{:S(2)}) collective-permute-start(bf16[1280,256]{1,0:T(8,128)(2,1)} %collective-permute-done.12.refs_2_), channel_id=1, source_target_pairs={{0,16},{1,17},{2,18},{3,19},{4,20},{5,21},{6,22},{7,23},{8,56},{9,... | collective-permute-start | bytes 1966088 | tf_op jit(solution)/shard_map/ppermute | solution.py:46
  91.3 14.9 %collective-permute-start.7 = (bf16[1280,256]{1,0:T(8,128)(2,1)}, bf16[1280,256]{1,0:T(8,128)(2,1)}, u32[]{:S(2)}, u32[]{:S(2)}) collective-permute-start(bf16[1280,256]{1,0:T(8,128)(2,1)} %collective-permute-done.4.refs_0_), channel_id=1, source_target_pairs={{0,16},{1,17},{2,18},{3,19},{4,20},{5,21},{6,22},{7,23},{8,56},{9,... | collective-permute-start | bytes 1966088 | tf_op jit(solution)/shard_map/ppermute | solution.py:46
  91.3 22.1 %collective-permute-start.13 = (bf16[1280,256]{1,0:T(8,128)(2,1)}, bf16[1280,256]{1,0:T(8,128)(2,1)}, u32[]{:S(2)}, u32[]{:S(2)}) collective-permute-start(bf16[1280,256]{1,0:T(8,128)(2,1)} %collective-permute-done.12.refs_2_), channel_id=1, source_target_pairs={{0,8},{1,9},{2,10},{3,11},{4,12},{5,13},{6,14},{7,15},{8,0},{9,1},... | collective-permute-start | bytes 1966088 | tf_op jit(solution)/shard_map/ppermute | solution.py:46
  91.3 22.2 %collective-permute-start.8 = (bf16[1280,256]{1,0:T(8,128)(2,1)}, bf16[1280,256]{1,0:T(8,128)(2,1)}, u32[]{:S(2)}, u32[]{:S(2)}) collective-permute-start(bf16[1280,256]{1,0:T(8,128)(2,1)} %collective-permute-done.6.refs_1_), channel_id=1, source_target_pairs={{0,16},{1,17},{2,18},{3,19},{4,20},{5,21},{6,22},{7,23},{8,56},{9,... | collective-permute-start | bytes 1966088 | tf_op jit(solution)/shard_map/ppermute | solution.py:46
  91.4 22.6 %collective-permute-start.14 = (bf16[1280,256]{1,0:T(8,128)(2,1)}, bf16[1280,256]{1,0:T(8,128)(2,1)}, u32[]{:S(2)}, u32[]{:S(2)}) collective-permute-start(bf16[1280,256]{1,0:T(8,128)(2,1)} %collective-permute-done.5.refs_3_), channel_id=1, source_target_pairs={{0,8},{1,9},{2,10},{3,11},{4,12},{5,13},{6,14},{7,15},{8,0},{9,1},... | collective-permute-start | bytes 1966088 | tf_op jit(solution)/shard_map/ppermute | solution.py:46
  99.1 14.9 %collective-permute-start.16 = (bf16[1280,256]{1,0:T(8,128)(2,1)}, bf16[1280,256]{1,0:T(8,128)(2,1)}, u32[]{:S(2)}, u32[]{:S(2)}) collective-permute-start(bf16[1280,256]{1,0:T(8,128)(2,1)} %collective-permute-done.15.refs_6_), channel_id=1, source_target_pairs={{0,8},{1,9},{2,10},{3,11},{4,12},{5,13},{6,14},{7,15},{8,0},{9,1},... | collective-permute-start | bytes 1966088 | tf_op jit(solution)/shard_map/ppermute | solution.py:46
  106.1 15.1 %collective-permute-start.11 = (bf16[1280,256]{1,0:T(8,128)(2,1)}, bf16[1280,256]{1,0:T(8,128)(2,1)}, u32[]{:S(2)}, u32[]{:S(2)}) collective-permute-start(bf16[1280,256]{1,0:T(8,128)(2,1)} %collective-permute-done.7.refs_2_), channel_id=1, source_target_pairs={{0,16},{1,17},{2,18},{3,19},{4,20},{5,21},{6,22},{7,23},{8,56},{9,... | collective-permute-start | bytes 1966088 | tf_op jit(solution)/shard_map/ppermute | solution.py:46
  109.9 1.3 copy-start.1
  111.3 1.3 copy-start.2
  113.4 8.2 %collective-permute-start.9 = (bf16[1280,256]{1,0:T(8,128)(2,1)}, bf16[1280,256]{1,0:T(8,128)(2,1)S(1)}, u32[]{:S(2)}, u32[]{:S(2)}) collective-permute-start(bf16[1280,256]{1,0:T(8,128)(2,1)} %collective-permute-done.7.refs_2_), channel_id=1, source_target_pairs={{0,8},{1,9},{2,10},{3,11},{4,12},{5,13},{6,14},{7,15},{8,0},{9,1},... | collective-permute-start | bytes 1966088 | tf_op jit(solution)/shard_map/ppermute | solution.py:46
  113.5 8.1 %collective-permute-start.10 = (bf16[1280,256]{1,0:T(8,128)(2,1)}, bf16[1280,256]{1,0:T(8,128)(2,1)S(1)}, u32[]{:S(2)}, u32[]{:S(2)}) collective-permute-start(bf16[1280,256]{1,0:T(8,128)(2,1)} %collective-permute-done.8.refs_3_), channel_id=1, source_target_pairs={{0,8},{1,9},{2,10},{3,11},{4,12},{5,13},{6,14},{7,15},{8,0},{9,1},... | collective-permute-start | bytes 1966088 | tf_op jit(solution)/shard_map/ppermute | solution.py:46
  121.2 2.4 %collective-permute-start.17 = (bf16[1280,256]{1,0:T(8,128)(2,1)}, bf16[1280,256]{1,0:T(8,128)(2,1)S(1)}, u32[]{:S(2)}, u32[]{:S(2)}) collective-permute-start(bf16[1280,256]{1,0:T(8,128)(2,1)} %collective-permute-done.11.refs_6_), channel_id=1, source_target_pairs={{0,8},{1,9},{2,10},{3,11},{4,12},{5,13},{6,14},{7,15},{8,0},{9,1},... | collective-permute-start | bytes 1966088 | tf_op jit(solution)/shard_map/ppermute | solution.py:46
  (2 other events, 1.8 us)
Sparse Core Ops, SparseCore 0:
  9.3 36.7 all-gather.4
  63.2 30.9 all-gather.6

commit v8 on v4

--- a/solution.py
+++ b/solution.py
@@ -194,19 +194,20 @@
     height = shard.shape[0]
     alike_y = [[zl * Y + y for y in range(Y)] for zl in range(ZL)]
     own = lax.all_gather(shard, "col", axis_index_groups=alike_y)
+
     other_zl = send(shard, OTHER_ZL)
-
-    p = send(shard, TO_HOME)
+    p = after(send(shard, TO_HOME), other_zl)
+    others = lax.all_gather(after(other_zl, p), "col", axis_index_groups=alike_y)
     ps = other(p)
     xp, xps = send(p, ALONG_X), send(ps, ALONG_X)
-    others = lax.all_gather(after(other_zl, own, xps), "col", axis_index_groups=alike_y)
     zz = send(jnp.concatenate([p, ps], 0), ALONG_Z)
-    fxp = send(xp, ALONG_X)
+    fxp = send(after(xp, own), ALONG_X)
+    their = [other(xp), other(xps), other(fxp)]
     zz = after(zz, xps, fxp)
     zs = other(zz)
     z2 = send(zz[:height], ALONG_Z)
     xzz, xzs = send(zz, ALONG_X), send(zs, ALONG_X)
-    z2 = after(z2, xzz)
+    z2 = after(z2, xzz, *their)
     z2s = other(z2)
     fxzz = send(xzz, ALONG_X)
     xz2, xz2s = send(z2, ALONG_X), send(z2s, ALONG_X)
@@ -232,11 +233,11 @@
             (their_fx, 0, ACROSS, 1),
         ]
 
-    out = block_step(HERE, alike(p, ps, xp, xps, other(xp), other(xps), fxp, other(fxp)), left, gamma, None)
-    their_fxzz = other(after(fxzz, out))
+    out = block_step(HERE, alike(p, ps, xp, xps, their[0], their[1], fxp, their[2]), left, gamma, None)
+    their_fxzz = other(after(fxzz, out, xz2, xz2s))
     out = block_step(BACK, both([zz, xzz, other(xzs), fxzz], 0), left, gamma, out)
     fxz2 = send(after(xz2, out), ALONG_X)
-    out = block_step(AHEAD, both([after(zs, xz2s), xzs, other(xzz), their_fxzz], 1), left, gamma, out)
+    out = block_step(AHEAD, both([zs, xzs, other(xzz), their_fxzz], 1), left, gamma, out)
     their_fx = other(after(fxz2, out))
     return block_step(ACROSS, alike(z2, z2s, xz2, xz2s, other(xz2), other(xz2s), fxz2, their_fx), left, gamma, out)
 

time: 119 us -> 120 us (level)
  local copies, waits for them, and re-layouts: 5.32 us -> 8.2 us
  waiting for transfers between devices: 29.8 us -> 27.4 us
  Pallas kernels: 17.7 us -> 19.7 us
  starting transfers between devices: 50.8 us -> 49.5 us
    unnamed x30 -> x34, local copies, waits for them, and re-layouts: 5.3 us -> 8.18 us
    ppermute x25, waiting for transfers between devices: 29.8 us -> 27.3 us  [send(): return lax.ppermute(value, AXES, way)]
    pallas_call x4, Pallas kernels: 16.1 us -> 18.2 us  [block_step(): pl.pallas_call(functools.partial(block_kernel, dz, places, len(arrays), h...]
    ppermute x25, starting transfers between devices: 50.7 us -> 49.5 us  [send(): return lax.ppermute(value, AXES, way)]
where the time goes in v8:
time: 120 us; the launch traced here: 119 us
  starting transfers between devices  49.5 us (41%)
  waiting for transfers between devices  27.4 us (23%)
  Pallas kernels  19.7 us (16%)
  between operations  13.6 us (11%)
  local copies, waits for them, and re-layouts  8.2 us (7%)
    ppermute x25, starting transfers between devices, send(): return lax.ppermute(value, AXES, way)  49.5 us
    ppermute x25, waiting for transfers between devices, send(): return lax.ppermute(value, AXES, way)  27.3 us
    pallas_call x4, Pallas kernels, block_step(): pl.pallas_call(functools.partial(block_kernel, dz, places, len(arrays), h...  18.2 us
    unnamed x34, local copies, waits for them, and re-layouts  8.18 us
  transfers between devices with their start and end apart: 27, of which 7 were waited for; matrix products, arithmetic and copies ran while one was open for 0% of the time, Pallas kernels for 12%

profile of v8, /device:TPU:25, one launch (start us, length us, event | category | flops | bytes accessed | tf_op | source)
XLA Modules:
  0.0 118.5 jit_solution(9203734807065516267)
XLA Ops:
  9.2 1.7 %collective-permute-start = (bf16[640,256]{1,0:T(8,128)(2,1)}, bf16[640,256]{1,0:T(8,128)(2,1)S(1)}, u32[]{:S(2)}, u32[]{:S(2)}) collective-permute-start(bf16[640,256]{1,0:T(8,128)(2,1)} %join_shard.1), channel_id=1, source_target_pairs={{0,4},{1,5},{2,6},{3,7},{4,0},{5,1},{6,2},{7,3},{8,12},{9,13},{10,... | collective-permute-start | bytes 983048 | tf_op jit(solution)/shard_map/ppermute | solution.py:45
  10.9 9.3 %collective-permute-start.1 = (bf16[640,256]{1,0:T(8,128)(2,1)}, bf16[640,256]{1,0:T(8,128)(2,1)S(1)}, u32[]{:S(2)}, u32[]{:S(2)}) collective-permute-start(bf16[640,256]{1,0:T(8,128)(2,1)} %join_shard.1), channel_id=1, source_target_pairs={{0,0},{1,16},{2,32},{3,48},{4,8},{5,24},{6,40},{7,56},{8,160},{9,1... | collective-permute-start | bytes 983048 | tf_op jit(solution)/shard_map/ppermute | solution.py:45
  20.3 7.5 %collective-permute-done.1.refs_0_ = bf16[640,256]{1,0:T(8,128)(2,1)S(1)} collective-permute-done((bf16[640,256]{1,0:T(8,128)(2,1)}, bf16[640,256]{1,0:T(8,128)(2,1)S(1)}, u32[]{:S(2)}, u32[]{:S(2)}) %collective-permute-start.1) | collective-permute-done | bytes 327712 | tf_op jit(solution)/shard_map/ppermute | solution.py:45
  27.8 2.4 %collective-permute-start.5 = (bf16[640,256]{1,0:T(8,128)(2,1)S(1)}, bf16[640,256]{1,0:T(8,128)(2,1)S(1)}, u32[]{:S(2)}, u32[]{:S(2)}) collective-permute-start(bf16[640,256]{1,0:T(8,128)(2,1)S(1)} %collective-permute-done.1.refs_0_), channel_id=1, source_target_pairs={{0,16},{1,17},{2,18},{3,19},{4,20},{5,21},{6,22},{7,23},{8,56},{9,... | collective-permute-start | bytes 983048 | tf_op jit(solution)/shard_map/ppermute | solution.py:45
  30.3 14.6 %collective-permute-start.3 = (bf16[1280,256]{1,0:T(8,128)(2,1)S(1)}, bf16[1280,256]{1,0:T(8,128)(2,1)S(1)}, u32[]{:S(2)}, u32[]{:S(2)}) collective-permute-start(bf16[1280,256]{1,0:T(8,128)(2,1)S(1)} %pad_maximum_fusion), channel_id=1, source_target_pairs={{0,64},{1,65},{2,66},{3,67},{4,68},{5,69},{6,70},{7,71},{8,200},{9... | collective-permute-start | bytes 1966088 | tf_op jit(solution)/shard_map/ppermute | solution.py:45
  44.9 1.7 %collective-permute-start.4 = (bf16[640,256]{1,0:T(8,128)(2,1)S(1)}, bf16[640,256]{1,0:T(8,128)(2,1)}, u32[]{:S(2)}, u32[]{:S(2)}) collective-permute-start(bf16[640,256]{1,0:T(8,128)(2,1)S(1)} %collective-permute-done.2.refs_1_), channel_id=1, source_target_pairs={{0,16},{1,17},{2,18},{3,19},{4,20},{5,21},{6,22},{7,23},{8,56},{9,... | collective-permute-start | bytes 983048 | tf_op jit(solution)/shard_map/ppermute | solution.py:45
  46.8 4.5 %collective-permute-done.4.refs_3_ = bf16[640,256]{1,0:T(8,128)(2,1)} collective-permute-done((bf16[640,256]{1,0:T(8,128)(2,1)S(1)}, bf16[640,256]{1,0:T(8,128)(2,1)}, u32[]{:S(2)}, u32[]{:S(2)}) %collective-permute-start.4) | collective-permute-done | bytes 327712 | tf_op jit(solution)/shard_map/ppermute | solution.py:45
  51.2 7.0 %collective-permute-done.3.refs_0_ = bf16[1280,256]{1,0:T(8,128)(2,1)S(1)} collective-permute-done((bf16[1280,256]{1,0:T(8,128)(2,1)S(1)}, bf16[1280,256]{1,0:T(8,128)(2,1)S(1)}, u32[]{:S(2)}, u32[]{:S(2)}) %collective-permute-start.3) | collective-permute-done | bytes 655392 | tf_op jit(solution)/shard_map/ppermute | solution.py:45
  58.7 1.6 %collective-permute-start.8 = (bf16[1280,256]{1,0:T(8,128)(2,1)S(1)}, bf16[1280,256]{1,0:T(8,128)(2,1)S(1)}, u32[]{:S(2)}, u32[]{:S(2)}) collective-permute-start(bf16[1280,256]{1,0:T(8,128)(2,1)S(1)} %collective-permute-done.3.refs_0_), channel_id=1, source_target_pairs={{0,16},{1,17},{2,18},{3,19},{4,20},{5,21},{6,22},{7,23},{8,56},{9,... | collective-permute-start | bytes 1966088 | tf_op jit(solution)/shard_map/ppermute | solution.py:45
  60.3 5.0 %collective-permute-start.7 = (bf16[640,256]{1,0:T(8,128)(2,1)S(1)}, bf16[640,256]{1,0:T(8,128)(2,1)}, u32[]{:S(2)}, u32[]{:S(2)}) collective-permute-start(bf16[640,256]{1,0:T(8,128)(2,1)S(1)} %slice.3), channel_id=1, source_target_pairs={{0,64},{1,65},{2,66},{3,67},{4,68},{5,69},{6,70},{7,71},{8,200},{9... | collective-permute-start | bytes 983048 | tf_op jit(solution)/shard_map/ppermute | solution.py:45
  67.8 3.6 %collective-permute-done.7.refs_0_ = bf16[640,256]{1,0:T(8,128)(2,1)} collective-permute-done((bf16[640,256]{1,0:T(8,128)(2,1)S(1)}, bf16[640,256]{1,0:T(8,128)(2,1)}, u32[]{:S(2)}, u32[]{:S(2)}) %collective-permute-start.7) | collective-permute-done | bytes 327712 | tf_op jit(solution)/shard_map/ppermute | solution.py:45
  72.6 1.6 %collective-permute-start.20 = (bf16[1280,256]{1,0:T(8,128)(2,1)S(1)}, bf16[1280,256]{1,0:T(8,128)(2,1)}, u32[]{:S(2)}, u32[]{:S(2)}) collective-permute-start(bf16[1280,256]{1,0:T(8,128)(2,1)S(1)} %collective-permute-done.8.refs_1_), channel_id=1, source_target_pairs={{0,16},{1,17},{2,18},{3,19},{4,20},{5,21},{6,22},{7,23},{8,56},{9,... | collective-permute-start | bytes 1966088 | tf_op jit(solution)/shard_map/ppermute | solution.py:45
  74.5 1.3 %collective-permute-start.14 = (bf16[640,256]{1,0:T(8,128)(2,1)}, bf16[640,256]{1,0:T(8,128)(2,1)}, u32[]{:S(2)}, u32[]{:S(2)}) collective-permute-start(bf16[640,256]{1,0:T(8,128)(2,1)} %collective-permute-done.12.refs_1_), channel_id=1, source_target_pairs={{0,16},{1,17},{2,18},{3,19},{4,20},{5,21},{6,22},{7,23},{8,56},{9,... | collective-permute-start | bytes 983048 | tf_op jit(solution)/shard_map/ppermute | solution.py:45
  75.9 2.5 %collective-permute-start.19 = (bf16[1280,256]{1,0:T(8,128)(2,1)S(1)}, bf16[1280,256]{1,0:T(8,128)(2,1)}, u32[]{:S(2)}, u32[]{:S(2)}) collective-permute-start(bf16[1280,256]{1,0:T(8,128)(2,1)S(1)} %collective-permute-done.18.refs_1_), channel_id=1, source_target_pairs={{0,8},{1,9},{2,10},{3,11},{4,12},{5,13},{6,14},{7,15},{8,0},{9,1},... | collective-permute-start | bytes 1966088 | tf_op jit(solution)/shard_map/ppermute | solution.py:45
  78.5 1.3 %copy-done.1 = bf16[2560,256]{1,0:T(8,128)(2,1)S(1)} copy-done((bf16[2560,256]{1,0:T(8,128)(2,1)S(1)}, bf16[2560,256]{1,0:T(8,128)(2,1)}, u32[]{:S(2)}) %copy-start.1) | copy-done | bytes 1310744
  79.8 1.3 %copy-done.2 = bf16[2560,256]{1,0:T(8,128)(2,1)S(1)} copy-done((bf16[2560,256]{1,0:T(8,128)(2,1)S(1)}, bf16[2560,256]{1,0:T(8,128)(2,1)}, u32[]{:S(2)}) %copy-start.2) | copy-done | bytes 1310744
  83.4 4.4 %block_step.4.refs_5_ = bf16[640,2560]{1,0:T(8,128)(2,1)} custom-call(bf16[8,640,256]{2,1,0:T(8,128)(2,1)S(1)} %weigh_left.1.left_ref, bf16[640,256]{1,0:T(8,128)(2,1)S(1)} %collective-permute-done.1.refs_0_, bf16[640,256]{1,0:T(8,128)(2,1)S(1)} %collective-permute-done.2.refs_1_, bf16[640,256]{1,0:T(8,128)(2,1)S(1)} %copy-done.4, ...), custom_call_target="tpu_custom_call" | custom-call | flops 409600 | bytes 409600 | tf_op jit(solution)/shard_map/block_step/pallas_call | solution.py:166
  87.8 2.1 %collective-permute-done.14.refs_3_ = bf16[640,256]{1,0:T(8,128)(2,1)} collective-permute-done((bf16[640,256]{1,0:T(8,128)(2,1)}, bf16[640,256]{1,0:T(8,128)(2,1)}, u32[]{:S(2)}, u32[]{:S(2)}) %collective-permute-start.14) | collective-permute-done | bytes 327712 | tf_op jit(solution)/shard_map/ppermute | solution.py:45
  90.0 2.5 %collective-permute-start.23 = (bf16[1280,256]{1,0:T(8,128)(2,1)}, bf16[1280,256]{1,0:T(8,128)(2,1)S(1)}, u32[]{:S(2)}, u32[]{:S(2)}) collective-permute-start(bf16[1280,256]{1,0:T(8,128)(2,1)} %collective-permute-done.20.refs_3_), channel_id=1, source_target_pairs={{0,8},{1,9},{2,10},{3,11},{4,12},{5,13},{6,14},{7,15},{8,0},{9,1},... | collective-permute-start | bytes 1966088 | tf_op jit(solution)/shard_map/ppermute | solution.py:45
  92.5 4.7 %block_step.5.refs_5_ = bf16[640,2560]{1,0:T(8,128)(2,1)} custom-call(bf16[8,640,256]{2,1,0:T(8,128)(2,1)S(1)} %weigh_left.1.left_ref, bf16[1280,256]{1,0:T(8,128)(2,1)S(1)} %collective-permute-done.3.refs_0_, bf16[1280,256]{1,0:T(8,128)(2,1)S(1)} %collective-permute-done.8.refs_1_, ...), custom_call_target="tpu_custom_call", output_to_operand_aliasing={{}: (6, {})} | custom-call | flops 409600 | bytes 409600 | tf_op jit(solution)/shard_map/block_step/pallas_call | solution.py:166
  97.9 4.5 %block_step.6.refs_9_ = bf16[640,2560]{1,0:T(8,128)(2,1)} custom-call(bf16[8,640,256]{2,1,0:T(8,128)(2,1)S(1)} %weigh_left.1.left_ref, bf16[1280,256]{1,0:T(8,128)(2,1)S(1)} %collective-permute-done.17.refs_0_, bf16[1280,256]{1,0:T(8,128)(2,1)S(1)} %collective-permute-done.18.refs_1_, ...), custom_call_target="tpu_custom_call", output_to_operand_aliasing={{}: (6, {})} | custom-call | flops 409600 | bytes 409600 | tf_op jit(solution)/shard_map/block_step/pallas_call | solution.py:166
  102.3 1.3 %collective-permute-done.21.refs_6_ = bf16[640,256]{1,0:T(8,128)(2,1)S(1)} collective-permute-done((bf16[640,256]{1,0:T(8,128)(2,1)}, bf16[640,256]{1,0:T(8,128)(2,1)S(1)}, u32[]{:S(2)}, u32[]{:S(2)}) %collective-permute-start.21) | collective-permute-done | bytes 327712 | tf_op jit(solution)/shard_map/ppermute | solution.py:45
  103.7 2.1 %collective-permute-start.24 = (bf16[640,256]{1,0:T(8,128)(2,1)S(1)}, bf16[640,256]{1,0:T(8,128)(2,1)S(1)}, u32[]{:S(2)}, u32[]{:S(2)}) collective-permute-start(bf16[640,256]{1,0:T(8,128)(2,1)S(1)} %collective-permute-done.21.refs_6_), channel_id=1, source_target_pairs={{0,8},{1,9},{2,10},{3,11},{4,12},{5,13},{6,14},{7,15},{8,0},{9,1},... | collective-permute-start | bytes 983048 | tf_op jit(solution)/shard_map/ppermute | solution.py:45
  107.0 4.7 %block_step.7 = bf16[640,2560]{1,0:T(8,128)(2,1)} custom-call(bf16[8,640,256]{2,1,0:T(8,128)(2,1)S(1)} %weigh_left.1.left_ref, bf16[640,256]{1,0:T(8,128)(2,1)} %collective-permute-done.7.refs_0_, bf16[640,256]{1,0:T(8,128)(2,1)} %collective-permute-done.12.refs_1_, ...), custom_call_target="tpu_custom_call", output_to_operand_aliasing={{}: (10, {})} | custom-call | flops 409600 | bytes 409600 | tf_op jit(solution)/shard_map/block_step/pallas_call | solution.py:166
  (75 shorter events, 11.8 us)
Async XLA Ops:
  6.5 40.1 %all-gather.5.cloned.1.call-start = ((), (), s32[]{:S(2)}) async-start(), calls=%async_computation | async-start | bytes 1638400 | tf_op jit(solution)/shard_map/all_gather | solution.py:196
  9.1 69.3 %all-gather.7.cloned.1.call-start = ((), (), s32[]{:S(2)}) async-start(), calls=%async_computation.1 | async-start | bytes 1638400 | tf_op jit(solution)/shard_map/all_gather | solution.py:200
  9.2 11.1 %collective-permute-start = (bf16[640,256]{1,0:T(8,128)(2,1)}, bf16[640,256]{1,0:T(8,128)(2,1)S(1)}, u32[]{:S(2)}, u32[]{:S(2)}) collective-permute-start(bf16[640,256]{1,0:T(8,128)(2,1)} %join_shard.1), channel_id=1, source_target_pairs={{0,4},{1,5},{2,6},{3,7},{4,0},{5,1},{6,2},{7,3},{8,12},{9,13},{10,... | collective-permute-start | bytes 983048 | tf_op jit(solution)/shard_map/ppermute | solution.py:45
  10.9 16.9 %collective-permute-start.1 = (bf16[640,256]{1,0:T(8,128)(2,1)}, bf16[640,256]{1,0:T(8,128)(2,1)S(1)}, u32[]{:S(2)}, u32[]{:S(2)}) collective-permute-start(bf16[640,256]{1,0:T(8,128)(2,1)} %join_shard.1), channel_id=1, source_target_pairs={{0,0},{1,16},{2,32},{3,48},{4,8},{5,24},{6,40},{7,56},{8,160},{9,1... | collective-permute-start | bytes 983048 | tf_op jit(solution)/shard_map/ppermute | solution.py:45
  27.8 18.8 %collective-permute-start.5 = (bf16[640,256]{1,0:T(8,128)(2,1)S(1)}, bf16[640,256]{1,0:T(8,128)(2,1)S(1)}, u32[]{:S(2)}, u32[]{:S(2)}) collective-permute-start(bf16[640,256]{1,0:T(8,128)(2,1)S(1)} %collective-permute-done.1.refs_0_), channel_id=1, source_target_pairs={{0,16},{1,17},{2,18},{3,19},{4,20},{5,21},{6,22},{7,23},{8,56},{9,... | collective-permute-start | bytes 983048 | tf_op jit(solution)/shard_map/ppermute | solution.py:45
  30.3 27.9 %collective-permute-start.3 = (bf16[1280,256]{1,0:T(8,128)(2,1)S(1)}, bf16[1280,256]{1,0:T(8,128)(2,1)S(1)}, u32[]{:S(2)}, u32[]{:S(2)}) collective-permute-start(bf16[1280,256]{1,0:T(8,128)(2,1)S(1)} %pad_maximum_fusion), channel_id=1, source_target_pairs={{0,64},{1,65},{2,66},{3,67},{4,68},{5,69},{6,70},{7,71},{8,200},{9... | collective-permute-start | bytes 1966088 | tf_op jit(solution)/shard_map/ppermute | solution.py:45
  44.9 6.3 %collective-permute-start.4 = (bf16[640,256]{1,0:T(8,128)(2,1)S(1)}, bf16[640,256]{1,0:T(8,128)(2,1)}, u32[]{:S(2)}, u32[]{:S(2)}) collective-permute-start(bf16[640,256]{1,0:T(8,128)(2,1)S(1)} %collective-permute-done.2.refs_1_), channel_id=1, source_target_pairs={{0,16},{1,17},{2,18},{3,19},{4,20},{5,21},{6,22},{7,23},{8,56},{9,... | collective-permute-start | bytes 983048 | tf_op jit(solution)/shard_map/ppermute | solution.py:45
  46.6 11.6 %collective-permute-start.6 = (bf16[640,256]{1,0:T(8,128)(2,1)S(1)}, bf16[640,256]{1,0:T(8,128)(2,1)S(1)}, u32[]{:S(2)}, u32[]{:S(2)}) collective-permute-start(bf16[640,256]{1,0:T(8,128)(2,1)S(1)} %collective-permute-done.5.refs_2_), channel_id=1, source_target_pairs={{0,16},{1,17},{2,18},{3,19},{4,20},{5,21},{6,22},{7,23},{8,56},{9,... | collective-permute-start | bytes 983048 | tf_op jit(solution)/shard_map/ppermute | solution.py:45
  58.2 7.8 %collective-permute-start.17 = (bf16[1280,256]{1,0:T(8,128)(2,1)S(1)}, bf16[1280,256]{1,0:T(8,128)(2,1)S(1)}, u32[]{:S(2)}, u32[]{:S(2)}) collective-permute-start(bf16[1280,256]{1,0:T(8,128)(2,1)S(1)} %collective-permute-done.3.refs_0_), channel_id=1, source_target_pairs={{0,8},{1,9},{2,10},{3,11},{4,12},{5,13},{6,14},{7,15},{8,0},{9,1},... | collective-permute-start | bytes 1966088 | tf_op jit(solution)/shard_map/ppermute | solution.py:45
  58.6 6.6 %collective-permute-start.9 = (bf16[640,256]{1,0:T(8,128)(2,1)S(1)}, bf16[640,256]{1,0:T(8,128)(2,1)S(1)}, u32[]{:S(2)}, u32[]{:S(2)}) collective-permute-start(bf16[640,256]{1,0:T(8,128)(2,1)S(1)} %collective-permute-done.5.refs_2_), channel_id=1, source_target_pairs={{0,8},{1,9},{2,10},{3,11},{4,12},{5,13},{6,14},{7,15},{8,0},{9,1},... | collective-permute-start | bytes 983048 | tf_op jit(solution)/shard_map/ppermute | solution.py:45
  58.7 13.4 %collective-permute-start.8 = (bf16[1280,256]{1,0:T(8,128)(2,1)S(1)}, bf16[1280,256]{1,0:T(8,128)(2,1)S(1)}, u32[]{:S(2)}, u32[]{:S(2)}) collective-permute-start(bf16[1280,256]{1,0:T(8,128)(2,1)S(1)} %collective-permute-done.3.refs_0_), channel_id=1, source_target_pairs={{0,16},{1,17},{2,18},{3,19},{4,20},{5,21},{6,22},{7,23},{8,56},{9,... | collective-permute-start | bytes 1966088 | tf_op jit(solution)/shard_map/ppermute | solution.py:45
  60.3 6.8 %collective-permute-start.10 = (bf16[640,256]{1,0:T(8,128)(2,1)}, bf16[640,256]{1,0:T(8,128)(2,1)S(1)}, u32[]{:S(2)}, u32[]{:S(2)}) collective-permute-start(bf16[640,256]{1,0:T(8,128)(2,1)} %collective-permute-done.4.refs_3_), channel_id=1, source_target_pairs={{0,8},{1,9},{2,10},{3,11},{4,12},{5,13},{6,14},{7,15},{8,0},{9,1},... | collective-permute-start | bytes 983048 | tf_op jit(solution)/shard_map/ppermute | solution.py:45
  60.3 11.1 %collective-permute-start.7 = (bf16[640,256]{1,0:T(8,128)(2,1)S(1)}, bf16[640,256]{1,0:T(8,128)(2,1)}, u32[]{:S(2)}, u32[]{:S(2)}) collective-permute-start(bf16[640,256]{1,0:T(8,128)(2,1)S(1)} %slice.3), channel_id=1, source_target_pairs={{0,64},{1,65},{2,66},{3,67},{4,68},{5,69},{6,70},{7,71},{8,200},{9... | collective-permute-start | bytes 983048 | tf_op jit(solution)/shard_map/ppermute | solution.py:45
  66.0 5.4 %collective-permute-start.11 = (bf16[640,256]{1,0:T(8,128)(2,1)S(1)}, bf16[640,256]{1,0:T(8,128)(2,1)S(1)}, u32[]{:S(2)}, u32[]{:S(2)}) collective-permute-start(bf16[640,256]{1,0:T(8,128)(2,1)S(1)} %collective-permute-done.6.refs_6_), channel_id=1, source_target_pairs={{0,8},{1,9},{2,10},{3,11},{4,12},{5,13},{6,14},{7,15},{8,0},{9,1},... | collective-permute-start | bytes 983048 | tf_op jit(solution)/shard_map/ppermute | solution.py:45
  66.0 9.9 %collective-permute-start.18 = (bf16[1280,256]{1,0:T(8,128)(2,1)S(1)}, bf16[1280,256]{1,0:T(8,128)(2,1)S(1)}, u32[]{:S(2)}, u32[]{:S(2)}) collective-permute-start(bf16[1280,256]{1,0:T(8,128)(2,1)S(1)} %collective-permute-done.17.refs_0_), channel_id=1, source_target_pairs={{0,16},{1,17},{2,18},{3,19},{4,20},{5,21},{6,22},{7,23},{8,56},{9,... | collective-permute-start | bytes 1966088 | tf_op jit(solution)/shard_map/ppermute | solution.py:45
  72.6 15.2 %collective-permute-start.20 = (bf16[1280,256]{1,0:T(8,128)(2,1)S(1)}, bf16[1280,256]{1,0:T(8,128)(2,1)}, u32[]{:S(2)}, u32[]{:S(2)}) collective-permute-start(bf16[1280,256]{1,0:T(8,128)(2,1)S(1)} %collective-permute-done.8.refs_1_), channel_id=1, source_target_pairs={{0,16},{1,17},{2,18},{3,19},{4,20},{5,21},{6,22},{7,23},{8,56},{9,... | collective-permute-start | bytes 1966088 | tf_op jit(solution)/shard_map/ppermute | solution.py:45
  74.3 13.6 %collective-permute-start.13 = (bf16[640,256]{1,0:T(8,128)(2,1)}, bf16[640,256]{1,0:T(8,128)(2,1)}, u32[]{:S(2)}, u32[]{:S(2)}) collective-permute-start(bf16[640,256]{1,0:T(8,128)(2,1)} %collective-permute-done.7.refs_0_), channel_id=1, source_target_pairs={{0,16},{1,17},{2,18},{3,19},{4,20},{5,21},{6,22},{7,23},{8,56},{9,... | collective-permute-start | bytes 983048 | tf_op jit(solution)/shard_map/ppermute | solution.py:45
  74.5 15.5 %collective-permute-start.14 = (bf16[640,256]{1,0:T(8,128)(2,1)}, bf16[640,256]{1,0:T(8,128)(2,1)}, u32[]{:S(2)}, u32[]{:S(2)}) collective-permute-start(bf16[640,256]{1,0:T(8,128)(2,1)} %collective-permute-done.12.refs_1_), channel_id=1, source_target_pairs={{0,16},{1,17},{2,18},{3,19},{4,20},{5,21},{6,22},{7,23},{8,56},{9,... | collective-permute-start | bytes 983048 | tf_op jit(solution)/shard_map/ppermute | solution.py:45
  75.9 16.6 %collective-permute-start.19 = (bf16[1280,256]{1,0:T(8,128)(2,1)S(1)}, bf16[1280,256]{1,0:T(8,128)(2,1)}, u32[]{:S(2)}, u32[]{:S(2)}) collective-permute-start(bf16[1280,256]{1,0:T(8,128)(2,1)S(1)} %collective-permute-done.18.refs_1_), channel_id=1, source_target_pairs={{0,8},{1,9},{2,10},{3,11},{4,12},{5,13},{6,14},{7,15},{8,0},{9,1},... | collective-permute-start | bytes 1966088 | tf_op jit(solution)/shard_map/ppermute | solution.py:45
  78.3 19.5 %collective-permute-start.22 = (bf16[1280,256]{1,0:T(8,128)(2,1)S(1)}, bf16[1280,256]{1,0:T(8,128)(2,1)}, u32[]{:S(2)}, u32[]{:S(2)}) collective-permute-start(bf16[1280,256]{1,0:T(8,128)(2,1)S(1)} %collective-permute-done.8.refs_1_), channel_id=1, source_target_pairs={{0,8},{1,9},{2,10},{3,11},{4,12},{5,13},{6,14},{7,15},{8,0},{9,1},... | collective-permute-start | bytes 1966088 | tf_op jit(solution)/shard_map/ppermute | solution.py:45
  90.0 7.9 %collective-permute-start.23 = (bf16[1280,256]{1,0:T(8,128)(2,1)}, bf16[1280,256]{1,0:T(8,128)(2,1)S(1)}, u32[]{:S(2)}, u32[]{:S(2)}) collective-permute-start(bf16[1280,256]{1,0:T(8,128)(2,1)} %collective-permute-done.20.refs_3_), channel_id=1, source_target_pairs={{0,8},{1,9},{2,10},{3,11},{4,12},{5,13},{6,14},{7,15},{8,0},{9,1},... | collective-permute-start | bytes 1966088 | tf_op jit(solution)/shard_map/ppermute | solution.py:45
  97.2 6.5 %collective-permute-start.21 = (bf16[640,256]{1,0:T(8,128)(2,1)}, bf16[640,256]{1,0:T(8,128)(2,1)S(1)}, u32[]{:S(2)}, u32[]{:S(2)}) collective-permute-start(bf16[640,256]{1,0:T(8,128)(2,1)} %collective-permute-done.13.refs_2_), channel_id=1, source_target_pairs={{0,16},{1,17},{2,18},{3,19},{4,20},{5,21},{6,22},{7,23},{8,56},{9,... | collective-permute-start | bytes 983048 | tf_op jit(solution)/shard_map/ppermute | solution.py:45
  97.2 8.5 %collective-permute-start.15 = (bf16[640,256]{1,0:T(8,128)(2,1)}, bf16[640,256]{1,0:T(8,128)(2,1)S(1)}, u32[]{:S(2)}, u32[]{:S(2)}) collective-permute-start(bf16[640,256]{1,0:T(8,128)(2,1)} %collective-permute-done.13.refs_2_), channel_id=1, source_target_pairs={{0,8},{1,9},{2,10},{3,11},{4,12},{5,13},{6,14},{7,15},{8,0},{9,1},... | collective-permute-start | bytes 983048 | tf_op jit(solution)/shard_map/ppermute | solution.py:45
  97.3 8.4 %collective-permute-start.16 = (bf16[640,256]{1,0:T(8,128)(2,1)}, bf16[640,256]{1,0:T(8,128)(2,1)S(1)}, u32[]{:S(2)}, u32[]{:S(2)}) collective-permute-start(bf16[640,256]{1,0:T(8,128)(2,1)} %collective-permute-done.14.refs_3_), channel_id=1, source_target_pairs={{0,8},{1,9},{2,10},{3,11},{4,12},{5,13},{6,14},{7,15},{8,0},{9,1},... | collective-permute-start | bytes 983048 | tf_op jit(solution)/shard_map/ppermute | solution.py:45
  (20 other events, 161.5 us)
Sparse Core Ops, SparseCore 0:
  9.3 29.5 all-gather.4
  45.1 30.2 all-gather.6

commit v9 on v8

--- a/solution.py
+++ b/solution.py
@@ -212,7 +212,7 @@
     fxzz = send(xzz, ALONG_X)
     xz2, xz2s = send(z2, ALONG_X), send(z2s, ALONG_X)
 
-    left = left_panel_of(own, after(others, z2s), weights)
+    left = left_panel_of(own, after(others, z2s, xzs), weights)
 
     def both(arrays, first_core):
         return [
@@ -234,9 +234,9 @@
         ]
 
     out = block_step(HERE, alike(p, ps, xp, xps, their[0], their[1], fxp, their[2]), left, gamma, None)
+    fxz2 = send(after(xz2, out), ALONG_X)
     their_fxzz = other(after(fxzz, out, xz2, xz2s))
     out = block_step(BACK, both([zz, xzz, other(xzs), fxzz], 0), left, gamma, out)
-    fxz2 = send(after(xz2, out), ALONG_X)
     out = block_step(AHEAD, both([zs, xzs, other(xzz), their_fxzz], 1), left, gamma, out)
     their_fx = other(after(fxz2, out))
     return block_step(ACROSS, alike(z2, z2s, xz2, xz2s, other(xz2), other(xz2s), fxz2, their_fx), left, gamma, out)

time: 120 us -> 117 us (0.975)
  starting transfers between devices: 49.5 us -> 47.5 us
  local copies, waits for them, and re-layouts: 8.2 us -> 6.69 us
    ppermute x25, starting transfers between devices: 49.5 us -> 47.5 us  [send(): return lax.ppermute(value, AXES, way)]
    unnamed x34, local copies, waits for them, and re-layouts: 8.18 us -> 6.67 us
where the time goes in v9:
time: 117 us; the launch traced here: 115 us
  starting transfers between devices  47.5 us (41%)
  waiting for transfers between devices  27.9 us (24%)
  Pallas kernels  19.6 us (17%)
  between operations  13.6 us (12%)
  local copies, waits for them, and re-layouts  6.69 us (6%)
    ppermute x25, starting transfers between devices, send(): return lax.ppermute(value, AXES, way)  47.5 us
    ppermute x25, waiting for transfers between devices, send(): return lax.ppermute(value, AXES, way)  27.8 us
    pallas_call x4, Pallas kernels, block_step(): pl.pallas_call(functools.partial(block_kernel, dz, places, len(arrays), h...  18 us
    unnamed x34, local copies, waits for them, and re-layouts  6.67 us
  transfers between devices with their start and end apart: 27, of which 7 were waited for; matrix products, arithmetic and copies ran while one was open for 0% of the time, Pallas kernels for 12%

profile of v9, /device:TPU:25, one launch (start us, length us, event | category | flops | bytes accessed | tf_op | source)
XLA Modules:
  0.0 115.2 jit_solution(4138882085367976881)
XLA Ops:
  9.2 1.7 %collective-permute-start = (bf16[640,256]{1,0:T(8,128)(2,1)}, bf16[640,256]{1,0:T(8,128)(2,1)S(1)}, u32[]{:S(2)}, u32[]{:S(2)}) collective-permute-start(bf16[640,256]{1,0:T(8,128)(2,1)} %join_shard.1), channel_id=1, source_target_pairs={{0,4},{1,5},{2,6},{3,7},{4,0},{5,1},{6,2},{7,3},{8,12},{9,13},{10,... | collective-permute-start | bytes 983048 | tf_op jit(solution)/shard_map/ppermute | solution.py:45
  10.9 9.3 %collective-permute-start.1 = (bf16[640,256]{1,0:T(8,128)(2,1)}, bf16[640,256]{1,0:T(8,128)(2,1)S(1)}, u32[]{:S(2)}, u32[]{:S(2)}) collective-permute-start(bf16[640,256]{1,0:T(8,128)(2,1)} %join_shard.1), channel_id=1, source_target_pairs={{0,0},{1,16},{2,32},{3,48},{4,8},{5,24},{6,40},{7,56},{8,160},{9,1... | collective-permute-start | bytes 983048 | tf_op jit(solution)/shard_map/ppermute | solution.py:45
  20.3 7.5 %collective-permute-done.1.refs_0_ = bf16[640,256]{1,0:T(8,128)(2,1)S(1)} collective-permute-done((bf16[640,256]{1,0:T(8,128)(2,1)}, bf16[640,256]{1,0:T(8,128)(2,1)S(1)}, u32[]{:S(2)}, u32[]{:S(2)}) %collective-permute-start.1) | collective-permute-done | bytes 327712 | tf_op jit(solution)/shard_map/ppermute | solution.py:45
  27.8 2.4 %collective-permute-start.5 = (bf16[640,256]{1,0:T(8,128)(2,1)S(1)}, bf16[640,256]{1,0:T(8,128)(2,1)S(1)}, u32[]{:S(2)}, u32[]{:S(2)}) collective-permute-start(bf16[640,256]{1,0:T(8,128)(2,1)S(1)} %collective-permute-done.1.refs_0_), channel_id=1, source_target_pairs={{0,16},{1,17},{2,18},{3,19},{4,20},{5,21},{6,22},{7,23},{8,56},{9,... | collective-permute-start | bytes 983048 | tf_op jit(solution)/shard_map/ppermute | solution.py:45
  30.3 14.6 %collective-permute-start.3 = (bf16[1280,256]{1,0:T(8,128)(2,1)S(1)}, bf16[1280,256]{1,0:T(8,128)(2,1)S(1)}, u32[]{:S(2)}, u32[]{:S(2)}) collective-permute-start(bf16[1280,256]{1,0:T(8,128)(2,1)S(1)} %pad_maximum_fusion), channel_id=1, source_target_pairs={{0,64},{1,65},{2,66},{3,67},{4,68},{5,69},{6,70},{7,71},{8,200},{9... | collective-permute-start | bytes 1966088 | tf_op jit(solution)/shard_map/ppermute | solution.py:45
  44.9 1.7 %collective-permute-start.4 = (bf16[640,256]{1,0:T(8,128)(2,1)S(1)}, bf16[640,256]{1,0:T(8,128)(2,1)}, u32[]{:S(2)}, u32[]{:S(2)}) collective-permute-start(bf16[640,256]{1,0:T(8,128)(2,1)S(1)} %collective-permute-done.2.refs_1_), channel_id=1, source_target_pairs={{0,16},{1,17},{2,18},{3,19},{4,20},{5,21},{6,22},{7,23},{8,56},{9,... | collective-permute-start | bytes 983048 | tf_op jit(solution)/shard_map/ppermute | solution.py:45
  46.8 4.5 %collective-permute-done.4.refs_3_ = bf16[640,256]{1,0:T(8,128)(2,1)} collective-permute-done((bf16[640,256]{1,0:T(8,128)(2,1)S(1)}, bf16[640,256]{1,0:T(8,128)(2,1)}, u32[]{:S(2)}, u32[]{:S(2)}) %collective-permute-start.4) | collective-permute-done | bytes 327712 | tf_op jit(solution)/shard_map/ppermute | solution.py:45
  51.2 7.0 %collective-permute-done.3.refs_0_ = bf16[1280,256]{1,0:T(8,128)(2,1)S(1)} collective-permute-done((bf16[1280,256]{1,0:T(8,128)(2,1)S(1)}, bf16[1280,256]{1,0:T(8,128)(2,1)S(1)}, u32[]{:S(2)}, u32[]{:S(2)}) %collective-permute-start.3) | collective-permute-done | bytes 655392 | tf_op jit(solution)/shard_map/ppermute | solution.py:45
  58.7 1.6 %collective-permute-start.8 = (bf16[1280,256]{1,0:T(8,128)(2,1)S(1)}, bf16[1280,256]{1,0:T(8,128)(2,1)S(1)}, u32[]{:S(2)}, u32[]{:S(2)}) collective-permute-start(bf16[1280,256]{1,0:T(8,128)(2,1)S(1)} %collective-permute-done.3.refs_0_), channel_id=1, source_target_pairs={{0,16},{1,17},{2,18},{3,19},{4,20},{5,21},{6,22},{7,23},{8,56},{9,... | collective-permute-start | bytes 1966088 | tf_op jit(solution)/shard_map/ppermute | solution.py:45
  60.3 5.0 %collective-permute-start.7 = (bf16[640,256]{1,0:T(8,128)(2,1)S(1)}, bf16[640,256]{1,0:T(8,128)(2,1)}, u32[]{:S(2)}, u32[]{:S(2)}) collective-permute-start(bf16[640,256]{1,0:T(8,128)(2,1)S(1)} %slice.3), channel_id=1, source_target_pairs={{0,64},{1,65},{2,66},{3,67},{4,68},{5,69},{6,70},{7,71},{8,200},{9... | collective-permute-start | bytes 983048 | tf_op jit(solution)/shard_map/ppermute | solution.py:45
  66.0 1.0 collective-permute-start.14
  67.8 3.6 %collective-permute-done.7.refs_0_ = bf16[640,256]{1,0:T(8,128)(2,1)} collective-permute-done((bf16[640,256]{1,0:T(8,128)(2,1)S(1)}, bf16[640,256]{1,0:T(8,128)(2,1)}, u32[]{:S(2)}, u32[]{:S(2)}) %collective-permute-start.7) | collective-permute-done | bytes 327712 | tf_op jit(solution)/shard_map/ppermute | solution.py:45
  72.6 1.6 %collective-permute-start.21 = (bf16[1280,256]{1,0:T(8,128)(2,1)S(1)}, bf16[1280,256]{1,0:T(8,128)(2,1)}, u32[]{:S(2)}, u32[]{:S(2)}) collective-permute-start(bf16[1280,256]{1,0:T(8,128)(2,1)S(1)} %collective-permute-done.8.refs_1_), channel_id=1, source_target_pairs={{0,16},{1,17},{2,18},{3,19},{4,20},{5,21},{6,22},{7,23},{8,56},{9,... | collective-permute-start | bytes 1966088 | tf_op jit(solution)/shard_map/ppermute | solution.py:45
  74.5 1.3 %collective-permute-start.16 = (bf16[640,256]{1,0:T(8,128)(2,1)}, bf16[640,256]{1,0:T(8,128)(2,1)}, u32[]{:S(2)}, u32[]{:S(2)}) collective-permute-start(bf16[640,256]{1,0:T(8,128)(2,1)} %collective-permute-done.12.refs_1_), channel_id=1, source_target_pairs={{0,16},{1,17},{2,18},{3,19},{4,20},{5,21},{6,22},{7,23},{8,56},{9,... | collective-permute-start | bytes 983048 | tf_op jit(solution)/shard_map/ppermute | solution.py:45
  76.2 1.3 %copy-done.1 = bf16[2560,256]{1,0:T(8,128)(2,1)S(1)} copy-done((bf16[2560,256]{1,0:T(8,128)(2,1)S(1)}, bf16[2560,256]{1,0:T(8,128)(2,1)}, u32[]{:S(2)}) %copy-start.1) | copy-done | bytes 1310744
  77.5 1.3 %copy-done.2 = bf16[2560,256]{1,0:T(8,128)(2,1)S(1)} copy-done((bf16[2560,256]{1,0:T(8,128)(2,1)S(1)}, bf16[2560,256]{1,0:T(8,128)(2,1)}, u32[]{:S(2)}) %copy-start.2) | copy-done | bytes 1310744
  79.7 2.2 %collective-permute-start.23 = (bf16[1280,256]{1,0:T(8,128)(2,1)S(1)}, bf16[1280,256]{1,0:T(8,128)(2,1)S(1)}, u32[]{:S(2)}, u32[]{:S(2)}) collective-permute-start(bf16[1280,256]{1,0:T(8,128)(2,1)S(1)} %collective-permute-done.14.refs_1_), channel_id=1, source_target_pairs={{0,8},{1,9},{2,10},{3,11},{4,12},{5,13},{6,14},{7,15},{8,0},{9,1},... | collective-permute-start | bytes 1966088 | tf_op jit(solution)/shard_map/ppermute | solution.py:45
  81.9 4.4 %block_step.4.refs_5_ = bf16[640,2560]{1,0:T(8,128)(2,1)} custom-call(bf16[8,640,256]{2,1,0:T(8,128)(2,1)S(1)} %weigh_left.1.left_ref, bf16[640,256]{1,0:T(8,128)(2,1)S(1)} %collective-permute-done.1.refs_0_, bf16[640,256]{1,0:T(8,128)(2,1)S(1)} %collective-permute-done.2.refs_1_, bf16[640,256]{1,0:T(8,128)(2,1)S(1)} %copy-done.4, ...), custom_call_target="tpu_custom_call" | custom-call | flops 409600 | bytes 409600 | tf_op jit(solution)/shard_map/block_step/pallas_call | solution.py:166
  86.5 3.5 %collective-permute-done.16.refs_3_ = bf16[640,256]{1,0:T(8,128)(2,1)} collective-permute-done((bf16[640,256]{1,0:T(8,128)(2,1)}, bf16[640,256]{1,0:T(8,128)(2,1)}, u32[]{:S(2)}, u32[]{:S(2)}) %collective-permute-start.16) | collective-permute-done | bytes 327712 | tf_op jit(solution)/shard_map/ppermute | solution.py:45
  90.0 2.5 %collective-permute-start.22 = (bf16[1280,256]{1,0:T(8,128)(2,1)}, bf16[1280,256]{1,0:T(8,128)(2,1)S(1)}, u32[]{:S(2)}, u32[]{:S(2)}) collective-permute-start(bf16[1280,256]{1,0:T(8,128)(2,1)} %collective-permute-done.21.refs_3_), channel_id=1, source_target_pairs={{0,8},{1,9},{2,10},{3,11},{4,12},{5,13},{6,14},{7,15},{8,0},{9,1},... | collective-permute-start | bytes 1966088 | tf_op jit(solution)/shard_map/ppermute | solution.py:45
  93.0 4.5 %block_step.5.refs_5_ = bf16[640,2560]{1,0:T(8,128)(2,1)} custom-call(bf16[8,640,256]{2,1,0:T(8,128)(2,1)S(1)} %weigh_left.1.left_ref, bf16[1280,256]{1,0:T(8,128)(2,1)S(1)} %collective-permute-done.3.refs_0_, bf16[1280,256]{1,0:T(8,128)(2,1)S(1)} %collective-permute-done.8.refs_1_, ...), custom_call_target="tpu_custom_call", output_to_operand_aliasing={{}: (6, {})} | custom-call | flops 409600 | bytes 409600 | tf_op jit(solution)/shard_map/block_step/pallas_call | solution.py:166
  97.5 4.5 %block_step.6.refs_9_ = bf16[640,2560]{1,0:T(8,128)(2,1)} custom-call(bf16[8,640,256]{2,1,0:T(8,128)(2,1)S(1)} %weigh_left.1.left_ref, bf16[1280,256]{1,0:T(8,128)(2,1)S(1)} %collective-permute-done.13.refs_0_, bf16[1280,256]{1,0:T(8,128)(2,1)S(1)} %collective-permute-done.14.refs_1_, ...), custom_call_target="tpu_custom_call", output_to_operand_aliasing={{}: (6, {})} | custom-call | flops 409600 | bytes 409600 | tf_op jit(solution)/shard_map/block_step/pallas_call | solution.py:166
  102.2 1.5 %collective-permute-done.24.refs_7_ = bf16[640,256]{1,0:T(8,128)(2,1)S(1)} collective-permute-done((bf16[640,256]{1,0:T(8,128)(2,1)S(1)}, bf16[640,256]{1,0:T(8,128)(2,1)S(1)}, u32[]{:S(2)}, u32[]{:S(2)}) %collective-permute-start.24) | collective-permute-done | bytes 327712 | tf_op jit(solution)/shard_map/ppermute | solution.py:45
  103.7 4.7 %block_step.7 = bf16[640,2560]{1,0:T(8,128)(2,1)} custom-call(bf16[8,640,256]{2,1,0:T(8,128)(2,1)S(1)} %weigh_left.1.left_ref, bf16[640,256]{1,0:T(8,128)(2,1)} %collective-permute-done.7.refs_0_, bf16[640,256]{1,0:T(8,128)(2,1)} %collective-permute-done.12.refs_1_, ...), custom_call_target="tpu_custom_call", output_to_operand_aliasing={{}: (10, {})} | custom-call | flops 409600 | bytes 409600 | tf_op jit(solution)/shard_map/block_step/pallas_call | solution.py:166
  (75 shorter events, 8.4 us)
Async XLA Ops:
  6.5 40.1 %all-gather.5.cloned.1.call-start = ((), (), s32[]{:S(2)}) async-start(), calls=%async_computation | async-start | bytes 1638400 | tf_op jit(solution)/shard_map/all_gather | solution.py:196
  9.1 67.1 %all-gather.7.cloned.1.call-start = ((), (), s32[]{:S(2)}) async-start(), calls=%async_computation.1 | async-start | bytes 1638400 | tf_op jit(solution)/shard_map/all_gather | solution.py:200
  9.2 11.1 %collective-permute-start = (bf16[640,256]{1,0:T(8,128)(2,1)}, bf16[640,256]{1,0:T(8,128)(2,1)S(1)}, u32[]{:S(2)}, u32[]{:S(2)}) collective-permute-start(bf16[640,256]{1,0:T(8,128)(2,1)} %join_shard.1), channel_id=1, source_target_pairs={{0,4},{1,5},{2,6},{3,7},{4,0},{5,1},{6,2},{7,3},{8,12},{9,13},{10,... | collective-permute-start | bytes 983048 | tf_op jit(solution)/shard_map/ppermute | solution.py:45
  10.9 16.9 %collective-permute-start.1 = (bf16[640,256]{1,0:T(8,128)(2,1)}, bf16[640,256]{1,0:T(8,128)(2,1)S(1)}, u32[]{:S(2)}, u32[]{:S(2)}) collective-permute-start(bf16[640,256]{1,0:T(8,128)(2,1)} %join_shard.1), channel_id=1, source_target_pairs={{0,0},{1,16},{2,32},{3,48},{4,8},{5,24},{6,40},{7,56},{8,160},{9,1... | collective-permute-start | bytes 983048 | tf_op jit(solution)/shard_map/ppermute | solution.py:45
  27.8 18.8 %collective-permute-start.5 = (bf16[640,256]{1,0:T(8,128)(2,1)S(1)}, bf16[640,256]{1,0:T(8,128)(2,1)S(1)}, u32[]{:S(2)}, u32[]{:S(2)}) collective-permute-start(bf16[640,256]{1,0:T(8,128)(2,1)S(1)} %collective-permute-done.1.refs_0_), channel_id=1, source_target_pairs={{0,16},{1,17},{2,18},{3,19},{4,20},{5,21},{6,22},{7,23},{8,56},{9,... | collective-permute-start | bytes 983048 | tf_op jit(solution)/shard_map/ppermute | solution.py:45
  30.3 27.9 %collective-permute-start.3 = (bf16[1280,256]{1,0:T(8,128)(2,1)S(1)}, bf16[1280,256]{1,0:T(8,128)(2,1)S(1)}, u32[]{:S(2)}, u32[]{:S(2)}) collective-permute-start(bf16[1280,256]{1,0:T(8,128)(2,1)S(1)} %pad_maximum_fusion), channel_id=1, source_target_pairs={{0,64},{1,65},{2,66},{3,67},{4,68},{5,69},{6,70},{7,71},{8,200},{9... | collective-permute-start | bytes 1966088 | tf_op jit(solution)/shard_map/ppermute | solution.py:45
  44.9 6.3 %collective-permute-start.4 = (bf16[640,256]{1,0:T(8,128)(2,1)S(1)}, bf16[640,256]{1,0:T(8,128)(2,1)}, u32[]{:S(2)}, u32[]{:S(2)}) collective-permute-start(bf16[640,256]{1,0:T(8,128)(2,1)S(1)} %collective-permute-done.2.refs_1_), channel_id=1, source_target_pairs={{0,16},{1,17},{2,18},{3,19},{4,20},{5,21},{6,22},{7,23},{8,56},{9,... | collective-permute-start | bytes 983048 | tf_op jit(solution)/shard_map/ppermute | solution.py:45
  46.6 11.6 %collective-permute-start.6 = (bf16[640,256]{1,0:T(8,128)(2,1)S(1)}, bf16[640,256]{1,0:T(8,128)(2,1)S(1)}, u32[]{:S(2)}, u32[]{:S(2)}) collective-permute-start(bf16[640,256]{1,0:T(8,128)(2,1)S(1)} %collective-permute-done.5.refs_2_), channel_id=1, source_target_pairs={{0,16},{1,17},{2,18},{3,19},{4,20},{5,21},{6,22},{7,23},{8,56},{9,... | collective-permute-start | bytes 983048 | tf_op jit(solution)/shard_map/ppermute | solution.py:45
  58.2 7.8 %collective-permute-start.13 = (bf16[1280,256]{1,0:T(8,128)(2,1)S(1)}, bf16[1280,256]{1,0:T(8,128)(2,1)S(1)}, u32[]{:S(2)}, u32[]{:S(2)}) collective-permute-start(bf16[1280,256]{1,0:T(8,128)(2,1)S(1)} %collective-permute-done.3.refs_0_), channel_id=1, source_target_pairs={{0,8},{1,9},{2,10},{3,11},{4,12},{5,13},{6,14},{7,15},{8,0},{9,1},... | collective-permute-start | bytes 1966088 | tf_op jit(solution)/shard_map/ppermute | solution.py:45
  58.6 6.6 %collective-permute-start.9 = (bf16[640,256]{1,0:T(8,128)(2,1)S(1)}, bf16[640,256]{1,0:T(8,128)(2,1)S(1)}, u32[]{:S(2)}, u32[]{:S(2)}) collective-permute-start(bf16[640,256]{1,0:T(8,128)(2,1)S(1)} %collective-permute-done.5.refs_2_), channel_id=1, source_target_pairs={{0,8},{1,9},{2,10},{3,11},{4,12},{5,13},{6,14},{7,15},{8,0},{9,1},... | collective-permute-start | bytes 983048 | tf_op jit(solution)/shard_map/ppermute | solution.py:45
  58.7 13.4 %collective-permute-start.8 = (bf16[1280,256]{1,0:T(8,128)(2,1)S(1)}, bf16[1280,256]{1,0:T(8,128)(2,1)S(1)}, u32[]{:S(2)}, u32[]{:S(2)}) collective-permute-start(bf16[1280,256]{1,0:T(8,128)(2,1)S(1)} %collective-permute-done.3.refs_0_), channel_id=1, source_target_pairs={{0,16},{1,17},{2,18},{3,19},{4,20},{5,21},{6,22},{7,23},{8,56},{9,... | collective-permute-start | bytes 1966088 | tf_op jit(solution)/shard_map/ppermute | solution.py:45
  60.3 6.8 %collective-permute-start.10 = (bf16[640,256]{1,0:T(8,128)(2,1)}, bf16[640,256]{1,0:T(8,128)(2,1)S(1)}, u32[]{:S(2)}, u32[]{:S(2)}) collective-permute-start(bf16[640,256]{1,0:T(8,128)(2,1)} %collective-permute-done.4.refs_3_), channel_id=1, source_target_pairs={{0,8},{1,9},{2,10},{3,11},{4,12},{5,13},{6,14},{7,15},{8,0},{9,1},... | collective-permute-start | bytes 983048 | tf_op jit(solution)/shard_map/ppermute | solution.py:45
  60.3 11.1 %collective-permute-start.7 = (bf16[640,256]{1,0:T(8,128)(2,1)S(1)}, bf16[640,256]{1,0:T(8,128)(2,1)}, u32[]{:S(2)}, u32[]{:S(2)}) collective-permute-start(bf16[640,256]{1,0:T(8,128)(2,1)S(1)} %slice.3), channel_id=1, source_target_pairs={{0,64},{1,65},{2,66},{3,67},{4,68},{5,69},{6,70},{7,71},{8,200},{9... | collective-permute-start | bytes 983048 | tf_op jit(solution)/shard_map/ppermute | solution.py:45
  66.0 5.4 %collective-permute-start.11 = (bf16[640,256]{1,0:T(8,128)(2,1)S(1)}, bf16[640,256]{1,0:T(8,128)(2,1)S(1)}, u32[]{:S(2)}, u32[]{:S(2)}) collective-permute-start(bf16[640,256]{1,0:T(8,128)(2,1)S(1)} %collective-permute-done.6.refs_6_), channel_id=1, source_target_pairs={{0,8},{1,9},{2,10},{3,11},{4,12},{5,13},{6,14},{7,15},{8,0},{9,1},... | collective-permute-start | bytes 983048 | tf_op jit(solution)/shard_map/ppermute | solution.py:45
  66.0 10.2 %collective-permute-start.14 = (bf16[1280,256]{1,0:T(8,128)(2,1)S(1)}, bf16[1280,256]{1,0:T(8,128)(2,1)S(1)}, u32[]{:S(2)}, u32[]{:S(2)}) collective-permute-start(bf16[1280,256]{1,0:T(8,128)(2,1)S(1)} %collective-permute-done.13.refs_0_), channel_id=1, source_target_pairs={{0,16},{1,17},{2,18},{3,19},{4,20},{5,21},{6,22},{7,23},{8,56},{9,... | collective-permute-start | bytes 1966088 | tf_op jit(solution)/shard_map/ppermute | solution.py:45
  72.6 13.9 %collective-permute-start.21 = (bf16[1280,256]{1,0:T(8,128)(2,1)S(1)}, bf16[1280,256]{1,0:T(8,128)(2,1)}, u32[]{:S(2)}, u32[]{:S(2)}) collective-permute-start(bf16[1280,256]{1,0:T(8,128)(2,1)S(1)} %collective-permute-done.8.refs_1_), channel_id=1, source_target_pairs={{0,16},{1,17},{2,18},{3,19},{4,20},{5,21},{6,22},{7,23},{8,56},{9,... | collective-permute-start | bytes 1966088 | tf_op jit(solution)/shard_map/ppermute | solution.py:45
  74.2 12.2 %collective-permute-start.15 = (bf16[640,256]{1,0:T(8,128)(2,1)}, bf16[640,256]{1,0:T(8,128)(2,1)}, u32[]{:S(2)}, u32[]{:S(2)}) collective-permute-start(bf16[640,256]{1,0:T(8,128)(2,1)} %collective-permute-done.7.refs_0_), channel_id=1, source_target_pairs={{0,16},{1,17},{2,18},{3,19},{4,20},{5,21},{6,22},{7,23},{8,56},{9,... | collective-permute-start | bytes 983048 | tf_op jit(solution)/shard_map/ppermute | solution.py:45
  74.5 15.5 %collective-permute-start.16 = (bf16[640,256]{1,0:T(8,128)(2,1)}, bf16[640,256]{1,0:T(8,128)(2,1)}, u32[]{:S(2)}, u32[]{:S(2)}) collective-permute-start(bf16[640,256]{1,0:T(8,128)(2,1)} %collective-permute-done.12.refs_1_), channel_id=1, source_target_pairs={{0,16},{1,17},{2,18},{3,19},{4,20},{5,21},{6,22},{7,23},{8,56},{9,... | collective-permute-start | bytes 983048 | tf_op jit(solution)/shard_map/ppermute | solution.py:45
  75.8 21.6 %collective-permute-start.20 = (bf16[1280,256]{1,0:T(8,128)(2,1)S(1)}, bf16[1280,256]{1,0:T(8,128)(2,1)}, u32[]{:S(2)}, u32[]{:S(2)}) collective-permute-start(bf16[1280,256]{1,0:T(8,128)(2,1)S(1)} %collective-permute-done.8.refs_1_), channel_id=1, source_target_pairs={{0,8},{1,9},{2,10},{3,11},{4,12},{5,13},{6,14},{7,15},{8,0},{9,1},... | collective-permute-start | bytes 1966088 | tf_op jit(solution)/shard_map/ppermute | solution.py:45
  79.7 12.8 %collective-permute-start.23 = (bf16[1280,256]{1,0:T(8,128)(2,1)S(1)}, bf16[1280,256]{1,0:T(8,128)(2,1)S(1)}, u32[]{:S(2)}, u32[]{:S(2)}) collective-permute-start(bf16[1280,256]{1,0:T(8,128)(2,1)S(1)} %collective-permute-done.14.refs_1_), channel_id=1, source_target_pairs={{0,8},{1,9},{2,10},{3,11},{4,12},{5,13},{6,14},{7,15},{8,0},{9,1},... | collective-permute-start | bytes 1966088 | tf_op jit(solution)/shard_map/ppermute | solution.py:45
  90.0 7.5 %collective-permute-start.22 = (bf16[1280,256]{1,0:T(8,128)(2,1)}, bf16[1280,256]{1,0:T(8,128)(2,1)S(1)}, u32[]{:S(2)}, u32[]{:S(2)}) collective-permute-start(bf16[1280,256]{1,0:T(8,128)(2,1)} %collective-permute-done.21.refs_3_), channel_id=1, source_target_pairs={{0,8},{1,9},{2,10},{3,11},{4,12},{5,13},{6,14},{7,15},{8,0},{9,1},... | collective-permute-start | bytes 1966088 | tf_op jit(solution)/shard_map/ppermute | solution.py:45
  92.5 9.5 %collective-permute-start.19 = (bf16[640,256]{1,0:T(8,128)(2,1)}, bf16[640,256]{1,0:T(8,128)(2,1)S(1)}, u32[]{:S(2)}, u32[]{:S(2)}) collective-permute-start(bf16[640,256]{1,0:T(8,128)(2,1)} %collective-permute-done.15.refs_2_), channel_id=1, source_target_pairs={{0,16},{1,17},{2,18},{3,19},{4,20},{5,21},{6,22},{7,23},{8,56},{9,... | collective-permute-start | bytes 983048 | tf_op jit(solution)/shard_map/ppermute | solution.py:45
  92.5 9.7 %collective-permute-start.17 = (bf16[640,256]{1,0:T(8,128)(2,1)}, bf16[640,256]{1,0:T(8,128)(2,1)S(1)}, u32[]{:S(2)}, u32[]{:S(2)}) collective-permute-start(bf16[640,256]{1,0:T(8,128)(2,1)} %collective-permute-done.15.refs_2_), channel_id=1, source_target_pairs={{0,8},{1,9},{2,10},{3,11},{4,12},{5,13},{6,14},{7,15},{8,0},{9,1},... | collective-permute-start | bytes 983048 | tf_op jit(solution)/shard_map/ppermute | solution.py:45
  92.5 9.7 %collective-permute-start.18 = (bf16[640,256]{1,0:T(8,128)(2,1)}, bf16[640,256]{1,0:T(8,128)(2,1)S(1)}, u32[]{:S(2)}, u32[]{:S(2)}) collective-permute-start(bf16[640,256]{1,0:T(8,128)(2,1)} %collective-permute-done.16.refs_3_), channel_id=1, source_target_pairs={{0,8},{1,9},{2,10},{3,11},{4,12},{5,13},{6,14},{7,15},{8,0},{9,1},... | collective-permute-start | bytes 983048 | tf_op jit(solution)/shard_map/ppermute | solution.py:45
  (20 other events, 160.5 us)
Sparse Core Ops, SparseCore 0:
  9.3 29.5 all-gather.4
  45.1 30.2 all-gather.6

commit v10 on v9

--- a/solution.py
+++ b/solution.py
@@ -53,39 +53,38 @@
     return lax.optimization_barrier((value, *earlier))[0]
 
 
-def weigh(own_ref, other_ref, weights_ref, out_ref):
-    half = own_ref.shape[-1] // 2
-    k = pl.program_id(0)
-    away, y = lax.div(k, jnp.int32(Y)), rem(k, Y)
+def weigh(away, panel_ref, weights_ref, *refs):
+    out_ref = refs[-1]
+    half = panel_ref.shape[-1] // 2
     side = rem(lax.div(lax.axis_index("col"), jnp.int32(Y)) + away, ZL)
-    weights = weights_ref[side * Y + y]
-
-    def put(panel_ref):
-        panel = panel_ref[...].astype(jnp.float32)
-        out_ref[:, :half] = (panel[:, half:] * weights).astype(jnp.bfloat16)
-        out_ref[:, half:] = (panel[:, :half] * weights).astype(jnp.bfloat16)
-
-    pl.when(away == 0)(lambda: put(own_ref))
-    pl.when(away == 1)(lambda: put(other_ref))
-
-
-def left_panel_of(own, others, weights):
-    side, height, width = own.shape
+    weights = weights_ref[side * Y + pl.program_id(0)]
+    panel = panel_ref[...].astype(jnp.float32)
+    out_ref[:, :half] = (panel[:, half:] * weights).astype(jnp.bfloat16)
+    out_ref[:, half:] = (panel[:, :half] * weights).astype(jnp.bfloat16)
+
+
+def left_panel_half(away, gathered, weights, out):
+    side, height, width = gathered.shape
     parts = ZL * side
+    operands = [gathered, weights.reshape(parts, 1, width // 2)]
+    specs = [
+        pl.BlockSpec((None, height, width), lambda k: (k, 0, 0)),
+        pl.BlockSpec((parts, 1, width // 2), lambda k: (0, 0, 0)),
+    ]
+    if out is not None:
+        operands.append(out)
+        specs.append(pl.BlockSpec(memory_space=pl.ANY))
     return pl.pallas_call(
-        weigh,
-        grid=(parts,),
-        in_specs=[
-            pl.BlockSpec((None, height, width), lambda k: (jnp.minimum(k, side - 1), 0, 0)),
-            pl.BlockSpec((None, height, width), lambda k: (jnp.maximum(k - side, 0), 0, 0)),
-            pl.BlockSpec((parts, 1, width // 2), lambda k: (0, 0, 0)),
-        ],
-        out_specs=pl.BlockSpec((None, height, width), lambda k: (k, 0, 0)),
+        functools.partial(weigh, away),
+        grid=(side,),
+        in_specs=specs,
+        out_specs=pl.BlockSpec((None, height, width), lambda k: (k + away * side, 0, 0)),
         out_shape=jax.ShapeDtypeStruct((parts, height, width), jnp.bfloat16),
+        input_output_aliases={} if out is None else {2: 0},
         compiler_params=pltpu.CompilerParams(vmem_limit_bytes=8 * 2**20),
         cost_estimate=pl.CostEstimate(flops=height, bytes_accessed=height * width, transcendentals=0),
         name="weigh_left",
-    )(own, others, weights.reshape(parts, 1, width // 2))
+    )(*operands)
 
 
 def rem(value, length):
@@ -207,12 +206,13 @@
     zs = other(zz)
     z2 = send(zz[:height], ALONG_Z)
     xzz, xzs = send(zz, ALONG_X), send(zs, ALONG_X)
-    z2 = after(z2, xzz, *their)
+    half_left = left_panel_half(0, own, weights, None)
+    z2 = after(z2, xzz, half_left, *their)
     z2s = other(z2)
     fxzz = send(xzz, ALONG_X)
     xz2, xz2s = send(z2, ALONG_X), send(z2s, ALONG_X)
 
-    left = left_panel_of(own, after(others, z2s, xzs), weights)
+    left = left_panel_half(1, after(others, z2s, xzs), weights, half_left)
 
     def both(arrays, first_core):
         return [
@@ -235,11 +235,12 @@
 
     out = block_step(HERE, alike(p, ps, xp, xps, their[0], their[1], fxp, their[2]), left, gamma, None)
     fxz2 = send(after(xz2, out), ALONG_X)
-    their_fxzz = other(after(fxzz, out, xz2, xz2s))
+    their_fxzz = other(after(fxzz, out, xz2))
     out = block_step(BACK, both([zz, xzz, other(xzs), fxzz], 0), left, gamma, out)
+    their_xz2s = other(after(xz2s, out))
     out = block_step(AHEAD, both([zs, xzs, other(xzz), their_fxzz], 1), left, gamma, out)
     their_fx = other(after(fxz2, out))
-    return block_step(ACROSS, alike(z2, z2s, xz2, xz2s, other(xz2), other(xz2s), fxz2, their_fx), left, gamma, out)
+    return block_step(ACROSS, alike(z2, z2s, xz2, xz2s, other(xz2), their_xz2s, fxz2, their_fx), left, gamma, out)
 
 
 def solution(mesh):

time: 117 us -> 117 us (level)
  starting transfers between devices: 47.5 us -> 50.1 us
  waiting for transfers between devices: 27.9 us -> 25.6 us
    ppermute x25, starting transfers between devices: 47.5 us -> 50.1 us  [send(): return lax.ppermute(value, AXES, way)]
    ppermute x25, waiting for transfers between devices: 27.8 us -> 25.6 us  [send(): return lax.ppermute(value, AXES, way)]
    unnamed x34 -> x42, local copies, waits for them, and re-layouts: 6.67 us -> 6.73 us
  transfers between devices with their start and end apart: 27 -> 27, of which waited for: 7 -> 8; matrix products, arithmetic and copies ran while one was open for 0% -> 0% of each run, Pallas kernels for 12% -> 13%
where the time goes in v10:
time: 117 us; the launch traced here: 116 us
  starting transfers between devices  50.1 us (43%)
  waiting for transfers between devices  25.6 us (22%)
  Pallas kernels  20 us (17%)
  between operations  13.7 us (12%)
  local copies, waits for them, and re-layouts  6.75 us (6%)
    ppermute x25, starting transfers between devices, send(): return lax.ppermute(value, AXES, way)  50.1 us
    ppermute x25, waiting for transfers between devices, send(): return lax.ppermute(value, AXES, way)  25.6 us
    pallas_call x4, Pallas kernels, block_step(): pl.pallas_call(functools.partial(block_kernel, dz, places, len(arrays), h...  18.5 us
    unnamed x42, local copies, waits for them, and re-layouts  6.73 us
  transfers between devices with their start and end apart: 27, of which 8 were waited for; matrix products, arithmetic and copies ran while one was open for 0% of the time, Pallas kernels for 13%

profile of v10, /device:TPU:25, one launch (start us, length us, event | category | flops | bytes accessed | tf_op | source)
XLA Modules:
  0.0 116.2 jit_solution(444229943832878933)
XLA Ops:
  9.2 1.7 %collective-permute-start = (bf16[640,256]{1,0:T(8,128)(2,1)}, bf16[640,256]{1,0:T(8,128)(2,1)S(1)}, u32[]{:S(2)}, u32[]{:S(2)}) collective-permute-start(bf16[640,256]{1,0:T(8,128)(2,1)} %join_shard.1), channel_id=1, source_target_pairs={{0,4},{1,5},{2,6},{3,7},{4,0},{5,1},{6,2},{7,3},{8,12},{9,13},{10,... | collective-permute-start | bytes 983048 | tf_op jit(solution)/shard_map/ppermute | solution.py:45
  10.9 9.3 %collective-permute-start.1 = (bf16[640,256]{1,0:T(8,128)(2,1)}, bf16[640,256]{1,0:T(8,128)(2,1)S(1)}, u32[]{:S(2)}, u32[]{:S(2)}) collective-permute-start(bf16[640,256]{1,0:T(8,128)(2,1)} %join_shard.1), channel_id=1, source_target_pairs={{0,0},{1,16},{2,32},{3,48},{4,8},{5,24},{6,40},{7,56},{8,160},{9,1... | collective-permute-start | bytes 983048 | tf_op jit(solution)/shard_map/ppermute | solution.py:45
  20.3 7.5 %collective-permute-done.1.refs_0_ = bf16[640,256]{1,0:T(8,128)(2,1)S(1)} collective-permute-done((bf16[640,256]{1,0:T(8,128)(2,1)}, bf16[640,256]{1,0:T(8,128)(2,1)S(1)}, u32[]{:S(2)}, u32[]{:S(2)}) %collective-permute-start.1) | collective-permute-done | bytes 327712 | tf_op jit(solution)/shard_map/ppermute | solution.py:45
  27.8 2.5 %collective-permute-start.5 = (bf16[640,256]{1,0:T(8,128)(2,1)S(1)}, bf16[640,256]{1,0:T(8,128)(2,1)S(1)}, u32[]{:S(2)}, u32[]{:S(2)}) collective-permute-start(bf16[640,256]{1,0:T(8,128)(2,1)S(1)} %collective-permute-done.1.refs_0_), channel_id=1, source_target_pairs={{0,16},{1,17},{2,18},{3,19},{4,20},{5,21},{6,22},{7,23},{8,56},{9,... | collective-permute-start | bytes 983048 | tf_op jit(solution)/shard_map/ppermute | solution.py:45
  30.4 14.5 %collective-permute-start.3 = (bf16[1280,256]{1,0:T(8,128)(2,1)S(1)}, bf16[1280,256]{1,0:T(8,128)(2,1)S(1)}, u32[]{:S(2)}, u32[]{:S(2)}) collective-permute-start(bf16[1280,256]{1,0:T(8,128)(2,1)S(1)} %pad_maximum_fusion), channel_id=1, source_target_pairs={{0,64},{1,65},{2,66},{3,67},{4,68},{5,69},{6,70},{7,71},{8,200},{9... | collective-permute-start | bytes 1966088 | tf_op jit(solution)/shard_map/ppermute | solution.py:45
  44.9 1.7 %collective-permute-start.4 = (bf16[640,256]{1,0:T(8,128)(2,1)S(1)}, bf16[640,256]{1,0:T(8,128)(2,1)}, u32[]{:S(2)}, u32[]{:S(2)}) collective-permute-start(bf16[640,256]{1,0:T(8,128)(2,1)S(1)} %collective-permute-done.2.refs_1_), channel_id=1, source_target_pairs={{0,16},{1,17},{2,18},{3,19},{4,20},{5,21},{6,22},{7,23},{8,56},{9,... | collective-permute-start | bytes 983048 | tf_op jit(solution)/shard_map/ppermute | solution.py:45
  46.8 4.5 %collective-permute-done.4.refs_3_ = bf16[640,256]{1,0:T(8,128)(2,1)} collective-permute-done((bf16[640,256]{1,0:T(8,128)(2,1)S(1)}, bf16[640,256]{1,0:T(8,128)(2,1)}, u32[]{:S(2)}, u32[]{:S(2)}) %collective-permute-start.4) | collective-permute-done | bytes 327712 | tf_op jit(solution)/shard_map/ppermute | solution.py:45
  51.2 7.0 %collective-permute-done.3.refs_0_ = bf16[1280,256]{1,0:T(8,128)(2,1)S(1)} collective-permute-done((bf16[1280,256]{1,0:T(8,128)(2,1)S(1)}, bf16[1280,256]{1,0:T(8,128)(2,1)S(1)}, u32[]{:S(2)}, u32[]{:S(2)}) %collective-permute-start.3) | collective-permute-done | bytes 655392 | tf_op jit(solution)/shard_map/ppermute | solution.py:45
  58.6 1.6 %collective-permute-start.8 = (bf16[1280,256]{1,0:T(8,128)(2,1)S(1)}, bf16[1280,256]{1,0:T(8,128)(2,1)}, u32[]{:S(2)}, u32[]{:S(2)}) collective-permute-start(bf16[1280,256]{1,0:T(8,128)(2,1)S(1)} %collective-permute-done.3.refs_0_), channel_id=1, source_target_pairs={{0,16},{1,17},{2,18},{3,19},{4,20},{5,21},{6,22},{7,23},{8,56},{9,... | collective-permute-start | bytes 1966088 | tf_op jit(solution)/shard_map/ppermute | solution.py:45
  60.7 5.0 %collective-permute-start.7 = (bf16[640,256]{1,0:T(8,128)(2,1)S(1)}, bf16[640,256]{1,0:T(8,128)(2,1)}, u32[]{:S(2)}, u32[]{:S(2)}) collective-permute-start(bf16[640,256]{1,0:T(8,128)(2,1)S(1)} %slice.3), channel_id=1, source_target_pairs={{0,64},{1,65},{2,66},{3,67},{4,68},{5,69},{6,70},{7,71},{8,200},{9... | collective-permute-start | bytes 983048 | tf_op jit(solution)/shard_map/ppermute | solution.py:45
  66.6 1.9 %collective-permute-done.8.refs_1_ = bf16[1280,256]{1,0:T(8,128)(2,1)} collective-permute-done((bf16[1280,256]{1,0:T(8,128)(2,1)S(1)}, bf16[1280,256]{1,0:T(8,128)(2,1)}, u32[]{:S(2)}, u32[]{:S(2)}) %collective-permute-start.8) | collective-permute-done | bytes 655392 | tf_op jit(solution)/shard_map/ppermute | solution.py:45
  68.5 2.8 %collective-permute-start.19 = (bf16[1280,256]{1,0:T(8,128)(2,1)}, bf16[1280,256]{1,0:T(8,128)(2,1)}, u32[]{:S(2)}, u32[]{:S(2)}) collective-permute-start(bf16[1280,256]{1,0:T(8,128)(2,1)} %collective-permute-done.8.refs_1_), channel_id=1, source_target_pairs={{0,16},{1,17},{2,18},{3,19},{4,20},{5,21},{6,22},{7,23},{8,56},{9,... | collective-permute-start | bytes 1966088 | tf_op jit(solution)/shard_map/ppermute | solution.py:45
  71.3 1.3 %copy-done.5 = bf16[2560,256]{1,0:T(8,128)(2,1)S(1)} copy-done((bf16[2560,256]{1,0:T(8,128)(2,1)S(1)}, bf16[2560,256]{1,0:T(8,128)(2,1)}, u32[]{:S(2)}) %copy-start.5) | copy-done | bytes 1310744
  74.5 2.3 %collective-permute-start.15 = (bf16[640,256]{1,0:T(8,128)(2,1)}, bf16[640,256]{1,0:T(8,128)(2,1)}, u32[]{:S(2)}, u32[]{:S(2)}) collective-permute-start(bf16[640,256]{1,0:T(8,128)(2,1)} %collective-permute-done.7.refs_0_), channel_id=1, source_target_pairs={{0,16},{1,17},{2,18},{3,19},{4,20},{5,21},{6,22},{7,23},{8,56},{9,... | collective-permute-start | bytes 983048 | tf_op jit(solution)/shard_map/ppermute | solution.py:45
  76.9 1.3 %copy-done.6 = bf16[2560,256]{1,0:T(8,128)(2,1)S(1)} copy-done((bf16[2560,256]{1,0:T(8,128)(2,1)S(1)}, bf16[2560,256]{1,0:T(8,128)(2,1)}, u32[]{:S(2)}) %copy-start.6) | copy-done | bytes 1310744
  78.7 2.4 %collective-permute-start.18 = (bf16[1280,256]{1,0:T(8,128)(2,1)}, bf16[1280,256]{1,0:T(8,128)(2,1)S(1)}, u32[]{:S(2)}, u32[]{:S(2)}) collective-permute-start(bf16[1280,256]{1,0:T(8,128)(2,1)} %collective-permute-done.14.refs_1_), channel_id=1, source_target_pairs={{0,8},{1,9},{2,10},{3,11},{4,12},{5,13},{6,14},{7,15},{8,0},{9,1},... | collective-permute-start | bytes 1966088 | tf_op jit(solution)/shard_map/ppermute | solution.py:45
  81.2 4.4 %block_step.4.refs_5_ = bf16[640,2560]{1,0:T(8,128)(2,1)} custom-call(bf16[8,640,256]{2,1,0:T(8,128)(2,1)S(1)} %weigh_left.3.left_ref, bf16[640,256]{1,0:T(8,128)(2,1)S(1)} %copy-done.2, bf16[640,256]{1,0:T(8,128)(2,1)S(1)} %copy-done.4, bf16[640,256]{1,0:T(8,128)(2,1)S(1)} %copy-done.8, bf16[640,256]{1,0:T(8,128)(2,1)} %collective-permute-done.4.refs_3_, ...), custom_call_target="tpu_custom_call" | custom-call | flops 409600 | bytes 409600 | tf_op jit(solution)/shard_map/block_step/pallas_call | solution.py:165
  85.5 1.5 %collective-permute-done.15.refs_2_ = bf16[640,256]{1,0:T(8,128)(2,1)} collective-permute-done((bf16[640,256]{1,0:T(8,128)(2,1)}, bf16[640,256]{1,0:T(8,128)(2,1)}, u32[]{:S(2)}, u32[]{:S(2)}) %collective-permute-start.15) | collective-permute-done | bytes 327712 | tf_op jit(solution)/shard_map/ppermute | solution.py:45
  87.0 2.6 %collective-permute-start.23 = (bf16[1280,256]{1,0:T(8,128)(2,1)}, bf16[1280,256]{1,0:T(8,128)(2,1)S(1)}, u32[]{:S(2)}, u32[]{:S(2)}) collective-permute-start(bf16[1280,256]{1,0:T(8,128)(2,1)} %collective-permute-done.19.refs_3_), channel_id=1, source_target_pairs={{0,8},{1,9},{2,10},{3,11},{4,12},{5,13},{6,14},{7,15},{8,0},{9,1},... | collective-permute-start | bytes 1966088 | tf_op jit(solution)/shard_map/ppermute | solution.py:45
  89.8 4.7 %block_step.5.refs_5_ = bf16[640,2560]{1,0:T(8,128)(2,1)} custom-call(bf16[8,640,256]{2,1,0:T(8,128)(2,1)S(1)} %weigh_left.3.left_ref, bf16[1280,256]{1,0:T(8,128)(2,1)S(1)} %collective-permute-done.3.refs_0_, bf16[1280,256]{1,0:T(8,128)(2,1)} %collective-permute-done.8.refs_1_, ...), custom_call_target="tpu_custom_call", output_to_operand_aliasing={{}: (6, {})} | custom-call | flops 409600 | bytes 409600 | tf_op jit(solution)/shard_map/block_step/pallas_call | solution.py:165
  94.5 1.5 %collective-permute-done.16.refs_3_ = bf16[640,256]{1,0:T(8,128)(2,1)S(1)} collective-permute-done((bf16[640,256]{1,0:T(8,128)(2,1)}, bf16[640,256]{1,0:T(8,128)(2,1)S(1)}, u32[]{:S(2)}, u32[]{:S(2)}) %collective-permute-start.16) | collective-permute-done | bytes 327712 | tf_op jit(solution)/shard_map/ppermute | solution.py:45
  96.0 4.9 %block_step.6.refs_9_ = bf16[640,2560]{1,0:T(8,128)(2,1)} custom-call(bf16[8,640,256]{2,1,0:T(8,128)(2,1)S(1)} %weigh_left.3.left_ref, bf16[1280,256]{1,0:T(8,128)(2,1)} %collective-permute-done.13.refs_0_, bf16[1280,256]{1,0:T(8,128)(2,1)} %collective-permute-done.14.refs_1_, ...), custom_call_target="tpu_custom_call", output_to_operand_aliasing={{}: (6, {})} | custom-call | flops 409600 | bytes 409600 | tf_op jit(solution)/shard_map/block_step/pallas_call | solution.py:165
  100.9 2.2 %collective-permute-start.24 = (bf16[640,256]{1,0:T(8,128)(2,1)S(1)}, bf16[640,256]{1,0:T(8,128)(2,1)S(1)}, u32[]{:S(2)}, u32[]{:S(2)}) collective-permute-start(bf16[640,256]{1,0:T(8,128)(2,1)S(1)} %collective-permute-done.21.refs_6_), channel_id=1, source_target_pairs={{0,8},{1,9},{2,10},{3,11},{4,12},{5,13},{6,14},{7,15},{8,0},{9,1},... | collective-permute-start | bytes 983048 | tf_op jit(solution)/shard_map/ppermute | solution.py:45
  104.8 4.6 %block_step.7 = bf16[640,2560]{1,0:T(8,128)(2,1)} custom-call(bf16[8,640,256]{2,1,0:T(8,128)(2,1)S(1)} %weigh_left.3.left_ref, bf16[640,256]{1,0:T(8,128)(2,1)} %collective-permute-done.7.refs_0_, bf16[640,256]{1,0:T(8,128)(2,1)} %collective-permute-done.12.refs_1_, ...), custom_call_target="tpu_custom_call", output_to_operand_aliasing={{}: (10, {})} | custom-call | flops 409600 | bytes 409600 | tf_op jit(solution)/shard_map/block_step/pallas_call | solution.py:165
  (84 shorter events, 8.9 us)
Async XLA Ops:
  6.5 40.1 %all-gather.7.cloned.1.call-start = ((), (), s32[]{:S(2)}) async-start(), calls=%async_computation.1 | async-start | bytes 1638400 | tf_op jit(solution)/shard_map/all_gather | solution.py:195
  9.1 67.7 %all-gather.5.cloned.1.call-start = ((), (), s32[]{:S(2)}) async-start(), calls=%async_computation | async-start | bytes 1638400 | tf_op jit(solution)/shard_map/all_gather | solution.py:199
  9.2 11.1 %collective-permute-start = (bf16[640,256]{1,0:T(8,128)(2,1)}, bf16[640,256]{1,0:T(8,128)(2,1)S(1)}, u32[]{:S(2)}, u32[]{:S(2)}) collective-permute-start(bf16[640,256]{1,0:T(8,128)(2,1)} %join_shard.1), channel_id=1, source_target_pairs={{0,4},{1,5},{2,6},{3,7},{4,0},{5,1},{6,2},{7,3},{8,12},{9,13},{10,... | collective-permute-start | bytes 983048 | tf_op jit(solution)/shard_map/ppermute | solution.py:45
  10.9 16.9 %collective-permute-start.1 = (bf16[640,256]{1,0:T(8,128)(2,1)}, bf16[640,256]{1,0:T(8,128)(2,1)S(1)}, u32[]{:S(2)}, u32[]{:S(2)}) collective-permute-start(bf16[640,256]{1,0:T(8,128)(2,1)} %join_shard.1), channel_id=1, source_target_pairs={{0,0},{1,16},{2,32},{3,48},{4,8},{5,24},{6,40},{7,56},{8,160},{9,1... | collective-permute-start | bytes 983048 | tf_op jit(solution)/shard_map/ppermute | solution.py:45
  27.8 18.8 %collective-permute-start.5 = (bf16[640,256]{1,0:T(8,128)(2,1)S(1)}, bf16[640,256]{1,0:T(8,128)(2,1)S(1)}, u32[]{:S(2)}, u32[]{:S(2)}) collective-permute-start(bf16[640,256]{1,0:T(8,128)(2,1)S(1)} %collective-permute-done.1.refs_0_), channel_id=1, source_target_pairs={{0,16},{1,17},{2,18},{3,19},{4,20},{5,21},{6,22},{7,23},{8,56},{9,... | collective-permute-start | bytes 983048 | tf_op jit(solution)/shard_map/ppermute | solution.py:45
  30.4 27.8 %collective-permute-start.3 = (bf16[1280,256]{1,0:T(8,128)(2,1)S(1)}, bf16[1280,256]{1,0:T(8,128)(2,1)S(1)}, u32[]{:S(2)}, u32[]{:S(2)}) collective-permute-start(bf16[1280,256]{1,0:T(8,128)(2,1)S(1)} %pad_maximum_fusion), channel_id=1, source_target_pairs={{0,64},{1,65},{2,66},{3,67},{4,68},{5,69},{6,70},{7,71},{8,200},{9... | collective-permute-start | bytes 1966088 | tf_op jit(solution)/shard_map/ppermute | solution.py:45
  44.9 6.3 %collective-permute-start.4 = (bf16[640,256]{1,0:T(8,128)(2,1)S(1)}, bf16[640,256]{1,0:T(8,128)(2,1)}, u32[]{:S(2)}, u32[]{:S(2)}) collective-permute-start(bf16[640,256]{1,0:T(8,128)(2,1)S(1)} %collective-permute-done.2.refs_1_), channel_id=1, source_target_pairs={{0,16},{1,17},{2,18},{3,19},{4,20},{5,21},{6,22},{7,23},{8,56},{9,... | collective-permute-start | bytes 983048 | tf_op jit(solution)/shard_map/ppermute | solution.py:45
  46.6 11.6 %collective-permute-start.6 = (bf16[640,256]{1,0:T(8,128)(2,1)S(1)}, bf16[640,256]{1,0:T(8,128)(2,1)S(1)}, u32[]{:S(2)}, u32[]{:S(2)}) collective-permute-start(bf16[640,256]{1,0:T(8,128)(2,1)S(1)} %collective-permute-done.5.refs_2_), channel_id=1, source_target_pairs={{0,16},{1,17},{2,18},{3,19},{4,20},{5,21},{6,22},{7,23},{8,56},{9,... | collective-permute-start | bytes 983048 | tf_op jit(solution)/shard_map/ppermute | solution.py:45
  58.2 8.2 %collective-permute-start.13 = (bf16[1280,256]{1,0:T(8,128)(2,1)S(1)}, bf16[1280,256]{1,0:T(8,128)(2,1)}, u32[]{:S(2)}, u32[]{:S(2)}) collective-permute-start(bf16[1280,256]{1,0:T(8,128)(2,1)S(1)} %collective-permute-done.3.refs_0_), channel_id=1, source_target_pairs={{0,8},{1,9},{2,10},{3,11},{4,12},{5,13},{6,14},{7,15},{8,0},{9,1},... | collective-permute-start | bytes 1966088 | tf_op jit(solution)/shard_map/ppermute | solution.py:45
  58.6 9.8 %collective-permute-start.8 = (bf16[1280,256]{1,0:T(8,128)(2,1)S(1)}, bf16[1280,256]{1,0:T(8,128)(2,1)}, u32[]{:S(2)}, u32[]{:S(2)}) collective-permute-start(bf16[1280,256]{1,0:T(8,128)(2,1)S(1)} %collective-permute-done.3.refs_0_), channel_id=1, source_target_pairs={{0,16},{1,17},{2,18},{3,19},{4,20},{5,21},{6,22},{7,23},{8,56},{9,... | collective-permute-start | bytes 1966088 | tf_op jit(solution)/shard_map/ppermute | solution.py:45
  60.2 5.5 %collective-permute-start.9 = (bf16[640,256]{1,0:T(8,128)(2,1)S(1)}, bf16[640,256]{1,0:T(8,128)(2,1)S(1)}, u32[]{:S(2)}, u32[]{:S(2)}) collective-permute-start(bf16[640,256]{1,0:T(8,128)(2,1)S(1)} %collective-permute-done.5.refs_2_), channel_id=1, source_target_pairs={{0,8},{1,9},{2,10},{3,11},{4,12},{5,13},{6,14},{7,15},{8,0},{9,1},... | collective-permute-start | bytes 983048 | tf_op jit(solution)/shard_map/ppermute | solution.py:45
  60.2 12.8 %collective-permute-start.10 = (bf16[640,256]{1,0:T(8,128)(2,1)}, bf16[640,256]{1,0:T(8,128)(2,1)S(1)}, u32[]{:S(2)}, u32[]{:S(2)}) collective-permute-start(bf16[640,256]{1,0:T(8,128)(2,1)} %collective-permute-done.4.refs_3_), channel_id=1, source_target_pairs={{0,8},{1,9},{2,10},{3,11},{4,12},{5,13},{6,14},{7,15},{8,0},{9,1},... | collective-permute-start | bytes 983048 | tf_op jit(solution)/shard_map/ppermute | solution.py:45
  60.7 13.0 %collective-permute-start.7 = (bf16[640,256]{1,0:T(8,128)(2,1)S(1)}, bf16[640,256]{1,0:T(8,128)(2,1)}, u32[]{:S(2)}, u32[]{:S(2)}) collective-permute-start(bf16[640,256]{1,0:T(8,128)(2,1)S(1)} %slice.3), channel_id=1, source_target_pairs={{0,64},{1,65},{2,66},{3,67},{4,68},{5,69},{6,70},{7,71},{8,200},{9... | collective-permute-start | bytes 983048 | tf_op jit(solution)/shard_map/ppermute | solution.py:45
  66.4 7.4 %collective-permute-start.11 = (bf16[640,256]{1,0:T(8,128)(2,1)S(1)}, bf16[640,256]{1,0:T(8,128)(2,1)S(1)}, u32[]{:S(2)}, u32[]{:S(2)}) collective-permute-start(bf16[640,256]{1,0:T(8,128)(2,1)S(1)} %collective-permute-done.6.refs_6_), channel_id=1, source_target_pairs={{0,8},{1,9},{2,10},{3,11},{4,12},{5,13},{6,14},{7,15},{8,0},{9,1},... | collective-permute-start | bytes 983048 | tf_op jit(solution)/shard_map/ppermute | solution.py:45
  66.4 10.5 %collective-permute-start.14 = (bf16[1280,256]{1,0:T(8,128)(2,1)}, bf16[1280,256]{1,0:T(8,128)(2,1)}, u32[]{:S(2)}, u32[]{:S(2)}) collective-permute-start(bf16[1280,256]{1,0:T(8,128)(2,1)} %collective-permute-done.13.refs_0_), channel_id=1, source_target_pairs={{0,16},{1,17},{2,18},{3,19},{4,20},{5,21},{6,22},{7,23},{8,56},{9,... | collective-permute-start | bytes 1966088 | tf_op jit(solution)/shard_map/ppermute | solution.py:45
  68.5 18.5 %collective-permute-start.19 = (bf16[1280,256]{1,0:T(8,128)(2,1)}, bf16[1280,256]{1,0:T(8,128)(2,1)}, u32[]{:S(2)}, u32[]{:S(2)}) collective-permute-start(bf16[1280,256]{1,0:T(8,128)(2,1)} %collective-permute-done.8.refs_1_), channel_id=1, source_target_pairs={{0,16},{1,17},{2,18},{3,19},{4,20},{5,21},{6,22},{7,23},{8,56},{9,... | collective-permute-start | bytes 1966088 | tf_op jit(solution)/shard_map/ppermute | solution.py:45
  74.5 12.5 %collective-permute-start.15 = (bf16[640,256]{1,0:T(8,128)(2,1)}, bf16[640,256]{1,0:T(8,128)(2,1)}, u32[]{:S(2)}, u32[]{:S(2)}) collective-permute-start(bf16[640,256]{1,0:T(8,128)(2,1)} %collective-permute-done.7.refs_0_), channel_id=1, source_target_pairs={{0,16},{1,17},{2,18},{3,19},{4,20},{5,21},{6,22},{7,23},{8,56},{9,... | collective-permute-start | bytes 983048 | tf_op jit(solution)/shard_map/ppermute | solution.py:45
  76.9 19.2 %collective-permute-start.22 = (bf16[1280,256]{1,0:T(8,128)(2,1)}, bf16[1280,256]{1,0:T(8,128)(2,1)}, u32[]{:S(2)}, u32[]{:S(2)}) collective-permute-start(bf16[1280,256]{1,0:T(8,128)(2,1)} %collective-permute-done.8.refs_1_), channel_id=1, source_target_pairs={{0,8},{1,9},{2,10},{3,11},{4,12},{5,13},{6,14},{7,15},{8,0},{9,1},... | collective-permute-start | bytes 1966088 | tf_op jit(solution)/shard_map/ppermute | solution.py:45
  78.7 11.0 %collective-permute-start.18 = (bf16[1280,256]{1,0:T(8,128)(2,1)}, bf16[1280,256]{1,0:T(8,128)(2,1)S(1)}, u32[]{:S(2)}, u32[]{:S(2)}) collective-permute-start(bf16[1280,256]{1,0:T(8,128)(2,1)} %collective-permute-done.14.refs_1_), channel_id=1, source_target_pairs={{0,8},{1,9},{2,10},{3,11},{4,12},{5,13},{6,14},{7,15},{8,0},{9,1},... | collective-permute-start | bytes 1966088 | tf_op jit(solution)/shard_map/ppermute | solution.py:45
  87.0 9.0 %collective-permute-start.23 = (bf16[1280,256]{1,0:T(8,128)(2,1)}, bf16[1280,256]{1,0:T(8,128)(2,1)S(1)}, u32[]{:S(2)}, u32[]{:S(2)}) collective-permute-start(bf16[1280,256]{1,0:T(8,128)(2,1)} %collective-permute-done.19.refs_3_), channel_id=1, source_target_pairs={{0,8},{1,9},{2,10},{3,11},{4,12},{5,13},{6,14},{7,15},{8,0},{9,1},... | collective-permute-start | bytes 1966088 | tf_op jit(solution)/shard_map/ppermute | solution.py:45
  89.6 6.4 %collective-permute-start.16 = (bf16[640,256]{1,0:T(8,128)(2,1)}, bf16[640,256]{1,0:T(8,128)(2,1)S(1)}, u32[]{:S(2)}, u32[]{:S(2)}) collective-permute-start(bf16[640,256]{1,0:T(8,128)(2,1)} %collective-permute-done.12.refs_1_), channel_id=1, source_target_pairs={{0,16},{1,17},{2,18},{3,19},{4,20},{5,21},{6,22},{7,23},{8,56},{9,... | collective-permute-start | bytes 983048 | tf_op jit(solution)/shard_map/ppermute | solution.py:45
  89.6 11.3 %collective-permute-start.21 = (bf16[640,256]{1,0:T(8,128)(2,1)}, bf16[640,256]{1,0:T(8,128)(2,1)S(1)}, u32[]{:S(2)}, u32[]{:S(2)}) collective-permute-start(bf16[640,256]{1,0:T(8,128)(2,1)} %collective-permute-done.15.refs_2_), channel_id=1, source_target_pairs={{0,16},{1,17},{2,18},{3,19},{4,20},{5,21},{6,22},{7,23},{8,56},{9,... | collective-permute-start | bytes 983048 | tf_op jit(solution)/shard_map/ppermute | solution.py:45
  89.7 13.5 %collective-permute-start.17 = (bf16[640,256]{1,0:T(8,128)(2,1)}, bf16[640,256]{1,0:T(8,128)(2,1)S(1)}, u32[]{:S(2)}, u32[]{:S(2)}) collective-permute-start(bf16[640,256]{1,0:T(8,128)(2,1)} %collective-permute-done.15.refs_2_), channel_id=1, source_target_pairs={{0,8},{1,9},{2,10},{3,11},{4,12},{5,13},{6,14},{7,15},{8,0},{9,1},... | collective-permute-start | bytes 983048 | tf_op jit(solution)/shard_map/ppermute | solution.py:45
  100.9 3.4 %collective-permute-start.24 = (bf16[640,256]{1,0:T(8,128)(2,1)S(1)}, bf16[640,256]{1,0:T(8,128)(2,1)S(1)}, u32[]{:S(2)}, u32[]{:S(2)}) collective-permute-start(bf16[640,256]{1,0:T(8,128)(2,1)S(1)} %collective-permute-done.21.refs_6_), channel_id=1, source_target_pairs={{0,8},{1,9},{2,10},{3,11},{4,12},{5,13},{6,14},{7,15},{8,0},{9,1},... | collective-permute-start | bytes 983048 | tf_op jit(solution)/shard_map/ppermute | solution.py:45
  (24 other events, 247.8 us)
Sparse Core Ops, SparseCore 0:
  9.3 29.5 all-gather.6
  45.1 30.2 all-gather.4
